TPU v7x, 32 devices: a whole 2x2x4 slice. The times are simulated.
32 devices in a mesh: dp: 4 (over z), seq: 8 (over y, x, core).
Axes of the slice: x: 2, y: 2, z: 4, core: 2. Of those that a mesh axis runs over, the one named last changes fastest.
Arguments:
- tokens: bfloat16 [4, 2, 1024, 2048], P('dp', None, 'seq'), may hold values from -6 to 6
- doc_lengths: int32 [4, 2, 8], P('dp'), may hold values from 1 to 1017, as said below
- w_query: bfloat16 [2048, 256], P('dp'), may hold values from -0.125 to 0.125
- w_key: bfloat16 [2048, 256], P('dp'), may hold values from -0.125 to 0.125
- w_value: bfloat16 [2048, 2048], P('dp'), may hold values from -0.125 to 0.125
- w_out: bfloat16 [2048, 2048], P('dp'), may hold values from -1 to 1
- w_gate: bfloat16 [2048, 5632], P('dp'), may hold values from -0.125 to 0.125
- w_up: bfloat16 [2048, 5632], P('dp'), may hold values from -0.125 to 0.125
- w_down: bfloat16 [5632, 2048], P('dp'), may hold values from -0.078125 to 0.078125
- gain_attn: bfloat16 [2048], P('dp'), may hold values from 0.5 to 1.5
- gain_mlp: bfloat16 [2048], P('dp'), may hold values from 0.5 to 1.5
- cotangent: bfloat16 [4, 2, 1024, 2048], P('dp', None, 'seq'), may hold values from -6 to 6
Outputs:
- output: bfloat16 [4, 2, 1024, 2048], P('dp', None, 'seq')
- input_grad: float32 [4, 2, 1024, 2048], P('dp', None, 'seq')
- grad_query: float32 [2048, 256], P(('dp', 'seq'))
- grad_key: float32 [2048, 256], P(('dp', 'seq'))
- grad_value: float32 [2048, 2048], P(('dp', 'seq'))
- grad_out: float32 [2048, 2048], P(('dp', 'seq'))
- grad_gate: float32 [2048, 5632], P(('dp', 'seq'))
- grad_up: float32 [2048, 5632], P(('dp', 'seq'))
- grad_down: float32 [5632, 2048], P(('dp', 'seq'))
- grad_gain_attn: float32 [2048], P(('dp', 'seq'))
- grad_gain_mlp: float32 [2048], P(('dp', 'seq'))
Inputs may be any that keep to these rules, and one draw needn't show every extreme that they name: `doc_lengths`: in every stream the 8 lengths add up to 1024; one document of each stream, at a place drawn from the seed, holds all tokens but fewer than 128 before it and fewer than 128 after it; in one stream, drawn from the seed, every other document has one token.
All inputs are finite; a program needn't handle non-finite values.
Results may differ from a plain program's by a relative error of at most 0.02.
Values may be sent and summed in bfloat16 or wider, within the bound.
A program may use at most 640 MiB of HBM per device.

v0:
```python
import math

import jax
import jax.numpy as jnp
from jax import lax
from jax.sharding import PartitionSpec as P

D = 2048
HEADS = 16
QK_DIM = 16
FF = 5632
MICRO = 2
BLOCK = 128
HEAD_V = 128


epsilon = 1e-06
highest = lax.Precision.HIGHEST


def prefix(x, axis, combine, identity, reverse):
    size, mine = (lax.axis_size(axis), lax.axis_index(axis))
    everything = jax.tree.map(
        lambda part, kind: lax.all_gather(part.astype(kind), axis),
        x,
        jax.tree.map(lambda a: jnp.bfloat16 if a.dtype == jnp.float32 else a.dtype, x),
    )
    start = jax.tree.map(
        lambda part, zero: jnp.broadcast_to(jnp.asarray(zero, part.dtype), part.shape), x, identity
    )

    def step(k, before):
        at = size - 1 - k if reverse else k
        reached = at > mine if reverse else at < mine
        new = combine(
            before, jax.tree.map(lambda part, own: part[at].astype(own.dtype), everything, x)
        )
        return jax.tree.map(lambda a, b: jnp.where(reached, a, b), new, before)

    return lax.fori_loop(0, size, step, start)


def taylor_map(vectors):
    width = vectors.shape[-1]
    outer = (vectors[..., :, None] * vectors[..., None, :]).reshape(
        vectors.shape[:-1] + (width * width,)
    )
    ones = jnp.ones(vectors.shape[:-1] + (1,), jnp.float32)
    return jnp.concatenate(
        [ones, vectors / math.sqrt(math.sqrt(width)), outer / math.sqrt(2.0 * width)], axis=-1
    )


def norm_forward(rows, gain):
    inverse = lax.rsqrt(jnp.mean(rows * rows, axis=-1, keepdims=True) + epsilon)
    normed = rows * inverse
    return (normed * gain, normed, inverse)


def norm_backward(grad_out, normed, inverse, gain):
    scaled = grad_out * gain
    grad_rows = inverse * (scaled - normed * jnp.mean(scaled * normed, axis=-1, keepdims=True))
    return (grad_rows, grad_out * normed)


def chain_combine(earlier, later):
    open_share = 1.0 - later[0]
    return (
        jnp.maximum(earlier[0], later[0]),
        later[1] + open_share * earlier[1],
        later[2] + open_share * earlier[2],
    )


def contract_rows(left, right):
    return lax.dot_general(
        left, right, (((0,), (0,)), ((), ())), preferred_element_type=jnp.float32
    )


def local_attention(query, key, value, doc, doc_before):
    blocks = doc.shape[0] // BLOCK
    q_low = query.reshape(blocks, BLOCK, HEADS, QK_DIM)
    k_low = key.reshape(blocks, BLOCK, HEADS, QK_DIM)
    values = value.astype(jnp.float32).reshape(blocks, BLOCK, HEADS, HEAD_V)
    scores = jnp.einsum("nihf,njhf->nhij", q_low, k_low, preferred_element_type=jnp.float32)
    poly = 1.0 + scores / math.sqrt(QK_DIM) + scores * scores / (2.0 * QK_DIM)
    doc_blocks = doc.reshape(blocks, BLOCK)
    causal = jnp.arange(BLOCK)[:, None] >= jnp.arange(BLOCK)[None, :]
    mask = (causal[None] & (doc_blocks[:, :, None] == doc_blocks[:, None, :]))[:, None]
    weight = jnp.where(mask, poly, 0.0)
    numer = jnp.einsum("nhij,njhe->nihe", weight, values, precision=highest)
    denom = jnp.transpose(jnp.sum(weight, axis=-1), (0, 2, 1))
    queries = q_low.astype(jnp.float32)
    keys = k_low.astype(jnp.float32)
    q_feat = taylor_map(queries)
    k_feat = taylor_map(keys)
    first_before = doc_before.reshape(blocks, BLOCK)[:, 0]
    carry = (doc_blocks == first_before[:, None]).astype(jnp.float32)
    tail = (doc_blocks == doc_blocks[:, -1:]).astype(jnp.float32)
    reset = (doc_blocks[:, -1] != first_before).astype(jnp.float32)
    tail_state = jnp.einsum("nj,njhf,njhe->nhfe", tail, k_feat, values, precision=highest)
    tail_norm = jnp.einsum("nj,njhf->nhf", tail, k_feat, precision=highest)
    run_state = jnp.zeros(tail_state.shape[1:], jnp.float32)
    run_norm = jnp.zeros(tail_norm.shape[1:], jnp.float32)
    run_flag = jnp.zeros((), jnp.float32)
    prior_states, prior_norms, prior_flags = ([], [], [])
    prior_states.append(run_state)
    prior_norms.append(run_norm)
    prior_flags.append(run_flag)
    run_state = tail_state[0] + (1.0 - reset[0]) * run_state
    run_norm = tail_norm[0] + (1.0 - reset[0]) * run_norm
    run_flag = jnp.maximum(run_flag, reset[0])
    kept = {
        "queries": queries,
        "keys": keys,
        "values": values,
        "scores": scores,
        "mask": mask,
        "weight": weight,
        "numer": numer,
        "denom": denom,
        "q_feat": q_feat,
        "k_feat": k_feat,
        "carry": carry,
        "tail": tail,
        "reset": reset,
        "prior_states": jnp.stack(prior_states),
        "prior_norms": jnp.stack(prior_norms),
        "prior_flags": jnp.stack(prior_flags),
    }
    return (kept, (run_flag, run_state, run_norm))


def finish_attention(kept, dev_state, dev_norm):
    open_share = 1.0 - kept["prior_flags"]
    in_state = kept["prior_states"] + open_share[:, None, None, None] * dev_state[None]
    in_norm = kept["prior_norms"] + open_share[:, None, None] * dev_norm[None]
    carry = kept["carry"]
    numer = kept["numer"] + carry[..., None, None] * jnp.einsum(
        "nihf,nhfe->nihe", kept["q_feat"], in_state, precision=highest
    )
    denom = kept["denom"] + carry[..., None] * jnp.einsum(
        "nihf,nhf->nih", kept["q_feat"], in_norm, precision=highest
    )
    attended = numer / denom[..., None]
    kept["in_state"] = in_state
    kept["in_norm"] = in_norm
    kept["full_denom"] = denom
    kept["attended"] = attended
    return attended


def attention_grads(kept, grad_out):
    blocks = kept["numer"].shape[0]
    grads = grad_out.reshape(blocks, BLOCK, HEADS, HEAD_V)
    g_numer = grads / kept["full_denom"][..., None]
    g_denom = -jnp.sum(grads * kept["attended"], axis=-1) / kept["full_denom"]
    g_weight = jnp.einsum("nihe,njhe->nhij", g_numer, kept["values"], precision=highest)
    g_weight = g_weight + jnp.transpose(g_denom, (0, 2, 1))[..., None]
    g_weight = jnp.where(kept["mask"], g_weight, 0.0)
    g_value = jnp.einsum("nhij,nihe->njhe", kept["weight"], g_numer, precision=highest)
    g_scores = g_weight * (1.0 / math.sqrt(QK_DIM) + kept["scores"] / QK_DIM)
    g_query = jnp.einsum("nhij,njhf->nihf", g_scores, kept["keys"], precision=highest)
    g_key = jnp.einsum("nhij,nihf->njhf", g_scores, kept["queries"], precision=highest)
    carry = kept["carry"]
    g_qfeat = carry[..., None, None] * (
        jnp.einsum("nihe,nhfe->nihf", g_numer, kept["in_state"], precision=highest)
        + g_denom[..., None] * kept["in_norm"][:, None]
    )
    g_in_state = jnp.einsum("ni,nihf,nihe->nhfe", carry, kept["q_feat"], g_numer, precision=highest)
    g_in_norm = jnp.einsum("ni,nihf,nih->nhf", carry, kept["q_feat"], g_denom, precision=highest)
    open_share = 1.0 - kept["prior_flags"]
    g_dev_state = jnp.einsum("n,nhfe->hfe", open_share, g_in_state, precision=highest)
    g_dev_norm = jnp.einsum("n,nhf->hf", open_share, g_in_norm, precision=highest)
    unused, pull_query = jax.vjp(taylor_map, kept["queries"])
    g_query = g_query + pull_query(g_qfeat)[0]
    partial_grads = (g_query, g_key, g_value, g_in_state, g_in_norm)
    return (partial_grads, (g_dev_state, g_dev_norm))


def tail_grads(kept, partial_grads, later_state, later_norm):
    g_query, g_key, g_value, g_in_state, g_in_norm = partial_grads
    blocks = g_in_state.shape[0]
    grad_state, grad_norm = (later_state, later_norm)
    tail_states, tail_norms = ([None] * blocks, [None] * blocks)
    for index in reversed(range(blocks)):
        tail_states[index] = grad_state
        tail_norms[index] = grad_norm
        grad_state = (1.0 - kept["reset"][index]) * grad_state + g_in_state[index]
        grad_norm = (1.0 - kept["reset"][index]) * grad_norm + g_in_norm[index]
    d_tail_state = jnp.stack(tail_states)
    d_tail_norm = jnp.stack(tail_norms)
    tail = kept["tail"]
    g_kfeat = tail[..., None, None] * (
        jnp.einsum("njhe,nhfe->njhf", kept["values"], d_tail_state, precision=highest)
        + d_tail_norm[:, None]
    )
    g_value = g_value + tail[..., None, None] * jnp.einsum(
        "njhf,nhfe->njhe", kept["k_feat"], d_tail_state, precision=highest
    )
    unused, pull_key = jax.vjp(taylor_map, kept["keys"])
    g_key = g_key + pull_key(g_kfeat)[0]
    rows = blocks * BLOCK
    return (
        g_query.reshape(rows, HEADS * QK_DIM),
        g_key.reshape(rows, HEADS * QK_DIM),
        g_value.reshape(rows, HEADS * HEAD_V),
    )


def local(
    tokens,
    doc_lengths,
    w_query,
    w_key,
    w_value,
    w_out,
    w_gate,
    w_up,
    w_down,
    gain_attn,
    gain_mlp,
    cotangent,
):
    span = tokens.shape[2]
    place = lax.axis_index("seq")
    position = place * span + jnp.arange(span, dtype=jnp.int32)
    outputs, input_grads = ([], [])
    saved = {
        "h_one": [],
        "g_attn": [],
        "att_low": [],
        "g_mid": [],
        "h_two": [],
        "g_ffn": [],
        "act": [],
        "cot": [],
        "gn_one": [],
        "gn_two": [],
    }
    for micro in range(MICRO):
        gathered = (
            lax.all_gather(w_query, "dp", axis=0, tiled=True),
            lax.all_gather(w_key, "dp", axis=0, tiled=True),
            lax.all_gather(w_value, "dp", axis=0, tiled=True),
            lax.all_gather(w_out, "dp", axis=0, tiled=True),
            lax.all_gather(w_gate, "dp", axis=0, tiled=True),
            lax.all_gather(w_up, "dp", axis=0, tiled=True),
            lax.all_gather(w_down, "dp", axis=0, tiled=True),
            lax.all_gather(gain_attn, "dp", axis=0, tiled=True),
            lax.all_gather(gain_mlp, "dp", axis=0, tiled=True),
        )
        (
            full_query,
            full_key,
            full_value,
            full_out,
            full_gate,
            full_up,
            full_down,
            full_gain1,
            full_gain2,
        ) = gathered
        gain_one = full_gain1.astype(jnp.float32)
        gain_two = full_gain2.astype(jnp.float32)
        rows = tokens[0, micro].astype(jnp.float32)
        lengths = doc_lengths[0, micro]
        starts = jnp.cumsum(lengths) - lengths
        doc = jnp.sum((starts[None, :] <= position[:, None]).astype(jnp.int32), axis=1) - 1
        doc_before = (
            jnp.sum((starts[None, :] <= position[:, None] - 1).astype(jnp.int32), axis=1) - 1
        )
        normed_one, plain_one, inverse_one = norm_forward(rows, gain_one)
        h_one = normed_one.astype(jnp.bfloat16)
        query = jnp.dot(h_one, full_query, preferred_element_type=jnp.float32).astype(jnp.bfloat16)
        key = jnp.dot(h_one, full_key, preferred_element_type=jnp.float32).astype(jnp.bfloat16)
        value = jnp.dot(h_one, full_value, preferred_element_type=jnp.float32).astype(jnp.bfloat16)
        kept, summary = local_attention(query, key, value, doc, doc_before)
        identity = (
            jnp.zeros((), jnp.float32),
            jnp.zeros_like(summary[1]),
            jnp.zeros_like(summary[2]),
        )
        unused_flag, dev_state, dev_norm = prefix(summary, "seq", chain_combine, identity, False)
        attended = finish_attention(kept, dev_state, dev_norm)
        attended_low = attended.reshape(span, HEADS * HEAD_V).astype(jnp.bfloat16)
        mid = rows + jnp.dot(attended_low, full_out, preferred_element_type=jnp.float32)
        normed_two, plain_two, inverse_two = norm_forward(mid, gain_two)
        h_two = normed_two.astype(jnp.bfloat16)
        gate = jnp.dot(h_two, full_gate, preferred_element_type=jnp.float32)
        up = jnp.dot(h_two, full_up, preferred_element_type=jnp.float32)
        sigmoid_gate = jax.nn.sigmoid(gate)
        silu_gate = gate * sigmoid_gate
        act = (silu_gate * up).astype(jnp.bfloat16)
        result = mid + jnp.dot(act, full_down, preferred_element_type=jnp.float32)
        outputs.append(result.astype(jnp.bfloat16))
        grad_low = cotangent[0, micro]
        grad_rows = grad_low.astype(jnp.float32)
        g_act = jnp.dot(grad_low, full_down.T, preferred_element_type=jnp.float32)
        g_gate = (g_act * up * sigmoid_gate * (1.0 + gate * (1.0 - sigmoid_gate))).astype(
            jnp.bfloat16
        )
        g_up = (g_act * silu_gate).astype(jnp.bfloat16)
        g_h_two = jnp.dot(g_gate, full_gate.T, preferred_element_type=jnp.float32) + jnp.dot(
            g_up, full_up.T, preferred_element_type=jnp.float32
        )
        g_mid_norm, gn_two = norm_backward(g_h_two, plain_two, inverse_two, gain_two)
        g_mid = grad_rows + g_mid_norm
        g_mid_low = g_mid.astype(jnp.bfloat16)
        g_att = jnp.dot(g_mid_low, full_out.T, preferred_element_type=jnp.float32)
        partial_grads, dev_grads = attention_grads(kept, g_att)
        back_identity = (
            jnp.zeros((), jnp.float32),
            jnp.zeros_like(dev_grads[0]),
            jnp.zeros_like(dev_grads[1]),
        )
        unused_back, later_state, later_norm = prefix(
            (summary[0], dev_grads[0], dev_grads[1]), "seq", chain_combine, back_identity, True
        )
        g_query, g_key, g_value = tail_grads(kept, partial_grads, later_state, later_norm)
        g_query = g_query.astype(jnp.bfloat16)
        g_key = g_key.astype(jnp.bfloat16)
        g_value = g_value.astype(jnp.bfloat16)
        g_h_one = (
            jnp.dot(g_query, full_query.T, preferred_element_type=jnp.float32)
            + jnp.dot(g_key, full_key.T, preferred_element_type=jnp.float32)
            + jnp.dot(g_value, full_value.T, preferred_element_type=jnp.float32)
        )
        g_rows_norm, gn_one = norm_backward(g_h_one, plain_one, inverse_one, gain_one)
        input_grads.append(g_mid + g_rows_norm)
        saved["h_one"].append(h_one)
        saved["g_attn"].append(jnp.concatenate([g_query, g_key, g_value], axis=1))
        saved["att_low"].append(attended_low)
        saved["g_mid"].append(g_mid_low)
        saved["h_two"].append(h_two)
        saved["g_ffn"].append(jnp.concatenate([g_gate, g_up], axis=1))
        saved["act"].append(act)
        saved["cot"].append(grad_low)
        saved["gn_one"].append(gn_one)
        saved["gn_two"].append(gn_two)
    every = {name: jnp.concatenate(items, axis=0) for name, items in saved.items()}
    attn_part = contract_rows(every["h_one"], every["g_attn"])
    out_part = contract_rows(every["att_low"], every["g_mid"])
    ffn_part = contract_rows(every["h_two"], every["g_ffn"])
    gain_part = jnp.stack(
        [jnp.sum(every["gn_one"], axis=0), jnp.sum(every["gn_two"], axis=0)], axis=1
    )
    width_group = lax.psum_scatter(
        jnp.concatenate([attn_part, out_part, ffn_part, gain_part], axis=1).astype(jnp.bfloat16),
        "dp",
        scatter_dimension=0,
        tiled=True,
    )
    down_group = lax.psum_scatter(
        contract_rows(every["act"], every["cot"]).astype(jnp.bfloat16),
        "dp",
        scatter_dimension=0,
        tiled=True,
    )
    width_sum, down_sum = (
        lax.psum_scatter(width_group, "seq", scatter_dimension=0, tiled=True).astype(jnp.float32),
        lax.psum_scatter(down_group, "seq", scatter_dimension=0, tiled=True).astype(jnp.float32),
    )
    qk = HEADS * QK_DIM
    edges = [
        0,
        qk,
        2 * qk,
        2 * qk + D,
        2 * qk + 2 * D,
        2 * qk + 2 * D + FF,
        2 * qk + 2 * D + 2 * FF,
    ]
    pieces = [width_sum[:, edges[index] : edges[index + 1]] for index in range(6)]
    grad_gain_one = width_sum[:, edges[6]]
    grad_gain_two = width_sum[:, edges[6] + 1]
    output = jnp.stack(outputs)[None]
    input_grad = jnp.stack(input_grads)[None]
    return (
        output,
        input_grad,
        pieces[0],
        pieces[1],
        pieces[2],
        pieces[3],
        pieces[4],
        pieces[5],
        down_sum,
        grad_gain_one,
        grad_gain_two,
    )


def solution(mesh):
    return jax.shard_map(
        local,
        mesh=mesh,
        in_specs=(
            P("dp", None, "seq", None),
            P("dp", None, None),
            P("dp", None),
            P("dp", None),
            P("dp", None),
            P("dp", None),
            P("dp", None),
            P("dp", None),
            P("dp", None),
            P("dp"),
            P("dp"),
            P("dp", None, "seq", None),
        ),
        out_specs=(
            P("dp", None, "seq", None),
            P("dp", None, "seq", None),
            P(("dp", "seq"), None),
            P(("dp", "seq"), None),
            P(("dp", "seq"), None),
            P(("dp", "seq"), None),
            P(("dp", "seq"), None),
            P(("dp", "seq"), None),
            P(("dp", "seq"), None),
            P(("dp", "seq")),
            P(("dp", "seq")),
        ),
        check_vma=False,
    )
```

profile of v0, /device:TPU:1, one launch (start us, length us, event | category | flops | bytes accessed | tf_op | source)
XLA Modules:
  0.0 3556.4 jit_solution(5623014280594997228)
XLA Ops:
  12.1 10.3 all-gather.10
  23.5 16.0 all-gather.28.cloned.1.call-done
  42.3 148.3 %all-gather.24.cloned.1.call-done = bf16[2048,2048]{1,0:T(8,128)(2,1)} async-done(((bf16[512,2048]{1,0:T(8,128)(2,1)}), bf16[2048,2048]{1,0:T(8,128)(2,1)}) %all-gather.24.cloned.1.call-update) | async-done | bytes 8388624 | tf_op jit(solution)/shard_map/all_gather | solution.py:246
  190.6 4.6 fusion.72
  195.3 4.0 add_convert_fusion
  205.3 5.4 fusion.71
  210.8 4.0 add_convert_fusion.1
  220.5 12.1 all-reduce.3
  232.6 9.7 all-gather.11
  253.7 4.1 fusion.69
  257.8 14.6 all-gather.5
  274.8 9.7 all-gather.2
  292.3 50.3 %while.69 = (s32[]{:T(128)}, f32[16,273,128]{2,1,0:T(8,128)}, f32[16,273]{1,0:T(8,128)S(1)}, s32[]{:T(128)}, bf16[8,16,273,128]{3,1,0,2:T(8,128)(2,1)}, /*index=...) while((s32[]{:T(128)}, f32[16,273,128]{2,1,0:T(8,128)}, ...), condition=%wide.region_13.14_spmd.clone, body=%wide.region_12.13_spmd.clone.sunk | while | flops 2817365 | bytes 25762684 | solution.py:40
  342.7 3.3 fusion.158
  346.0 8.0 fusion.209
  354.1 76.1 %all-gather.30.cloned.1.call-done = bf16[2048,2048]{1,0:T(8,128)(2,1)} async-done(((bf16[512,2048]{1,0:T(8,128)(2,1)}), bf16[2048,2048]{1,0:T(8,128)(2,1)}) %all-gather.30.cloned.1.call-update) | async-done | bytes 8388624 | tf_op jit(solution)/shard_map/all_gather | solution.py:247
  430.1 5.2 multiply_reduce_fusion.14
  435.3 54.0 %all-gather.38.cloned.1.call-done = bf16[128,273,128]{2,0,1:T(8,128)(2,1)} async-done(((bf16[16,273,128]{2,0,1:T(8,128)(2,1)}), bf16[128,273,128]{2,0,1:T(8,128)(2,1)}) %all-gather.38.cloned.1.call-update) | async-done | bytes 8945680 | tf_op jit(solution)/shard_map/all_gather | solution.py:24
  489.3 33.4 while.68
  522.8 4.0 fusion.160
  526.8 8.2 fusion.210
  536.6 345.1 %all-gather.34.cloned.1.call-done = bf16[2048,5632]{1,0:T(8,128)(2,1)} async-done(((bf16[512,5632]{1,0:T(8,128)(2,1)}), bf16[2048,5632]{1,0:T(8,128)(2,1)}) %all-gather.34.cloned.1.call-update) | async-done | bytes 23068688 | tf_op jit(solution)/shard_map/all_gather | solution.py:249
  881.8 13.0 fusion.212
  894.8 378.0 %all-gather.32.cloned.1.call-done = bf16[2048,5632]{1,0:T(8,128)(2,1)} async-done(((bf16[512,5632]{1,0:T(8,128)(2,1)}), bf16[2048,5632]{1,0:T(8,128)(2,1)}) %all-gather.32.cloned.1.call-update) | async-done | bytes 23068688 | tf_op jit(solution)/shard_map/all_gather | solution.py:248
  1272.8 13.3 fusion.211
  1286.1 377.8 %all-gather.36.cloned.1.call-done = bf16[5632,2048]{1,0:T(8,128)(2,1)} async-done(((bf16[1408,2048]{1,0:T(8,128)(2,1)}), bf16[5632,2048]{1,0:T(8,128)(2,1)}) %all-gather.36.cloned.1.call-update) | async-done | bytes 23068688 | tf_op jit(solution)/shard_map/all_gather | solution.py:250
  1663.8 15.3 multiply_convert_fusion.2
  1679.1 12.9 fusion.215
  1692.0 13.6 multiply_reduce_fusion.9
  1705.7 12.5 fusion.214
  1718.2 12.4 fusion.213
  1730.6 15.5 multiply_convert_fusion
  1746.1 13.1 fusion.219
  1759.2 14.3 multiply_reduce_fusion.8
  1776.3 6.0 fusion.220
  1782.4 3.9 convolution_convert_fusion.6
  1787.8 5.9 fusion.216
  1793.7 3.9 convolution_convert_fusion.7
  1800.2 12.1 convolution_convert_fusion.1
  1821.8 5.7 convolution_convert_fusion.3
  1827.5 12.5 copy.210
  1840.0 10.4 all-gather.9
  1850.4 10.4 all-gather.7
  1860.9 5.5 fusion.27
  1868.5 3.9 fusion.26
  1881.1 3.3 convolution_bitcast_fusion.5
  1884.4 3.4 convolution_bitcast_fusion.4
  1887.8 21.1 convolution_convert_fusion
  1908.9 49.8 %while.71 = (s32[]{:T(128)}, f32[16,273,128]{2,1,0:T(8,128)}, f32[16,273]{1,0:T(8,128)S(1)}, s32[]{:T(128)}, bf16[8,16,273,128]{3,1,0,2:T(8,128)(2,1)}, /*index=...) while((s32[]{:T(128)}, f32[16,273,128]{2,1,0:T(8,128)}, ...), condition=%wide.region_30.31_spmd.clone, body=%wide.region_29.30_spmd.clone.sunk | while | flops 2817369 | bytes 25762748 | solution.py:40
  1958.6 3.9 fusion.29
  1965.6 38.4 %while.70 = (s32[]{:T(128)}, f32[16,273,128]{2,1,0:T(8,128)S(1)}, f32[16,273]{1,0:T(8,128)S(1)}, s32[]{:T(128)}, bf16[8,16,273,128]{3,1,0,2:T(8,128)(2,1)}, /*in...) while((s32[]{:T(128)}, f32[16,273,128]{2,1,0:T(8,128)S(1)}, ...), condition=%wide.region_21.22_spmd.clone, body=%wide.region_20.21_spmd.clone.sunk | while | flops 2817369 | bytes 7871363 | solution.py:40
  2007.7 3.0 fusion.83
  2011.7 5.3 fusion.68
  2017.0 5.5 fusion.67
  2022.6 2.9 fusion.222
  2026.0 2.9 fusion.218
  2031.2 6.3 convolution_convert_fusion.2
  2037.5 88.0 %concatenate.68 = bf16[2048,15874]{1,0:T(8,128)(2,1)} concatenate(bf16[2048,2560]{1,0:T(8,128)(2,1)} %convolution_convert_fusion.2, bf16[2048,2048]{1,0:T(8,128)(2,1)} %copy.210, bf16[2048,11264]{1,0:T(8,128)(2,1)} %convolution_convert_fusion, bf16[2048,1]{1,0:T(8,128)(2,1)S(1)} %reduce_sum.338, bf16[2048,1]{1,0:T(8,128)(2,1)S(1)} %copy-done.76), dimensions={1} | concatenate | bytes 130039808 | tf_op jit(solution)/shard_map/concatenate | solution.py:350
  2125.5 161.8 %reduce-scatter.9.cloned.1.call-done = bf16[1408,2048]{1,0:T(8,128)(2,1)} async-done(((bf16[5632,2048]{1,0:T(8,128)(2,1)}), bf16[1408,2048]{1,0:T(8,128)(2,1)}) %reduce-scatter.9.cloned.1.call-update) | async-done | bytes 5767184 | tf_op jit(solution)/shard_map/reduce_scatter | solution.py:355
  2287.7 1073.3 %reduce-scatter.13.cloned.1.call-done = bf16[512,15874]{1,0:T(8,128)(2,1)} async-done(((bf16[2048,15874]{1,0:T(8,128)(2,1)}), bf16[512,15874]{1,0:T(8,128)(2,1)}) %reduce-scatter.13.cloned.1.call-update) | async-done | bytes 16254992
  3362.2 11.3 fusion.25
  3373.6 13.1 fusion.24
  3392.8 32.2 reduce-scatter.11.cloned.1.call-done
  3427.3 115.8 %reduce-scatter.7.cloned.1.call-done = bf16[64,15874]{1,0:T(8,128)(2,1)} async-done(((bf16[512,15874]{1,0:T(8,128)(2,1)}), bf16[64,15874]{1,0:T(8,128)(2,1)}) %reduce-scatter.7.cloned.1.call-update) | async-done | bytes 2031888 | tf_op jit(solution)/shard_map/reduce_scatter | solution.py:362
  (669 shorter events, 242.1 us)
Async XLA Ops:
  7.2 32.3 all-gather.28.cloned.1.call-start
  7.9 182.7 %all-gather.24.cloned.1.call-start = ((), (), s32[]{:S(2)}) async-start(), calls=%async_computation.4 | async-start | bytes 10485760 | tf_op jit(solution)/shard_map/all_gather | solution.py:246
  8.7 234.5 %all-gather.26.cloned.1.call-start = ((), (), s32[]{:S(2)}) async-start(), calls=%async_computation.5 | async-start | bytes 1310720 | tf_op jit(solution)/shard_map/all_gather | solution.py:244
  9.4 282.9 %all-gather.40.cloned.1.call-start = ((), (), s32[]{:S(2)}) async-start(), calls=%async_computation.15 | async-start | bytes 10063872 | tf_op jit(solution)/shard_map/all_gather | solution.py:24
  10.0 31.1 copy-start.145
  10.0 192.7 %copy-start.143 = (s32[128]{0:T(128)}, s32[128]{0:T(128)S(1)}, u32[]{:S(2)}) copy-start(s32[128]{0:T(128)S(1)} %get-tuple-element.798) | copy-start | bytes 1540
  22.4 18.9 copy-start.109
  23.1 172.2 %copy-start.146 = (f32[128]{0:T(128)}, f32[128]{0:T(128)S(1)}, u32[]{:S(2)}) copy-start(f32[128]{0:T(128)S(1)} %get-tuple-element.891) | copy-start | bytes 1540
  23.2 16.4 copy-start.139
  23.2 16.4 copy-start.141
  23.5 167.1 %copy-start.28 = (bf16[128,2048]{1,0:T(8,128)(2,1)}, bf16[128,2048]{1,0:T(8,128)(2,1)S(1)}, u32[]{:S(2)}) copy-start(bf16[128,2048]{1,0:T(8,128)(2,1)S(1)} %get-tuple-element.878) | copy-start | bytes 1572868
  23.5 181.8 %copy-start.26 = (bf16[128,2048]{1,0:T(8,128)(2,1)}, bf16[128,2048]{1,0:T(8,128)(2,1)S(1)}, u32[]{:S(2)}) copy-start(bf16[128,2048]{1,0:T(8,128)(2,1)S(1)} %get-tuple-element.877) | copy-start | bytes 1572868
  41.2 212.5 %copy-start.81 = (f32[128,256]{0,1:T(8,128)}, f32[128,256]{0,1:T(8,128)S(1)}, u32[]{:S(2)}) copy-start(f32[128,256]{0,1:T(8,128)S(1)} %copy.179) | copy-start | bytes 393220
  41.3 154.0 %copy-start.101 = (bf16[128,256]{0,1:T(8,128)(2,1)}, bf16[128,256]{0,1:T(8,128)(2,1)S(1)}, u32[]{:S(2)}) copy-start(bf16[128,256]{0,1:T(8,128)(2,1)S(1)} %copy.176) | copy-start | bytes 196612
  42.3 153.0 %copy-start.16 = (f32[128,16,16,16]{0,3,2,1:T(8,128)}, f32[128,16,16,16]{0,3,2,1:T(8,128)S(1)}, u32[]{:S(2)}) copy-start(f32[128,16,16,16]{0,3,2,1:T(8,128)S(1)} %multiply_multiply_fusion.1) | copy-start | bytes 6291460
  200.5 229.6 %all-gather.30.cloned.1.call-start = ((), (), s32[]{:S(2)}) async-start(), calls=%async_computation.7 | async-start | bytes 10485760 | tf_op jit(solution)/shard_map/all_gather | solution.py:247
  201.1 288.2 %all-gather.38.cloned.1.call-start = ((), (), s32[]{:S(2)}) async-start(), calls=%async_computation.14 | async-start | bytes 10063872 | tf_op jit(solution)/shard_map/all_gather | solution.py:24
  216.0 665.7 %all-gather.34.cloned.1.call-start = ((), (), s32[]{:S(2)}) async-start(), calls=%async_computation.9 | async-start | bytes 28835840 | tf_op jit(solution)/shard_map/all_gather | solution.py:249
  216.8 1056.0 %all-gather.32.cloned.1.call-start = ((), (), s32[]{:S(2)}) async-start(), calls=%async_computation.8 | async-start | bytes 28835840 | tf_op jit(solution)/shard_map/all_gather | solution.py:248
  217.6 15.1 copy-start.157
  217.6 25.5 copy-start.155
  217.6 1446.3 %all-gather.36.cloned.1.call-start = ((), (), s32[]{:S(2)}) async-start(), calls=%async_computation.10 | async-start | bytes 28835840 | tf_op jit(solution)/shard_map/all_gather | solution.py:250
  218.3 1690.5 %all-gather.44.cloned.1.call-start = ((), (), s32[]{:S(2)}) async-start(), calls=%async_computation.17 | async-start | bytes 10063872 | tf_op jit(solution)/shard_map/all_gather | solution.py:24
  242.3 1531.1 %copy-start.107 = (f32[4,1,512]{2,1,0:T(1,128)}, f32[4,1,512]{2,1,0:T(1,128)S(1)}, u32[]{:S(2)}) copy-start(f32[4,1,512]{2,1,0:T(1,128)S(1)} %convert_element_type.582) | copy-start | bytes 24580
  243.1 46.3 %copy-start.115 = (pred[128,128]{0,1:T(8,128)(4,1)}, pred[128,128]{0,1:T(8,128)(4,1)S(1)}, u32[]{:S(2)}) copy-start(pred[128,128]{0,1:T(8,128)(4,1)S(1)} %fusion.154) | copy-start | bytes 49156
  251.0 21.4 copy-start.84
  251.0 21.4 copy-start.144
  253.7 30.8 copy-start.99
  253.7 18.7 copy-start.19
  253.7 30.8 copy-start.97
  253.7 30.8 copy-start.102
  272.4 12.7 copy-start.105
  272.4 12.7 copy-start.117
  285.0 60.9 %copy-start.120 = (f32[16,128]{1,0:T(8,128)}, f32[16,128]{1,0:T(8,128)S(1)}, u32[]{:S(2)}) copy-start(f32[16,128]{1,0:T(8,128)S(1)} %get-tuple-element.898) | copy-start | bytes 24580
  430.1 59.2 %copy-start.158 = (bf16[8]{0:T(256)(128)(2,1)S(1)}, bf16[8]{0:T(256)(128)(2,1)}, u32[]{:S(2)}) copy-start(bf16[8]{0:T(256)(128)(2,1)} %get-tuple-element.1194) | copy-start | bytes 52
  435.3 1338.2 %copy-start.9 = (f32[128,2048]{1,0:T(8,128)}, f32[128,2048]{1,0:T(8,128)S(1)}, u32[]{:S(2)}) copy-start(f32[128,2048]{1,0:T(8,128)S(1)} %get-tuple-element.913) | copy-start | bytes 3145732
  435.3 1338.2 %copy-start.128 = (f32[128]{0:T(128)}, f32[128]{0:T(128)S(1)}, u32[]{:S(2)}) copy-start(f32[128]{0:T(128)S(1)} %add_rsqrt_fusion) | copy-start | bytes 1540
  522.7 12.3 copy-start.4
  522.7 12.3 copy-start.93
  522.7 12.3 copy-start
  526.8 1266.9 %copy-start.135 = (f32[128,16]{0,1:T(8,128)}, f32[128,16]{0,1:T(8,128)S(1)}, u32[]{:S(2)}) copy-start(f32[128,16]{0,1:T(8,128)S(1)} %fusion.164) | copy-start | bytes 24580
  536.4 1237.0 %copy-start.11 = (f32[128,2048]{1,0:T(8,128)}, f32[128,2048]{1,0:T(8,128)S(1)}, u32[]{:S(2)}) copy-start(f32[128,2048]{1,0:T(8,128)S(1)} %get-tuple-element.911) | copy-start | bytes 3145732
  536.5 1237.0 %copy-start.130 = (f32[128]{0:T(128)}, f32[128]{0:T(128)S(1)}, u32[]{:S(2)}) copy-start(f32[128]{0:T(128)S(1)} %add_rsqrt_fusion.2) | copy-start | bytes 1540
  536.6 736.2 %copy-start.33 = (bf16[128,2048]{1,0:T(8,128)(2,1)}, bf16[128,2048]{1,0:T(8,128)(2,1)S(1)}, u32[]{:S(2)}) copy-start(bf16[128,2048]{1,0:T(8,128)(2,1)S(1)} %multiply_convert_fusion.7) | copy-start | bytes 1572868
  1705.7 12.5 copy-start.31
  1705.7 67.8 %copy-start.151 = (f32[128]{0:T(128)}, f32[128]{0:T(128)S(1)}, u32[]{:S(2)}) copy-start(f32[128]{0:T(128)S(1)} %broadcast_multiply_fusion.5) | copy-start | bytes 1540
  1746.1 13.1 copy-start.30
  1759.2 14.3 copy-start.35
  1787.5 178.1 %all-gather.42.cloned.1.call-start = ((), (), s32[]{:S(2)}) async-start(), calls=%async_computation.16 | async-start | bytes 10063872 | tf_op jit(solution)/shard_map/all_gather | solution.py:24
  1798.9 488.5 %reduce-scatter.9.cloned.1.call-start = ((), (), s32[]{:S(2)}) async-start(), calls=%async_computation.12 | async-start | bytes 28835840 | tf_op jit(solution)/shard_map/reduce_scatter | solution.py:355
  1812.3 1548.6 %reduce-scatter.13.cloned.1.call-start = ((), (), s32[]{:S(2)}) async-start(), calls=%async_computation.18 | async-start | bytes 81920000
  1827.5 33.4 copy-start.64
  1827.5 33.4 copy-start.94
  1827.5 33.4 copy-start.136
  1887.8 21.1 copy-start.161
  1908.8 49.8 %copy-start.147 = (f32[128]{0:T(128)S(1)}, f32[128]{0:T(128)}, u32[]{:S(2)}) copy-start(f32[128]{0:T(128)} %copy-done.146) | copy-start | bytes 1540
  1965.6 38.4 %copy-start.49 = (bf16[16,16,8,128]{3,2,1,0:T(8,128)(2,1)S(1)}, bf16[16,16,8,128]{3,2,1,0:T(8,128)(2,1)}, u32[]{:S(2)}) copy-start(bf16[16,16,8,128]{3,2,1,0:T(8,128)(2,1)} %copy-done.46) | copy-start | bytes 1572868
  1965.6 38.4 %copy-start.149 = (f32[128]{0:T(128)S(1)}, f32[128]{0:T(128)}, u32[]{:S(2)}) copy-start(f32[128]{0:T(128)} %copy-done.148) | copy-start | bytes 1540
  2007.0 15.5 slice-start
  2125.5 1299.5 %reduce-scatter.11.cloned.1.call-start = ((), (), s32[]{:S(2)}) async-start(), calls=%async_computation.13 | async-start | bytes 6488064 | tf_op jit(solution)/shard_map/reduce_scatter | solution.py:363
  2287.4 1255.8 %reduce-scatter.7.cloned.1.call-start = ((), (), s32[]{:S(2)}) async-start(), calls=%async_computation.11 | async-start | bytes 18432000 | tf_op jit(solution)/shard_map/reduce_scatter | solution.py:362
  3373.5 14.2 copy-start.108
  3373.5 14.2 copy-start.129
  3373.6 14.2 copy-start.154
  (144 other events, 496.9 us)
Sparse Core Ops, SparseCore 0:
  9.6 29.8 all-gather.27
  41.1 149.4 all-gather.23
  192.2 25.7 all-gather.25
  220.3 58.8 all-gather.39
  280.6 149.4 all-gather.29
  432.4 56.8 all-gather.37
  490.9 390.8 all-gather.33
  883.4 389.4 all-gather.31
  1274.4 389.3 all-gather.35
  1787.6 56.9 all-gather.43
  1846.5 58.4 all-gather.41
  1907.2 380.0 reduce-scatter.8
  2289.9 1071.0 reduce-scatter.12
  3364.3 60.6 reduce-scatter.10
  3429.0 114.0 reduce-scatter.6
where the time goes:
time: 3570 us; the launch traced here: 3560 us
  waiting for transfers between devices  2780 us (78%)
  matrix products  347 us (10%)
  local copies, waits for them, and re-layouts  221 us (6%)
  other arithmetic  83.9 us (2%)
  blocking collectives  77.3 us (2%)
    unnamed x16, waiting for transfers between devices  1080 us
    all_gather x1, waiting for transfers between devices, local(): lax.all_gather(w_gate, 'dp', axis=0, tiled=True)  378 us
    all_gather x1, waiting for transfers between devices, local(): lax.all_gather(w_down, 'dp', axis=0, tiled=True)  378 us
    all_gather x1, waiting for transfers between devices, local(): lax.all_gather(w_up, 'dp', axis=0, tiled=True)  345 us
    reduce_scatter x1, waiting for transfers between devices, local(): lax.psum_scatter(contract_rows(every['act'], every['cot']).astype(jnp.bfl...  162 us
    all_gather x1, waiting for transfers between devices, local(): lax.all_gather(w_value, 'dp', axis=0, tiled=True)  148 us
    reduce_scatter x1, waiting for transfers between devices, local(): lax.psum_scatter(width_group, 'seq', scatter_dimension=0, tiled=True)  116 us
    concatenate x1, local copies, waits for them, and re-layouts, local(): jnp.concatenate([attn_part, out_part, ffn_part, gain_part], axis=1)  88 us
  transfers between devices with their start and end apart: 15, of which 11 were waited for; matrix products, arithmetic and copies ran while one was open for 14% of the time, Pallas kernels for 0%

commit v1 on v0

v1 whole, which is shorter than its diff:
```python
import functools
import math

import jax
import jax.numpy as jnp
from jax import lax
from jax.experimental import pallas as pl
from jax.experimental.pallas import tpu as pltpu
from jax.sharding import PartitionSpec as P

D = 2048
HEADS = 16
QK_DIM = 16
FF = 5632
HEAD_V = 128
epsilon = 1e-06
MIB = 1024 * 1024


def dot(left, right):
    return jnp.dot(left, right, preferred_element_type=jnp.float32)


def contract(left, right, left_dim, right_dim):
    return lax.dot_general(
        left, right, (((left_dim,), (right_dim,)), ((), ())), preferred_element_type=jnp.float32
    )


def head_lanes(rows, head):
    lane = lax.broadcasted_iota(jnp.int32, rows.shape, 1)
    inside = (lane >= head * QK_DIM) & (lane < (head + 1) * QK_DIM)
    return jnp.where(inside, rows, jnp.zeros_like(rows))


def weights_of(query, key, head, first, base):
    scores = contract(head_lanes(query, head), key, 1, 1)
    row = base + lax.broadcasted_iota(jnp.int32, scores.shape, 0)
    column = lax.broadcasted_iota(jnp.int32, scores.shape, 1)
    mask = (column <= row) & (column >= first)
    poly = 1.0 + scores * (1.0 / math.sqrt(QK_DIM)) + scores * scores * (0.5 / QK_DIM)
    return scores, mask, jnp.where(mask, poly, 0.0)


def attend_kernel(heads, q_ref, k_ref, v_ref, first_ref, out_ref):
    rows = q_ref.shape[1]
    base = pl.program_id(1) * rows
    for head in range(heads):
        columns = slice(head * HEAD_V, (head + 1) * HEAD_V)
        unused, unused_mask, weight = weights_of(
            q_ref[0], k_ref[0], head, first_ref[0], base
        )
        denom = jnp.sum(weight, axis=1, keepdims=True)
        numer = dot(weight.astype(jnp.bfloat16), v_ref[0, :, columns])
        out_ref[0, :, columns] = (numer / denom).astype(jnp.bfloat16)


def attend(query, key, value, first, heads):
    streams, length, width = query.shape
    rows = min(256, length)
    return pl.pallas_call(
        functools.partial(attend_kernel, heads),
        grid=(streams, length // rows),
        in_specs=[
            pl.BlockSpec((1, rows, width), lambda m, i: (m, i, 0)),
            pl.BlockSpec((1, length, width), lambda m, i: (m, 0, 0)),
            pl.BlockSpec((1, length, heads * HEAD_V), lambda m, i: (m, 0, 0)),
            pl.BlockSpec((1, rows, 1), lambda m, i: (m, i, 0)),
        ],
        out_specs=pl.BlockSpec((1, rows, heads * HEAD_V), lambda m, i: (m, i, 0)),
        out_shape=jax.ShapeDtypeStruct(value.shape, jnp.bfloat16),
        compiler_params=pltpu.CompilerParams(vmem_limit_bytes=48 * MIB),
        name="attend",
    )(query, key, value, first)


def attend_back_kernel(
    heads, q_ref, k_ref, v_ref, first_ref, att_ref, g_ref, gq_ref, gk_ref, gv_ref, gk_sum, gv_sum
):
    rows = q_ref.shape[1]
    step = pl.program_id(1)
    base = step * rows

    @pl.when(step == 0)
    def _():
        gk_sum[...] = jnp.zeros_like(gk_sum)
        gv_sum[...] = jnp.zeros_like(gv_sum)

    query, key = q_ref[0], k_ref[0]
    g_query = jnp.zeros(query.shape, jnp.float32)
    for head in range(heads):
        columns = slice(head * HEAD_V, (head + 1) * HEAD_V)
        scores, mask, weight = weights_of(query, key, head, first_ref[0], base)
        denom = jnp.sum(weight, axis=1, keepdims=True)
        a = (g_ref[0, :, columns].astype(jnp.float32) / denom).astype(jnp.bfloat16)
        b = -jnp.sum(
            a.astype(jnp.float32) * att_ref[0, :, columns].astype(jnp.float32),
            axis=1,
            keepdims=True,
        )
        g_weight = contract(a, v_ref[0, :, columns], 1, 1) + b
        slope = 1.0 / math.sqrt(QK_DIM) + scores * (1.0 / QK_DIM)
        g_scores = jnp.where(mask, g_weight * slope, 0.0).astype(jnp.bfloat16)
        g_query += head_lanes(dot(g_scores, key), head)
        gk_sum[...] += contract(g_scores, head_lanes(query, head), 0, 0)
        gv_sum[:, columns] += contract(weight.astype(jnp.bfloat16), a, 0, 0)
    gq_ref[0] = g_query.astype(jnp.bfloat16)

    @pl.when(step == pl.num_programs(1) - 1)
    def _():
        gk_ref[0] = gk_sum[...].astype(jnp.bfloat16)
        gv_ref[0] = gv_sum[...].astype(jnp.bfloat16)


def attend_back(query, key, value, first, attended, grad, heads):
    streams, length, width = query.shape
    rows = min(256, length)
    some = pl.BlockSpec((1, rows, width), lambda m, i: (m, i, 0))
    all_narrow = pl.BlockSpec((1, length, width), lambda m, i: (m, 0, 0))
    all_wide = pl.BlockSpec((1, length, heads * HEAD_V), lambda m, i: (m, 0, 0))
    some_wide = pl.BlockSpec((1, rows, heads * HEAD_V), lambda m, i: (m, i, 0))
    return pl.pallas_call(
        functools.partial(attend_back_kernel, heads),
        grid=(streams, length // rows),
        in_specs=[
            some,
            all_narrow,
            all_wide,
            pl.BlockSpec((1, rows, 1), lambda m, i: (m, i, 0)),
            some_wide,
            some_wide,
        ],
        out_specs=[some, all_narrow, all_wide],
        out_shape=[
            jax.ShapeDtypeStruct(query.shape, jnp.bfloat16),
            jax.ShapeDtypeStruct(key.shape, jnp.bfloat16),
            jax.ShapeDtypeStruct(value.shape, jnp.bfloat16),
        ],
        scratch_shapes=[
            pltpu.VMEM((length, width), jnp.float32),
            pltpu.VMEM((length, heads * HEAD_V), jnp.float32),
        ],
        compiler_params=pltpu.CompilerParams(vmem_limit_bytes=56 * MIB),
        name="attend_back",
    )(query, key, value, first, attended, grad)


def norm_scale(rows):
    return lax.rsqrt(jnp.mean(rows * rows, axis=-1, keepdims=True) + epsilon)


def norm_backward(grad, normed, inverse, gain):
    scaled = grad * gain
    return inverse * (scaled - normed * jnp.mean(scaled * normed, axis=-1, keepdims=True))


def local(
    tokens,
    doc_lengths,
    w_query,
    w_key,
    w_value,
    w_out,
    w_gate,
    w_up,
    w_down,
    gain_attn,
    gain_mlp,
    cotangent,
):
    micro, span = tokens.shape[1:3]
    pieces, groups = lax.axis_size("seq"), lax.axis_size("dp")
    place = lax.axis_index("seq")
    length = pieces * span
    heads = max(1, HEADS // pieces)
    sharers = max(1, pieces // HEADS)
    streams = micro // sharers
    first_head = place // sharers * heads
    first_stream = place % sharers * streams
    qk, wide = heads * QK_DIM, heads * HEAD_V
    hidden = FF // pieces
    low = jnp.bfloat16

    attn_slice = jnp.concatenate(
        [
            lax.dynamic_slice_in_dim(w_value, first_head * HEAD_V, wide, 1),
            lax.dynamic_slice_in_dim(w_query, first_head * QK_DIM, qk, 1),
            lax.dynamic_slice_in_dim(w_key, first_head * QK_DIM, qk, 1),
        ],
        axis=1,
    )
    rows_dp = w_gate.shape[0]
    share = hidden // groups

    def hidden_columns(w):
        return lax.dynamic_slice_in_dim(
            w.reshape(rows_dp, groups, pieces, share), place, 1, 2
        ).reshape(rows_dp, hidden)

    ffn_slice = jnp.concatenate([hidden_columns(w_gate), hidden_columns(w_up)], axis=1)
    down_slice = lax.dynamic_slice_in_dim(w_down, place * share, share, 0)
    out_width = D // pieces
    out_slice = lax.dynamic_slice_in_dim(w_out, place * out_width, out_width, 1)

    def gather_dp(w):
        return lax.all_gather(w, "dp", axis=0, tiled=True)

    gains = gather_dp(jnp.stack([gain_attn, gain_mlp], axis=1)).astype(jnp.float32)
    gain_one, gain_two = gains[:, 0], gains[:, 1]
    attn_full = gather_dp(attn_slice)
    out_full = lax.all_gather(gather_dp(out_slice), "seq", axis=1, tiled=True)
    ffn_full = gather_dp(ffn_slice)
    down_full = gather_dp(down_slice)
    gate_full, up_full = ffn_full[:, :hidden], ffn_full[:, hidden:]

    lengths = lax.dynamic_slice_in_dim(doc_lengths[0], first_stream, streams, 0)
    starts = jnp.cumsum(lengths, axis=1) - lengths
    position = jnp.arange(length, dtype=jnp.int32)
    begun = starts[:, None, :] <= position[None, :, None]
    first = jnp.max(jnp.where(begun, starts[:, None, :], 0), axis=2)[..., None]

    rows = tokens[0].astype(jnp.float32)
    inverse_one = norm_scale(rows)
    plain_one = rows * inverse_one
    h_one = (plain_one * gain_one).astype(low)
    if sharers == 1:
        h_all = jnp.stack(
            [lax.all_gather(h_one[m], "seq", axis=0, tiled=True) for m in range(micro)]
        )
    else:
        h_all = lax.all_gather(h_one, "seq", axis=1, tiled=True)
        h_all = lax.dynamic_slice_in_dim(h_all, first_stream, streams, 0)
    h_flat = h_all.reshape(streams * length, D)
    projected = dot(h_flat, attn_full).astype(low)
    value = projected[:, :wide].reshape(streams, length, wide)
    query = projected[:, wide : wide + qk].reshape(streams, length, qk)
    key = projected[:, wide + qk :].reshape(streams, length, qk)
    att_heads = attend(query, key, value, first, heads)

    def to_tokens(by_head):
        sent = by_head.reshape(streams, pieces, span, wide)
        got = lax.all_to_all(sent, "seq", 1, 0, tiled=False)
        got = got.reshape(pieces // sharers, micro, span, wide)
        return got.transpose(1, 2, 0, 3).reshape(micro * span, HEADS * HEAD_V)

    def to_heads(by_token):
        sent = by_token.reshape(micro, span, pieces // sharers, wide).transpose(2, 0, 1, 3)
        sent = sent.reshape(pieces, streams, span, wide)
        got = lax.all_to_all(sent, "seq", 0, 1, tiled=False)
        return got.reshape(streams, length, wide)

    attended = to_tokens(att_heads)
    flat = rows.reshape(micro * span, D)
    mid = flat + dot(attended, out_full)
    inverse_two = norm_scale(mid)
    plain_two = mid * inverse_two
    h_two = (plain_two * gain_two).astype(low)
    cot = cotangent[0].reshape(micro * span, D)

    h_two_all = lax.all_gather(h_two, "seq", axis=0, tiled=True)
    cot_all = lax.all_gather(cot, "seq", axis=0, tiled=True)
    gate = dot(h_two_all, gate_full)
    up = dot(h_two_all, up_full)
    g_act = contract(cot_all, down_full, 1, 1)
    sigmoid = jax.nn.sigmoid(gate)
    silu = gate * sigmoid
    act = (silu * up).astype(low)
    g_gate = (g_act * up * sigmoid * (1.0 + gate * (1.0 - sigmoid))).astype(low)
    g_up = (g_act * silu).astype(low)
    g_h_two_part = (contract(g_gate, gate_full, 1, 1) + contract(g_up, up_full, 1, 1)).astype(low)
    out_part = dot(act, down_full).astype(low)

    def scatter(part):
        return lax.psum_scatter(part, "seq", scatter_dimension=0, tiled=True).astype(jnp.float32)

    g_h_two = scatter(g_h_two_part)
    output = (mid + scatter(out_part)).astype(low)
    grad_down = lax.psum_scatter(
        contract(act, cot_all, 0, 0).astype(low), "dp", scatter_dimension=0, tiled=True
    ).astype(jnp.float32)
    grad_ffn = lax.psum_scatter(
        jnp.concatenate(
            [contract(h_two_all, g_gate, 0, 0).astype(low), contract(h_two_all, g_up, 0, 0).astype(low)],
            axis=1,
        ),
        "dp",
        scatter_dimension=0,
        tiled=True,
    )

    g_mid = cot.astype(jnp.float32) + norm_backward(g_h_two, plain_two, inverse_two, gain_two)
    g_mid_low = g_mid.astype(low)
    g_att = to_heads(contract(g_mid_low, out_full, 1, 1).astype(low))
    g_query, g_key, g_value = attend_back(query, key, value, first, att_heads, g_att, heads)
    g_all = jnp.concatenate([g_value, g_query, g_key], axis=2).reshape(streams * length, -1)
    g_h_one_part = contract(g_all, attn_full, 1, 1).astype(low).reshape(streams, length, D)
    if sharers == 1:
        g_h_one = jnp.stack([scatter(g_h_one_part[m]) for m in range(micro)])
    else:
        padded = jnp.zeros((micro, length, D), low)
        padded = lax.dynamic_update_slice_in_dim(padded, g_h_one_part, first_stream, 0)
        g_h_one = lax.psum_scatter(padded, "seq", scatter_dimension=1, tiled=True)
        g_h_one = g_h_one.astype(jnp.float32)
    input_grad = g_mid.reshape(micro, span, D) + norm_backward(
        g_h_one, plain_one, inverse_one, gain_one
    )

    grad_attn = lax.psum_scatter(
        contract(h_flat, g_all, 0, 0).astype(low), "dp", scatter_dimension=0, tiled=True
    )
    own = rows_dp // pieces
    exchanged = lax.all_to_all(
        jnp.concatenate([grad_attn, grad_ffn], axis=1).reshape(pieces, own, -1), "seq", 0, 0
    ).astype(jnp.float32)
    attn_got = exchanged[:, :, : wide + 2 * qk]
    attn_got = jnp.sum(attn_got.reshape(pieces // sharers, sharers, own, -1), axis=1)

    def by_rows(block):
        return block.transpose(1, 0, 2).reshape(own, -1)

    grad_value = by_rows(attn_got[:, :, :wide])
    grad_query = by_rows(attn_got[:, :, wide : wide + qk])
    grad_key = by_rows(attn_got[:, :, wide + qk :])

    def by_hidden(block):
        return block.reshape(pieces, own, groups, share).transpose(1, 2, 0, 3).reshape(own, FF)

    ffn_got = exchanged[:, :, wide + 2 * qk :]
    grad_gate = by_hidden(ffn_got[:, :, :hidden])
    grad_up = by_hidden(ffn_got[:, :, hidden:])
    gain_part = jnp.stack(
        [
            jnp.sum(g_h_one * plain_one, axis=(0, 1)),
            jnp.sum(g_h_two * plain_two, axis=0),
        ],
        axis=1,
    )
    out_part = jnp.concatenate([contract(attended, g_mid_low, 0, 0), gain_part], axis=1)
    out_part = out_part.astype(low).reshape(groups, pieces, own, -1).transpose(1, 0, 2, 3)
    out_group = lax.psum_scatter(out_part, "seq", scatter_dimension=0, tiled=False)
    out_sum = lax.psum_scatter(out_group, "dp", scatter_dimension=0, tiled=False)
    out_sum = out_sum.astype(jnp.float32)
    return (
        output.reshape(tokens.shape),
        input_grad[None],
        grad_query,
        grad_key,
        grad_value,
        out_sum[:, :D],
        grad_gate,
        grad_up,
        grad_down,
        out_sum[:, D],
        out_sum[:, D + 1],
    )


def solution(mesh):
    by_token, by_row = P("dp", None, "seq", None), P("dp", None)
    grad_rows, grad_entries = P(("dp", "seq"), None), P(("dp", "seq"))
    return jax.shard_map(
        local,
        mesh=mesh,
        in_specs=(by_token, P("dp", None, None)) + (by_row,) * 7 + (P("dp"), P("dp"), by_token),
        out_specs=(by_token, by_token) + (grad_rows,) * 7 + (grad_entries,) * 2,
        check_vma=False,
    )
```

time: 3570 us -> 1270 us (0.36)
  waiting for transfers between devices: 2780 us -> 869 us
  matrix products: 347 us -> 141 us
  local copies, waits for them, and re-layouts: 221 us -> 104 us
  other arithmetic: 83.9 us -> 32.7 us
    all_gather x11 -> x9, waiting for transfers between devices: 1400 us -> 361 us  [the longest x4 182 us: gather_dp(): return lax.all_gather(w, 'dp', axis=0, tiled=True)]
    unnamed x16 -> x19, waiting for transfers between devices: 1080 us -> 146 us
    dot_general x60 -> x15, matrix products: 335 us -> 141 us  [the longest x10 96.4 us: contract(): lax.dot_general(left, right, (((left_dim,), (right_dim,)), ((), ())), pre...]
    concatenate x2 -> x4, local copies, waits for them, and re-layouts: 88 us -> 19.2 us  [the longest x3 16.7 us: local(): jnp.concatenate([contract(attended, g_mid_low, 0, 0), gain_part], axis=1)]
    all_gather x7 -> x1, blocking collectives: 77.3 us -> 10.3 us  [gather_dp(): return lax.all_gather(w, 'dp', axis=0, tiled=True)]
    dynamic_slice x64 -> x5, local copies, waits for them, and re-layouts: 67 us -> 5.44 us  [the longest x1 2.17 us: local(): down_slice = lax.dynamic_slice_in_dim(w_down, place * share, share, 0)]
    select_n x64 -> x0, other arithmetic: 58.4 us -> none  [step(): return jax.tree.map(lambda a, b: jnp.where(reached, a, b), new, before)]
    reduce_scatter x3 -> x8, waiting for transfers between devices: 310 us -> 362 us  [the longest x4 196 us: scatter(): lax.psum_scatter(part, 'seq', scatter_dimension=0, tiled=True)]
  transfers between devices with their start and end apart: 15 -> 19, of which waited for: 11 -> 17; matrix products, arithmetic and copies ran while one was open for 14% -> 16% of each run, Pallas kernels for 0% -> 1%
where the time goes in v1:
time: 1270 us; the launch traced here: 1260 us
  waiting for transfers between devices  869 us (68%)
  matrix products  141 us (11%)
  local copies, waits for them, and re-layouts  104 us (8%)
  blocking collectives  55.3 us (4%)
  Pallas kernels  35.1 us (3%)
  other arithmetic  32.7 us (3%)
  between operations  15.2 us (1%)
    reduce_scatter x4, waiting for transfers between devices, scatter(): lax.psum_scatter(part, 'seq', scatter_dimension=0, tiled=True)  196 us
    all_gather x4, waiting for transfers between devices, gather_dp(): return lax.all_gather(w, 'dp', axis=0, tiled=True)  182 us
    unnamed x19, waiting for transfers between devices  146 us
    dot_general x10, matrix products, contract(): lax.dot_general(left, right, (((left_dim,), (right_dim,)), ((), ())), pre...  96.4 us
    reduce_scatter x1, waiting for transfers between devices, local(): lax.psum_scatter(jnp.concatenate([contract(h_two_all, g_gate, 0, 0).astyp...  75.9 us
    reduce_scatter x1, waiting for transfers between devices, local(): lax.psum_scatter(contract(act, cot_all, 0, 0).astype(low), 'dp', scatter_...  56 us
    all_gather x1, waiting for transfers between devices, local(): cot_all = lax.all_gather(cot, 'seq', axis=0, tiled=True)  55.5 us
    all_gather x1, waiting for transfers between devices, local(): h_two_all = lax.all_gather(h_two, 'seq', axis=0, tiled=True)  55.3 us
  transfers between devices with their start and end apart: 19, of which 17 were waited for; matrix products, arithmetic and copies ran while one was open for 16% of the time, Pallas kernels for 1%

profile of v1, /device:TPU:1, one launch (start us, length us, event | category | flops | bytes accessed | tf_op | source)
XLA Modules:
  0.0 1258.6 jit_solution(4763848687612107136)
XLA Ops:
  12.5 10.3 all_gather.30
  28.5 11.6 all-gather.14.cloned.1.call-done
  40.2 8.4 copy.103
  48.5 8.4 copy.104
  60.3 19.1 %all-gather.26.cloned.1.call-done = bf16[1,1024,2048]{2,1,0:T(8,128)(2,1)} async-done(((bf16[1,128,2048]{2,1,0:T(8,128)(2,1)}), bf16[1,1024,2048]{2,1,0:T(8,128)(2,1)}) %all-gather.26.cloned.1.call-update) | async-done | bytes 4194320 | tf_op jit(solution)/shard_map/all_gather | solution.py:228
  79.4 4.7 constant_dynamic-update-slice_fusion.1
  84.1 34.5 %all-gather.28.cloned.1.call-done = bf16[1,1024,2048]{2,1,0:T(8,128)(2,1)} async-done(((bf16[1,128,2048]{2,1,0:T(8,128)(2,1)}), bf16[1,1024,2048]{2,1,0:T(8,128)(2,1)}) %all-gather.28.cloned.1.call-update) | async-done | bytes 4194320 | tf_op jit(solution)/shard_map/all_gather | solution.py:228
  118.6 4.7 constant_dynamic-update-slice_fusion
  123.4 33.8 %all-gather.12.cloned.1.call-done = bf16[2048,320]{1,0:T(8,128)(2,1)} async-done(((bf16[512,320]{1,0:T(8,128)(2,1)}), bf16[2048,320]{1,0:T(8,128)(2,1)}) %all-gather.12.cloned.1.call-update) | async-done | bytes 1310736 | tf_op jit(solution)/shard_map/all_gather | solution.py:206
  157.2 6.7 convolution_convert_fusion.6
  171.1 10.4 attend.1.att_ref
  181.6 27.7 %all_to_all.35 = bf16[1,2,8,128,256]{4,3,1,0,2:T(8,128)(2,1)S(1)} all-to-all(bf16[1,2,8,128,256]{4,3,1,0,2:T(8,128)(2,1)S(1)} %copy.101), channel_id=1, replica_groups=mesh['dp'=4,'seq'=8] {'seq'}, dimensions={2} | all-to-all | bytes 2097152 | tf_op jit(solution)/shard_map/all_to_all | solution.py:242
  211.2 14.4 %all-gather.16.cloned.1.call-done = bf16[2048,2048]{1,0:T(8,128)(2,1)} async-done(((bf16[2048,256]{1,0:T(8,128)(2,1)}), bf16[2048,2048]{1,0:T(8,128)(2,1)}) %all-gather.16.cloned.1.call-update) | async-done | bytes 8388624 | tf_op jit(solution)/shard_map/all_gather | solution.py:211
  225.6 6.2 multiply_reduce_fusion.2
  233.3 2.2 constant_dynamic-slice_fusion
  236.4 96.5 %all-gather.20.cloned.1.call-done = bf16[2048,1408]{0,1:T(8,128)(2,1)} async-done(((bf16[512,1408]{0,1:T(8,128)(2,1)}), bf16[2048,1408]{0,1:T(8,128)(2,1)}) %all-gather.20.cloned.1.call-update) | async-done | bytes 5767184 | tf_op jit(solution)/shard_map/all_gather | solution.py:206
  332.9 55.3 %all-gather.18.cloned.1.call-done = bf16[2048,2048]{1,0:T(8,128)(2,1)} async-done(((bf16[256,2048]{1,0:T(8,128)(2,1)}), bf16[2048,2048]{1,0:T(8,128)(2,1)}) %all-gather.18.cloned.1.call-update) | async-done | bytes 8388624 | tf_op jit(solution)/shard_map/all_gather | solution.py:260
  388.2 12.1 fusion.7
  400.4 7.9 fusion.11
  408.3 40.3 %all-gather.22.cloned.1.call-done = bf16[704,2048]{1,0:T(8,128)(2,1)} async-done(((bf16[176,2048]{1,0:T(8,128)(2,1)}), bf16[704,2048]{1,0:T(8,128)(2,1)}) %all-gather.22.cloned.1.call-update) | async-done | bytes 2883600 | tf_op jit(solution)/shard_map/all_gather | solution.py:206
  448.6 55.5 %all-gather.24.cloned.1.call-done = bf16[2048,2048]{1,0:T(8,128)(2,1)} async-done(((bf16[256,2048]{1,0:T(8,128)(2,1)}), bf16[2048,2048]{1,0:T(8,128)(2,1)}) %all-gather.24.cloned.1.call-update) | async-done | bytes 8388624 | tf_op jit(solution)/shard_map/all_gather | solution.py:261
  504.0 15.1 %fusion.3 = (bf16[2048,704]{0,1:T(8,128)(2,1)S(1)}, bf16[2048,704]{0,1:T(8,128)(2,1)S(1)}, bf16[2048,704]{0,1:T(8,128)(2,1)}) fusion(f32[2048,704]{0,1:T(8,128)} %fusion.11, f32[2048,704]{0,1:T(8,128)} %fusion.7, bf16[704,2048]{1,0:T(8,128)(2,1)} %all-gather.22.cloned.1.call-done, bf16[2048,2048]{1,0:T(8,128)(2,1)} %all-gather.24.cloned.1.call-done), kind=kOutput, calls=%fused_computation.9 | convolution fusion | flops 5927206912 | bytes 31457280 | tf_op jit(solution)/shard_map/dot_general | solution.py:25
  519.2 14.1 %fusion.9 = f32[2048,2048]{1,0:T(8,128)} fusion(bf16[2048,704]{0,1:T(8,128)(2,1)S(1)} %get-tuple-element.68, bf16[2048,1408]{0,1:T(8,128)(2,1)} %all-gather.20.cloned.1.call-done), kind=kOutput, calls=%fused_computation.27 | convolution fusion | flops 5905580032 | bytes 22544384 | tf_op jit(solution)/shard_map/dot_general | solution.py:25
  533.3 13.1 %add_convert_fusion = bf16[2048,2048]{1,0:T(8,128)(2,1)} fusion(f32[2048,2048]{1,0:T(8,128)} %fusion.9, bf16[2048,704]{0,1:T(8,128)(2,1)S(1)} %get-tuple-element.67, bf16[2048,1408]{0,1:T(8,128)(2,1)} %all-gather.20.cloned.1.call-done), kind=kOutput, calls=%fused_computation | convolution fusion | flops 5913968640 | bytes 30932992 | tf_op jit(solution)/shard_map/dot_general | solution.py:25
  546.5 11.5 convolution_convert_fusion.1
  558.5 59.0 %reduce-scatter.12.cloned.1.call-done = bf16[256,2048]{1,0:T(8,128)(2,1)} async-done(((bf16[2048,2048]{1,0:T(8,128)(2,1)}), bf16[256,2048]{1,0:T(8,128)(2,1)}) %reduce-scatter.12.cloned.1.call-update) | async-done | bytes 1048592 | tf_op jit(solution)/shard_map/reduce_scatter | solution.py:274
  617.5 2.0 fusion.18
  619.5 73.1 %reduce-scatter.10.cloned.1.call-done = bf16[256,2048]{1,0:T(8,128)(2,1)} async-done(((bf16[2048,2048]{1,0:T(8,128)(2,1)}), bf16[256,2048]{1,0:T(8,128)(2,1)}) %reduce-scatter.10.cloned.1.call-update) | async-done | bytes 1048592 | tf_op jit(solution)/shard_map/reduce_scatter | solution.py:274
  692.6 4.1 fusion.17
  696.7 6.5 convolution_convert_fusion.7
  703.8 17.3 %all_to_all.36 = bf16[8,2,1,128,256]{4,3,1,2,0:T(8,128)(2,1)S(1)} all-to-all(bf16[8,2,1,128,256]{4,3,1,2,0:T(8,128)(2,1)S(1)} %bitcast.159), channel_id=1, replica_groups=mesh['dp'=4,'seq'=8] {'seq'}, dimensions={0} | all-to-all | bytes 2097152 | tf_op jit(solution)/shard_map/all_to_all | solution.py:249
  722.1 24.7 %attend_back.1 = (bf16[2,1024,32]{2,1,0:T(8,128)(2,1)}, bf16[2,1024,32]{2,1,0:T(8,128)(2,1)}, bf16[2,1024,256]{2,1,0:T(8,128)(2,1)}) custom-call(bf16[2,1024,32]{2,1,0:T(8,128)(2,1)} %bitcast.142, bf16[2,1024,32]{2,1,0:T(8,128)(2,1)} %bitcast.140, bf16[2,1024,256]{2,1,0:T(8,128)(2,1)} %bitcast.138, s32[2,1024,1]{2,1,0:T(8,128)} %copy-done.2, ...), custom_call_target="tpu_custom_call" | custom-call | tf_op jit(solution)/shard_map/attend_back/pallas_call | solution.py:122
  746.7 2.0 pad_maximum_fusion.3
  748.8 4.8 convolution_convert_fusion
  753.6 3.6 fusion.26
  758.2 9.6 convolution_convert_fusion.3
  767.8 9.0 convolution_convert_fusion.4
  776.8 3.2 pad_maximum_fusion
  780.1 7.8 fusion.5
  789.7 1.8 concatenate.40
  791.5 5.6 convolution_convert_fusion.2
  797.2 11.3 reduce-scatter.16.cloned.1.call-done
  808.5 2.2 convert_bitcast_fusion
  810.7 52.8 %reduce-scatter.14.cloned.1.call-done = bf16[128,2048]{1,0:T(8,128)(2,1)} async-done(((bf16[1024,2048]{1,0:T(8,128)(2,1)}), bf16[128,2048]{1,0:T(8,128)(2,1)}) %reduce-scatter.14.cloned.1.call-update) | async-done | bytes 524304 | tf_op jit(solution)/shard_map/reduce_scatter | solution.py:274
  863.6 2.2 convert_bitcast_fusion.2
  867.5 13.9 %concatenate.38 = bf16[4,8,64,2050]{3,2,1,0:T(8,128)(2,1)} concatenate(bf16[4,8,64,2048]{3,2,1,0:T(8,128)(2,1)} %convolution_convert_fusion.2, bf16[4,8,64,1]{3,2,1,0:T(8,128)(2,1)S(1)} %concatenate.39, bf16[4,8,64,1]{3,2,1,0:T(8,128)(2,1)} %concatenate.40), dimensions={3} | concatenate | bytes 16793600 | tf_op jit(solution)/shard_map/concatenate | solution.py:338
  881.4 10.7 convolution_convert_fusion.5
  892.1 75.9 %reduce-scatter.20.cloned.1.call-done = bf16[512,1408]{0,1:T(8,128)(2,1)} async-done(((bf16[2048,1408]{0,1:T(8,128)(2,1)}), bf16[512,1408]{0,1:T(8,128)(2,1)}) %reduce-scatter.20.cloned.1.call-update) | async-done | bytes 1441808 | tf_op jit(solution)/shard_map/reduce_scatter | solution.py:281
  968.0 34.3 %reduce-scatter.18.cloned.1.call-done = bf16[512,320]{0,1:T(8,128)(2,1)} async-done(((bf16[2048,320]{0,1:T(8,128)(2,1)}), bf16[512,320]{0,1:T(8,128)(2,1)}) %reduce-scatter.18.cloned.1.call-update) | async-done | bytes 327696 | tf_op jit(solution)/shard_map/reduce_scatter | solution.py:308
  1003.8 2.5 copy.109
  1006.3 4.5 all-to-all-start.2
  1011.7 143.3 %all-reduce.3.cloned.1.call-done = bf16[8,4,64,2050]{3,2,0,1:T(8,128)(2,1)} async-done(((bf16[8,4,64,2050]{3,2,0,1:T(8,128)(2,1)}), bf16[8,4,64,2050]{3,2,0,1:T(8,128)(2,1)}) %all-reduce.3.cloned.1.call-update) | async-done | bytes 8396816
  1155.0 3.0 dynamic-slice_bitcast_fusion
  1158.0 56.0 %reduce-scatter.24.cloned.1.call-done = bf16[176,2048]{1,0:T(8,128)(2,1)} async-done(((bf16[704,2048]{1,0:T(8,128)(2,1)}), bf16[176,2048]{1,0:T(8,128)(2,1)}) %reduce-scatter.24.cloned.1.call-update) | async-done | bytes 720912 | tf_op jit(solution)/shard_map/reduce_scatter | solution.py:278
  1213.9 2.4 convert_element_type.125
  1216.3 2.2 fusion.27
  1218.5 3.9 reshape.201
  1222.4 4.2 copy.117
  1226.6 3.3 reshape.202
  1230.2 1.8 copy-done.11
  1235.8 3.0 reshape.199
  1238.8 2.6 copy.116
  1241.4 3.3 reshape.200
  1244.6 4.2 fusion.21
  (144 shorter events, 41.4 us)
Async XLA Ops:
  7.2 1.6 copy-start
  7.2 32.9 %all-gather.14.cloned.1.call-start = ((), (), s32[]{:S(2)}) async-start(), calls=%async_computation.12 | async-start | bytes 1310720 | tf_op jit(solution)/shard_map/all_gather | solution.py:206
  9.5 69.9 %all-gather.26.cloned.1.call-start = ((), (), s32[]{:S(2)}) async-start(), calls=%async_computation.26 | async-start | bytes 4718592 | tf_op jit(solution)/shard_map/all_gather | solution.py:228
  22.8 4.5 copy-start.19
  22.9 4.5 copy-start.15
  22.9 4.5 copy-start.17
  22.9 4.5 copy-start.18
  25.6 93.0 %all-gather.28.cloned.1.call-start = ((), (), s32[]{:S(2)}) async-start(), calls=%async_computation.27 | async-start | bytes 4718592 | tf_op jit(solution)/shard_map/all_gather | solution.py:228
  26.3 130.9 %all-gather.12.cloned.1.call-start = ((), (), s32[]{:S(2)}) async-start(), calls=%async_computation.11 | async-start | bytes 1966080 | tf_op jit(solution)/shard_map/all_gather | solution.py:206
  28.4 197.1 %all-gather.16.cloned.1.call-start = ((), (), s32[]{:S(2)}) async-start(), calls=%async_computation.13 | async-start | bytes 9437184 | tf_op jit(solution)/shard_map/all_gather | solution.py:211
  40.1 292.8 %all-gather.20.cloned.1.call-start = ((), (), s32[]{:S(2)}) async-start(), calls=%async_computation.15 | async-start | bytes 7208960 | tf_op jit(solution)/shard_map/all_gather | solution.py:206
  58.3 1.3 copy-start.21
  59.6 328.7 %all-gather.18.cloned.1.call-start = ((), (), s32[]{:S(2)}) async-start(), calls=%async_computation.14 | async-start | bytes 9437184 | tf_op jit(solution)/shard_map/all_gather | solution.py:260
  60.3 108.7 %copy-start.2 = (s32[2,1024,1]{2,1,0:T(8,128)}, s32[2,1024,1]{2,1,0:T(8,128)S(1)}, u32[]{:S(2)}) copy-start(s32[2,1024,1]{2,1,0:T(8,128)S(1)} %copy.100.first_ref) | copy-start | bytes 24580
  163.9 1.1 copy-start.14
  165.6 15.9 %copy-start.3 = (bf16[2048,256]{1,0:T(8,128)(2,1)}, bf16[2048,256]{1,0:T(8,128)(2,1)S(1)}, u32[]{:S(2)}) copy-start(bf16[2048,256]{1,0:T(8,128)(2,1)S(1)} %copy.99) | copy-start | bytes 3145732
  169.0 1.1 copy-start.5
  170.1 1.0 copy-start.6
  181.5 28.4 %copy-start.4 = (bf16[2,1024,256]{2,1,0:T(8,128)(2,1)}, bf16[2,1024,256]{2,1,0:T(8,128)(2,1)S(1)}, u32[]{:S(2)}) copy-start(bf16[2,1024,256]{2,1,0:T(8,128)(2,1)S(1)} %attend.1.att_ref) | copy-start | bytes 3145732
  181.6 43.9 %copy-start.9 = (bf16[1,2,128,2048]{3,2,1,0:T(8,128)(2,1)S(1)}, bf16[1,2,128,2048]{3,2,1,0:T(8,128)(2,1)}, u32[]{:S(2)}) copy-start(bf16[1,2,128,2048]{3,2,1,0:T(8,128)(2,1)} %param.12) | copy-start | bytes 3145732
  231.8 385.7 %copy-start.8 = (f32[256,2048]{1,0:T(8,128)}, f32[256,2048]{1,0:T(8,128)S(1)}, u32[]{:S(2)}) copy-start(f32[256,2048]{1,0:T(8,128)S(1)} %get-tuple-element.89) | copy-start | bytes 6291460
  233.2 215.3 %all-gather.22.cloned.1.call-start = ((), (), s32[]{:S(2)}) async-start(), calls=%async_computation.16 | async-start | bytes 3604480 | tf_op jit(solution)/shard_map/all_gather | solution.py:206
  235.5 268.5 %all-gather.24.cloned.1.call-start = ((), (), s32[]{:S(2)}) async-start(), calls=%async_computation.18 | async-start | bytes 9437184 | tf_op jit(solution)/shard_map/all_gather | solution.py:261
  236.2 381.2 %reduce-scatter.12.cloned.1.call-start = ((), (), s32[]{:S(2)}) async-start(), calls=%async_computation.19 | async-start | bytes 9437184 | tf_op jit(solution)/shard_map/reduce_scatter | solution.py:274
  388.2 12.1 copy-start.22
  388.2 12.1 copy-start.23
  519.1 14.1 %copy-start.27 = (bf16[2048,704]{0,1:T(8,128)(2,1)}, bf16[2048,704]{0,1:T(8,128)(2,1)S(1)}, u32[]{:S(2)}) copy-start(bf16[2048,704]{0,1:T(8,128)(2,1)S(1)} %get-tuple-element.68) | copy-start | bytes 8650756
  519.1 14.1 %copy-start.26 = (bf16[2048,704]{0,1:T(8,128)(2,1)}, bf16[2048,704]{0,1:T(8,128)(2,1)S(1)}, u32[]{:S(2)}) copy-start(bf16[2048,704]{0,1:T(8,128)(2,1)S(1)} %get-tuple-element.67) | copy-start | bytes 8650756
  546.4 146.2 %reduce-scatter.10.cloned.1.call-start = ((), (), s32[]{:S(2)}) async-start(), calls=%async_computation.17 | async-start | bytes 9437184 | tf_op jit(solution)/shard_map/reduce_scatter | solution.py:274
  558.0 134.6 %copy-start.12 = (bf16[1,2,128,2048]{3,2,1,0:T(8,128)(2,1)S(1)}, bf16[1,2,128,2048]{3,2,1,0:T(8,128)(2,1)}, u32[]{:S(2)}) copy-start(bf16[1,2,128,2048]{3,2,1,0:T(8,128)(2,1)} %param.23) | copy-start | bytes 3145732
  558.0 250.5 %reduce-scatter.16.cloned.1.call-start = ((), (), s32[]{:S(2)}) async-start(), calls=%async_computation.21 | async-start | bytes 4718592 | tf_op jit(solution)/shard_map/reduce_scatter | solution.py:274
  696.7 94.8 %copy-start.7 = (f32[256,2048]{1,0:T(8,128)}, f32[256,2048]{1,0:T(8,128)S(1)}, u32[]{:S(2)}) copy-start(f32[256,2048]{1,0:T(8,128)S(1)} %get-tuple-element.74) | copy-start | bytes 6291460
  746.7 2.0 copy-start.24
  748.7 4.9 copy-start.13
  757.2 106.4 %reduce-scatter.14.cloned.1.call-start = ((), (), s32[]{:S(2)}) async-start(), calls=%async_computation.20 | async-start | bytes 4718592 | tf_op jit(solution)/shard_map/reduce_scatter | solution.py:274
  758.0 210.1 %reduce-scatter.20.cloned.1.call-start = ((), (), s32[]{:S(2)}) async-start(), calls=%async_computation.23 | async-start | bytes 7208960 | tf_op jit(solution)/shard_map/reduce_scatter | solution.py:281
  758.2 9.6 copy-start.28
  780.0 222.3 %reduce-scatter.18.cloned.1.call-start = ((), (), s32[]{:S(2)}) async-start(), calls=%async_computation.22 | async-start | bytes 1638400 | tf_op jit(solution)/shard_map/reduce_scatter | solution.py:308
  788.0 367.0 %all-reduce.3.cloned.1.call-start = ((), (), s32[]{:S(2)}) async-start(), calls=%async_computation.28 | async-start | bytes 17825792
  797.2 68.7 %copy-start.10 = (bf16[1,2,128,2048]{3,2,1,0:T(8,128)(2,1)S(1)}, bf16[1,2,128,2048]{3,2,1,0:T(8,128)(2,1)}, u32[]{:S(2)}) copy-start(bf16[1,2,128,2048]{3,2,1,0:T(8,128)(2,1)} %param.12) | copy-start | bytes 3145732
  797.2 68.7 %copy-start.16 = (f32[2048,1]{0,1:T(1,128)S(1)}, f32[2048,1]{0,1:T(1,128)}, u32[]{:S(2)}) copy-start(f32[2048,1]{0,1:T(1,128)} %copy-done.15) | copy-start | bytes 24580
  797.2 68.7 %copy-start.20 = (f32[2,128]{1,0:T(2,128)S(1)}, f32[2,128]{1,0:T(2,128)}, u32[]{:S(2)}) copy-start(f32[2,128]{1,0:T(2,128)} %copy-done.19) | copy-start | bytes 3076
  881.4 332.6 %reduce-scatter.24.cloned.1.call-start = ((), (), s32[]{:S(2)}) async-start(), calls=%async_computation.25 | async-start | bytes 3604480 | tf_op jit(solution)/shard_map/reduce_scatter | solution.py:278
  1003.8 7.3 copy-start.25
  1006.3 210.0 %all-to-all-start.2 = ((bf16[8,64,1728]{2,1,0:T(8,128)(2,1)}), bf16[8,64,1728]{2,1,0:T(8,128)(2,1)S(1)}, u32[]{:S(2)}, u32[]{:S(2)}) async-start(bf16[8,64,1728]{2,1,0:T(8,128)(2,1)} %bitcast.150), calls=%async_computation.8 | async-start | bytes 3670016 | tf_op jit(solution)/shard_map/all_to_all | solution.py:312
  1010.8 238.0 %reduce-scatter.22.cloned.1.call-start = ((), (), s32[]{:S(2)}) async-start(), calls=%async_computation.24 | async-start | bytes 1392640 | tf_op jit(solution)/shard_map/reduce_scatter | solution.py:341
  1230.2 1.8 copy-start.11
  1244.6 6.7 copy-start.1
Sparse Core Ops, SparseCore 0:
  10.2 29.8 all-gather.13
  42.6 36.8 all-gather.25
  81.9 36.7 all-gather.27
  120.6 36.5 all-gather.11
  158.9 66.5 all-gather.15
  227.6 105.2 all-gather.19
  335.4 52.8 all-gather.17
  389.8 58.7 all-gather.21
  450.5 53.5 all-gather.23
  546.5 70.8 reduce-scatter.11
  621.3 71.2 reduce-scatter.9
  757.3 51.1 reduce-scatter.15
  812.2 51.3 reduce-scatter.13
  865.7 102.2 reduce-scatter.19
  970.8 31.4 reduce-scatter.17
  1005.7 149.2 all-reduce.2
  1157.2 56.6 reduce-scatter.23
  1216.2 28.0 reduce-scatter.21

commit v2 on v1

--- a/solution.py
+++ b/solution.py
@@ -143,6 +143,215 @@
         compiler_params=pltpu.CompilerParams(vmem_limit_bytes=56 * MIB),
         name="attend_back",
     )(query, key, value, first, attended, grad)
+
+MESH = pl.DeviceIdType.MESH
+LOW = jnp.bfloat16
+
+
+def partners():
+    me = lax.axis_index("seq")
+    core, x, y = me % 2, me // 2 % 2, me // 4
+    return me, me + 1 - 2 * core, me + 2 - 4 * x, me + 4 - 8 * y
+
+
+def greet(others):
+    barrier = pltpu.get_barrier_semaphore()
+    for other in others:
+        pl.semaphore_signal(barrier, inc=1, device_id={"seq": other}, device_id_type=MESH)
+    pl.semaphore_wait(barrier, len(others))
+
+
+def remote(send, recv, k, src, dst, to):
+    return pltpu.make_async_remote_copy(
+        src_ref=src,
+        dst_ref=dst,
+        send_sem=send.at[k],
+        recv_sem=recv.at[k],
+        device_id={"seq": to},
+        device_id_type=MESH,
+    )
+
+
+def gather_kernel(x_ref, o_ref, send, recv, own_sem):
+    me, sib, xn, yn = partners()
+    diag = xn + yn - me
+    half = x_ref.shape[0] // 2
+    copy = functools.partial(remote, send, recv)
+    upper, lower = pl.ds(0, half), pl.ds(half, half)
+    greet((sib, xn, yn))
+    own = pltpu.make_async_copy(x_ref, o_ref.at[me], own_sem)
+    own.start()
+    xa = copy(0, x_ref.at[upper], o_ref.at[me, upper], xn)
+    yb = copy(1, x_ref.at[lower], o_ref.at[me, lower], yn)
+    xb = copy(2, x_ref.at[lower], o_ref.at[me, lower], xn)
+    ya = copy(3, x_ref.at[upper], o_ref.at[me, upper], yn)
+    beside = [copy(4, x_ref, o_ref.at[me], sib)]
+    started = [xa, yb, xb, ya, beside[0]]
+    for c in started:
+        c.start()
+
+    def pass_on(k, origin, part, to):
+        block = o_ref.at[origin, part]
+        c = copy(k, block, block, to)
+        c.start()
+        started.append(c)
+        return c
+
+    xa.wait_recv()
+    fy = pass_on(5, xn, upper, yn)
+    beside.append(pass_on(6, xn, upper, sib))
+    yb.wait_recv()
+    fx = pass_on(7, yn, lower, xn)
+    beside.append(pass_on(8, yn, lower, sib))
+    xb.wait_recv()
+    beside.append(pass_on(9, xn, lower, sib))
+    ya.wait_recv()
+    beside.append(pass_on(10, yn, upper, sib))
+    fy.wait_recv()
+    beside.append(pass_on(11, diag, upper, sib))
+    fx.wait_recv()
+    beside.append(pass_on(12, diag, lower, sib))
+    own.wait()
+    for c in beside:
+        c.wait_recv()
+    for c in started:
+        c.wait_send()
+
+
+def moved(nbytes):
+    return pl.CostEstimate(flops=0, bytes_accessed=nbytes * 10, transcendentals=0)
+
+
+def gather_plane(x, number):
+    pieces = lax.axis_size("seq")
+    if pieces != 8:
+        return lax.all_gather(x, "seq", axis=0)
+    return pl.pallas_call(
+        gather_kernel,
+        out_shape=jax.ShapeDtypeStruct((8,) + x.shape, x.dtype),
+        in_specs=[pl.BlockSpec(memory_space=pl.ANY)],
+        out_specs=pl.BlockSpec(memory_space=pl.ANY),
+        scratch_shapes=[
+            pltpu.SemaphoreType.DMA((13,)),
+            pltpu.SemaphoreType.DMA((13,)),
+            pltpu.SemaphoreType.DMA,
+        ],
+        compiler_params=pltpu.CompilerParams(collective_id=number, has_side_effects=True),
+        cost_estimate=moved(16 * x.size),
+        name="gather",
+    )(x)
+
+
+def scatter_kernel(p_ref, o_ref, held, got, one, two, send, recv, own_sem):
+    me, sib, xn, yn = partners()
+    diag = xn + yn - me
+    half = p_ref.shape[1] // 2
+    copy = functools.partial(remote, send, recv)
+    upper, lower = pl.ds(0, half), pl.ds(half, half)
+    greet((sib, xn, yn))
+    beside, loads = [], []
+    for i, owner in enumerate((diag, xn, yn, me)):
+        beside.append(copy(i, p_ref.at[owner + sib - me], got.at[i], sib))
+        loads.append(pltpu.make_async_copy(p_ref.at[owner], held.at[i], own_sem.at[i]))
+        beside[i].start()
+        loads[i].start()
+
+    def pair_sum(i):
+        beside[i].wait_recv()
+        loads[i].wait()
+        held[i] = held[i] + got[i]
+
+    pair_sum(0)
+    x0 = copy(4, held.at[0, upper], one.at[0], xn)
+    x0.start()
+    y0 = copy(5, held.at[0, lower], one.at[1], yn)
+    y0.start()
+    pair_sum(1)
+    x1 = copy(6, held.at[1, upper], one.at[2], xn)
+    x1.start()
+    pair_sum(2)
+    y1 = copy(7, held.at[2, lower], one.at[3], yn)
+    y1.start()
+    pair_sum(3)
+    x0.wait_recv()
+    held[2, :half] = held[2, :half] + one[0]
+    y2 = copy(8, held.at[2, upper], two.at[0], yn)
+    y2.start()
+    y0.wait_recv()
+    held[1, half:] = held[1, half:] + one[1]
+    x2 = copy(9, held.at[1, lower], two.at[1], xn)
+    x2.start()
+    x1.wait_recv()
+    y1.wait_recv()
+    y2.wait_recv()
+    wide = jnp.float32
+    o_ref[:half] = held[3, :half].astype(wide) + one[2].astype(wide) + two[0].astype(wide)
+    x2.wait_recv()
+    o_ref[half:] = held[3, half:].astype(wide) + one[3].astype(wide) + two[1].astype(wide)
+    for c in (*beside, x0, y0, x1, y1, y2, x2):
+        c.wait_send()
+
+
+def scatter_plane(part, number):
+    pieces, rows, columns = part.shape
+    if pieces != 8:
+        return lax.psum_scatter(part, "seq", scatter_dimension=0).astype(jnp.float32)
+    return pl.pallas_call(
+        scatter_kernel,
+        out_shape=jax.ShapeDtypeStruct((rows, columns), jnp.float32),
+        in_specs=[pl.BlockSpec(memory_space=pl.ANY)],
+        out_specs=pl.BlockSpec(memory_space=pltpu.VMEM),
+        scratch_shapes=[
+            pltpu.VMEM((4, rows, columns), LOW),
+            pltpu.VMEM((4, rows, columns), LOW),
+            pltpu.VMEM((4, rows // 2, columns), LOW),
+            pltpu.VMEM((2, rows // 2, columns), LOW),
+            pltpu.SemaphoreType.DMA((10,)),
+            pltpu.SemaphoreType.DMA((10,)),
+            pltpu.SemaphoreType.DMA((4,)),
+        ],
+        compiler_params=pltpu.CompilerParams(
+            collective_id=number, has_side_effects=True, vmem_limit_bytes=40 * MIB
+        ),
+        cost_estimate=moved(2 * part.size),
+        name="scatter",
+    )(part)
+
+
+def exchange_kernel(x_ref, o_ref, send, recv, own_sem):
+    me = lax.axis_index("seq")
+    others = [lax.rem(me + i, 8) for i in range(1, 8)]
+    greet(others)
+    own = pltpu.make_async_copy(x_ref.at[me], o_ref.at[me], own_sem)
+    own.start()
+    copies = [
+        remote(send, recv, i, x_ref.at[other], o_ref.at[me], other)
+        for i, other in enumerate(others)
+    ]
+    for c in copies:
+        c.start()
+    own.wait()
+    for c in copies:
+        c.wait()
+
+
+def exchange_plane(x, number):
+    if lax.axis_size("seq") != 8:
+        return lax.all_to_all(x, "seq", 0, 0)
+    return pl.pallas_call(
+        exchange_kernel,
+        out_shape=jax.ShapeDtypeStruct(x.shape, x.dtype),
+        in_specs=[pl.BlockSpec(memory_space=pl.ANY)],
+        out_specs=pl.BlockSpec(memory_space=pl.ANY),
+        scratch_shapes=[
+            pltpu.SemaphoreType.DMA((7,)),
+            pltpu.SemaphoreType.DMA((7,)),
+            pltpu.SemaphoreType.DMA,
+        ],
+        compiler_params=pltpu.CompilerParams(collective_id=number, has_side_effects=True),
+        cost_estimate=moved(4 * x.size),
+        name="exchange",
+    )(x)
 
 
 def norm_scale(rows):
@@ -179,38 +388,42 @@
     first_stream = place % sharers * streams
     qk, wide = heads * QK_DIM, heads * HEAD_V
     hidden = FF // pieces
-    low = jnp.bfloat16
-
+
+    out_width = D // pieces
     attn_slice = jnp.concatenate(
         [
             lax.dynamic_slice_in_dim(w_value, first_head * HEAD_V, wide, 1),
+            lax.dynamic_slice_in_dim(w_out, place * out_width, out_width, 1),
             lax.dynamic_slice_in_dim(w_query, first_head * QK_DIM, qk, 1),
             lax.dynamic_slice_in_dim(w_key, first_head * QK_DIM, qk, 1),
+            gain_attn[:, None],
+            gain_mlp[:, None],
         ],
         axis=1,
     )
     rows_dp = w_gate.shape[0]
     share = hidden // groups
+    block = FF // groups
 
     def hidden_columns(w):
-        return lax.dynamic_slice_in_dim(
-            w.reshape(rows_dp, groups, pieces, share), place, 1, 2
-        ).reshape(rows_dp, hidden)
-
-    ffn_slice = jnp.concatenate([hidden_columns(w_gate), hidden_columns(w_up)], axis=1)
+        return [
+            lax.dynamic_slice_in_dim(w, z * block + place * share, share, 1) for z in range(groups)
+        ]
+
+    ffn_slice = jnp.concatenate(hidden_columns(w_gate) + hidden_columns(w_up), axis=1)
     down_slice = lax.dynamic_slice_in_dim(w_down, place * share, share, 0)
-    out_width = D // pieces
-    out_slice = lax.dynamic_slice_in_dim(w_out, place * out_width, out_width, 1)
 
     def gather_dp(w):
         return lax.all_gather(w, "dp", axis=0, tiled=True)
 
-    gains = gather_dp(jnp.stack([gain_attn, gain_mlp], axis=1)).astype(jnp.float32)
-    gain_one, gain_two = gains[:, 0], gains[:, 1]
-    attn_full = gather_dp(attn_slice)
-    out_full = lax.all_gather(gather_dp(out_slice), "seq", axis=1, tiled=True)
+    attn_got = gather_dp(attn_slice)
     ffn_full = gather_dp(ffn_slice)
     down_full = gather_dp(down_slice)
+    value_full = attn_got[:, :wide]
+    query_full = attn_got[:, wide + out_width : wide + out_width + qk]
+    key_full = attn_got[:, wide + out_width + qk : wide + out_width + 2 * qk]
+    gains = attn_got[:, wide + out_width + 2 * qk :].astype(jnp.float32)
+    gain_one, gain_two = gains[:, 0], gains[:, 1]
     gate_full, up_full = ffn_full[:, :hidden], ffn_full[:, hidden:]
 
     lengths = lax.dynamic_slice_in_dim(doc_lengths[0], first_stream, streams, 0)
@@ -219,139 +432,131 @@
     begun = starts[:, None, :] <= position[None, :, None]
     first = jnp.max(jnp.where(begun, starts[:, None, :], 0), axis=2)[..., None]
 
-    rows = tokens[0].astype(jnp.float32)
-    inverse_one = norm_scale(rows)
-    plain_one = rows * inverse_one
-    h_one = (plain_one * gain_one).astype(low)
-    if sharers == 1:
-        h_all = jnp.stack(
-            [lax.all_gather(h_one[m], "seq", axis=0, tiled=True) for m in range(micro)]
-        )
-    else:
-        h_all = lax.all_gather(h_one, "seq", axis=1, tiled=True)
-        h_all = lax.dynamic_slice_in_dim(h_all, first_stream, streams, 0)
-    h_flat = h_all.reshape(streams * length, D)
-    projected = dot(h_flat, attn_full).astype(low)
-    value = projected[:, :wide].reshape(streams, length, wide)
-    query = projected[:, wide : wide + qk].reshape(streams, length, qk)
-    key = projected[:, wide + qk :].reshape(streams, length, qk)
+    mine = micro * span
+    cot = cotangent[0].reshape(mine, D)
+    x_all = gather_plane(tokens[0].reshape(mine, D), 1)
+    out_full = gather_plane(attn_got[:, wide : wide + out_width], 2)
+    x_all = x_all.reshape(pieces, micro, span, D).transpose(1, 0, 2, 3)
+    x_all = lax.dynamic_slice_in_dim(x_all, first_stream, streams, 0)
+    x_all = x_all.astype(jnp.float32)
+    h_flat = (x_all * norm_scale(x_all) * gain_one).astype(LOW).reshape(streams * length, D)
+    value = dot(h_flat, value_full).astype(LOW).reshape(streams, length, wide)
+    query = dot(h_flat, query_full).astype(LOW).reshape(streams, length, qk)
+    key = dot(h_flat, key_full).astype(LOW).reshape(streams, length, qk)
     att_heads = attend(query, key, value, first, heads)
 
     def to_tokens(by_head):
-        sent = by_head.reshape(streams, pieces, span, wide)
-        got = lax.all_to_all(sent, "seq", 1, 0, tiled=False)
-        got = got.reshape(pieces // sharers, micro, span, wide)
-        return got.transpose(1, 2, 0, 3).reshape(micro * span, HEADS * HEAD_V)
+        sent = by_head.reshape(streams, pieces, span, wide).transpose(1, 0, 2, 3)
+        got = exchange_plane(sent, 3).reshape(pieces // sharers, micro, span, wide)
+        return got.transpose(1, 2, 0, 3).reshape(mine, HEADS * HEAD_V)
 
     def to_heads(by_token):
         sent = by_token.reshape(micro, span, pieces // sharers, wide).transpose(2, 0, 1, 3)
-        sent = sent.reshape(pieces, streams, span, wide)
-        got = lax.all_to_all(sent, "seq", 0, 1, tiled=False)
-        return got.reshape(streams, length, wide)
+        got = exchange_plane(sent.reshape(pieces, streams, span, wide), 4)
+        return got.transpose(1, 0, 2, 3).reshape(streams, length, wide)
 
     attended = to_tokens(att_heads)
-    flat = rows.reshape(micro * span, D)
-    mid = flat + dot(attended, out_full)
+    flat = tokens[0].reshape(mine, D).astype(jnp.float32)
+    mid = flat + jnp.einsum(
+        "tk,skn->tsn", attended, out_full, preferred_element_type=jnp.float32
+    ).reshape(mine, D)
     inverse_two = norm_scale(mid)
     plain_two = mid * inverse_two
-    h_two = (plain_two * gain_two).astype(low)
-    cot = cotangent[0].reshape(micro * span, D)
-
-    h_two_all = lax.all_gather(h_two, "seq", axis=0, tiled=True)
-    cot_all = lax.all_gather(cot, "seq", axis=0, tiled=True)
+    h_two = (plain_two * gain_two).astype(LOW)
+
+    h_two_all = gather_plane(h_two, 5).reshape(-1, D)
+    cot_all = gather_plane(cot, 6).reshape(-1, D)
     gate = dot(h_two_all, gate_full)
     up = dot(h_two_all, up_full)
     g_act = contract(cot_all, down_full, 1, 1)
     sigmoid = jax.nn.sigmoid(gate)
     silu = gate * sigmoid
-    act = (silu * up).astype(low)
-    g_gate = (g_act * up * sigmoid * (1.0 + gate * (1.0 - sigmoid))).astype(low)
-    g_up = (g_act * silu).astype(low)
-    g_h_two_part = (contract(g_gate, gate_full, 1, 1) + contract(g_up, up_full, 1, 1)).astype(low)
-    out_part = dot(act, down_full).astype(low)
-
-    def scatter(part):
-        return lax.psum_scatter(part, "seq", scatter_dimension=0, tiled=True).astype(jnp.float32)
-
-    g_h_two = scatter(g_h_two_part)
-    output = (mid + scatter(out_part)).astype(low)
+    act = (silu * up).astype(LOW)
+    g_gate = (g_act * up * sigmoid * (1.0 + gate * (1.0 - sigmoid))).astype(LOW)
+    g_up = (g_act * silu).astype(LOW)
+    g_h_two_part = (contract(g_gate, gate_full, 1, 1) + contract(g_up, up_full, 1, 1)).astype(LOW)
+    g_h_two = scatter_plane(g_h_two_part.reshape(pieces, mine, D), 7)
     grad_down = lax.psum_scatter(
-        contract(act, cot_all, 0, 0).astype(low), "dp", scatter_dimension=0, tiled=True
+        contract(act, cot_all, 0, 0).astype(LOW), "dp", scatter_dimension=0, tiled=True
     ).astype(jnp.float32)
     grad_ffn = lax.psum_scatter(
         jnp.concatenate(
-            [contract(h_two_all, g_gate, 0, 0).astype(low), contract(h_two_all, g_up, 0, 0).astype(low)],
+            [contract(h_two_all, g_gate, 0, 0).astype(LOW), contract(h_two_all, g_up, 0, 0).astype(LOW)],
             axis=1,
         ),
         "dp",
         scatter_dimension=0,
         tiled=True,
     )
+    out_part = dot(act, down_full).astype(LOW)
+    output = (mid + scatter_plane(out_part.reshape(pieces, mine, D), 8)).astype(LOW)
 
     g_mid = cot.astype(jnp.float32) + norm_backward(g_h_two, plain_two, inverse_two, gain_two)
-    g_mid_low = g_mid.astype(low)
-    g_att = to_heads(contract(g_mid_low, out_full, 1, 1).astype(low))
+    g_mid_low = g_mid.astype(LOW)
+    g_att = jnp.einsum(
+        "tsn,skn->tk",
+        g_mid_low.reshape(mine, pieces, out_width),
+        out_full,
+        preferred_element_type=jnp.float32,
+    )
+    g_att = to_heads(g_att.astype(LOW))
     g_query, g_key, g_value = attend_back(query, key, value, first, att_heads, g_att, heads)
-    g_all = jnp.concatenate([g_value, g_query, g_key], axis=2).reshape(streams * length, -1)
-    g_h_one_part = contract(g_all, attn_full, 1, 1).astype(low).reshape(streams, length, D)
-    if sharers == 1:
-        g_h_one = jnp.stack([scatter(g_h_one_part[m]) for m in range(micro)])
-    else:
-        padded = jnp.zeros((micro, length, D), low)
-        padded = lax.dynamic_update_slice_in_dim(padded, g_h_one_part, first_stream, 0)
-        g_h_one = lax.psum_scatter(padded, "seq", scatter_dimension=1, tiled=True)
-        g_h_one = g_h_one.astype(jnp.float32)
-    input_grad = g_mid.reshape(micro, span, D) + norm_backward(
-        g_h_one, plain_one, inverse_one, gain_one
-    )
-
-    grad_attn = lax.psum_scatter(
-        contract(h_flat, g_all, 0, 0).astype(low), "dp", scatter_dimension=0, tiled=True
-    )
+    g_value = g_value.reshape(streams * length, wide)
+    g_query = g_query.reshape(streams * length, qk)
+    g_key = g_key.reshape(streams * length, qk)
+    g_h_one_part = (
+        contract(g_value, value_full, 1, 1)
+        + contract(g_query, query_full, 1, 1)
+        + contract(g_key, key_full, 1, 1)
+    ).astype(LOW)
+    g_h_one_part = g_h_one_part.reshape(streams, pieces, span, D).transpose(1, 0, 2, 3)
+    if sharers > 1:
+        padded = jnp.zeros((pieces, micro, span, D), LOW)
+        g_h_one_part = lax.dynamic_update_slice_in_dim(padded, g_h_one_part, first_stream, 1)
+    g_h_one = scatter_plane(g_h_one_part.reshape(pieces, mine, D), 9)
+    inverse_one = norm_scale(flat)
+    plain_one = flat * inverse_one
+    input_grad = g_mid + norm_backward(g_h_one, plain_one, inverse_one, gain_one)
+
     own = rows_dp // pieces
-    exchanged = lax.all_to_all(
-        jnp.concatenate([grad_attn, grad_ffn], axis=1).reshape(pieces, own, -1), "seq", 0, 0
-    ).astype(jnp.float32)
-    attn_got = exchanged[:, :, : wide + 2 * qk]
+    grad_out = contract(attended, g_mid_low, 0, 0).astype(LOW)
+    grad_out = grad_out.reshape(groups, pieces, own, D).transpose(1, 0, 2, 3)
+    grad_out = scatter_plane(grad_out.reshape(pieces, groups * own, D), 10).astype(LOW)
+    grad_out = lax.psum_scatter(grad_out, "dp", scatter_dimension=0, tiled=True)
+    grad_attn = jnp.concatenate(
+        [
+            contract(h_flat, g_value, 0, 0).astype(LOW),
+            contract(h_flat, g_query, 0, 0).astype(LOW),
+            contract(h_flat, g_key, 0, 0).astype(LOW),
+            jnp.sum(g_h_one * plain_one, axis=0).astype(LOW)[:, None],
+            jnp.sum(g_h_two * plain_two, axis=0).astype(LOW)[:, None],
+        ],
+        axis=1,
+    )
+    grad_attn = lax.psum_scatter(grad_attn, "dp", scatter_dimension=0, tiled=True)
+    ffn_got = exchange_plane(grad_ffn.reshape(pieces, own, 2 * hidden), 11).astype(jnp.float32)
+    attn_got = exchange_plane(grad_attn.reshape(pieces, own, -1), 12).astype(jnp.float32)
+    grad_gains = jnp.sum(attn_got[:, :, wide + 2 * qk :], axis=0)
     attn_got = jnp.sum(attn_got.reshape(pieces // sharers, sharers, own, -1), axis=1)
 
     def by_rows(block):
         return block.transpose(1, 0, 2).reshape(own, -1)
 
-    grad_value = by_rows(attn_got[:, :, :wide])
-    grad_query = by_rows(attn_got[:, :, wide : wide + qk])
-    grad_key = by_rows(attn_got[:, :, wide + qk :])
-
     def by_hidden(block):
         return block.reshape(pieces, own, groups, share).transpose(1, 2, 0, 3).reshape(own, FF)
 
-    ffn_got = exchanged[:, :, wide + 2 * qk :]
-    grad_gate = by_hidden(ffn_got[:, :, :hidden])
-    grad_up = by_hidden(ffn_got[:, :, hidden:])
-    gain_part = jnp.stack(
-        [
-            jnp.sum(g_h_one * plain_one, axis=(0, 1)),
-            jnp.sum(g_h_two * plain_two, axis=0),
-        ],
-        axis=1,
-    )
-    out_part = jnp.concatenate([contract(attended, g_mid_low, 0, 0), gain_part], axis=1)
-    out_part = out_part.astype(low).reshape(groups, pieces, own, -1).transpose(1, 0, 2, 3)
-    out_group = lax.psum_scatter(out_part, "seq", scatter_dimension=0, tiled=False)
-    out_sum = lax.psum_scatter(out_group, "dp", scatter_dimension=0, tiled=False)
-    out_sum = out_sum.astype(jnp.float32)
     return (
         output.reshape(tokens.shape),
-        input_grad[None],
-        grad_query,
-        grad_key,
-        grad_value,
-        out_sum[:, :D],
-        grad_gate,
-        grad_up,
+        input_grad.reshape(tokens.shape),
+        by_rows(attn_got[:, :, wide : wide + qk]),
+        by_rows(attn_got[:, :, wide + qk : wide + 2 * qk]),
+        by_rows(attn_got[:, :, :wide]),
+        grad_out.astype(jnp.float32),
+        by_hidden(ffn_got[:, :, :hidden]),
+        by_hidden(ffn_got[:, :, hidden:]),
         grad_down,
-        out_sum[:, D],
-        out_sum[:, D + 1],
+        grad_gains[:, 0],
+        grad_gains[:, 1],
     )
 
 

time: 1270 us -> 845 us (0.67)
  waiting for transfers between devices: 869 us -> 90.6 us
  Pallas kernels: 35.1 us -> 413 us
  blocking collectives: 55.3 us -> 0 us
  matrix products: 141 us -> 175 us
    pallas_call x0 -> x12, Pallas kernels: none -> 377 us  [the longest x4 161 us: gather_plane(): pl.pallas_call(gather_kernel, out_shape=jax.ShapeDtypeStruct((8,) + x.sha...]
    reduce_scatter x7 -> x3, waiting for transfers between devices: 287 us -> 0.01 us  [the longest x1 0.01 us: local(): grad_out = lax.psum_scatter(grad_out, 'dp', scatter_dimension=0, tiled=True)]
    all_gather x4 -> x3, waiting for transfers between devices: 182 us -> 0.04 us  [gather_dp(): return lax.all_gather(w, 'dp', axis=0, tiled=True)]
    all_gather x5 -> x0, waiting for transfers between devices: 179 us -> none  [the longest x1 55.5 us: local(): cot_all = lax.all_gather(cot, 'seq', axis=0, tiled=True)]
    unnamed x19 -> x7, waiting for transfers between devices: 146 us -> 0.11 us
    all_to_all x2 -> x0, blocking collectives: 44.9 us -> none  [the longest x1 27.7 us: to_tokens(): got = lax.all_to_all(sent, 'seq', 1, 0, tiled=False)]
    dot_general x10 -> x13, matrix products: 96.4 us -> 120 us  [contract(): lax.dot_general(left, right, (((left_dim,), (right_dim,)), ((), ())), pre...]
    convert_element_type x5 -> x9, other arithmetic: 6.71 us -> 25.8 us  [the longest x1 11.2 us: local(): x_all = x_all.astype(jnp.float32)]
  transfers between devices with their start and end apart: 19 -> 7, of which waited for: 17 -> 1; matrix products, arithmetic and copies ran while one was open for 16% -> 26% of each run, Pallas kernels for 1% -> 33%
where the time goes in v2:
time: 845 us; the launch traced here: 838 us
  Pallas kernels  413 us (49%)
  matrix products  175 us (21%)
  local copies, waits for them, and re-layouts  101 us (12%)
  waiting for transfers between devices  90.6 us (11%)
  other arithmetic  41.5 us (5%)
  between operations  15.4 us (2%)
    pallas_call x4, Pallas kernels, gather_plane(): pl.pallas_call(gather_kernel, out_shape=jax.ShapeDtypeStruct((8,) + x.sha...  161 us
    pallas_call x4, Pallas kernels, scatter_plane(): pl.pallas_call(scatter_kernel, out_shape=jax.ShapeDtypeStruct((rows, colu...  159 us
    dot_general x13, matrix products, contract(): lax.dot_general(left, right, (((left_dim,), (right_dim,)), ((), ())), pre...  120 us
    reduce_scatter x1, waiting for transfers between devices, local(): lax.psum_scatter(jnp.concatenate([contract(h_two_all, g_gate, 0, 0).astyp...  90.5 us
    pallas_call x4, Pallas kernels, exchange_plane(): pl.pallas_call(exchange_kernel, out_shape=jax.ShapeDtypeStruct(x.shape, x...  57.7 us
    dot_general x6, matrix products, dot(): return jnp.dot(left, right, preferred_element_type=jnp.float32)  46.4 us
    pallas_call x1, Pallas kernels, attend_back(): pl.pallas_call(functools.partial(attend_back_kernel, heads), grid=(stream...  24.7 us
  transfers between devices with their start and end apart: 7, of which 1 were waited for; matrix products, arithmetic and copies ran while one was open for 26% of the time, Pallas kernels for 33%

profile of v2, /device:TPU:1, one launch (start us, length us, event | category | flops | bytes accessed | tf_op | source)
XLA Modules:
  0.0 838.0 jit_solution(3508175623800278704)
XLA Ops:
  12.2 2.9 constant_dynamic-slice_fusion.1
  15.2 2.4 concatenate.13
  17.6 2.0 constant_dynamic-slice_fusion
  21.3 41.6 %gather.4 = bf16[8,256,2048]{2,1,0:T(8,128)(2,1)} custom-call(bf16[256,2048]{1,0:T(8,128)(2,1)} %bitcast.159), custom_call_target="tpu_custom_call" | custom-call | bytes 83886080 | tf_op jit(solution)/shard_map/gather/pallas_call | solution.py:229
  62.9 39.9 %gather.7 = bf16[8,256,2048]{2,1,0:T(8,128)(2,1)} custom-call(bf16[256,2048]{1,0:T(8,128)(2,1)} %bitcast.161), custom_call_target="tpu_custom_call" | custom-call | bytes 83886080 | tf_op jit(solution)/shard_map/gather/pallas_call | solution.py:229
  102.9 11.2 %bitcast_convert_fusion = f32[8,2,128,2048]{3,2,1,0:T(8,128)} fusion(bf16[8,256,2048]{2,1,0:T(8,128)(2,1)} %gather.4), kind=kLoop, calls=%fused_computation.95 | loop fusion | flops 4194304 | bytes 25165824 | tf_op jit(solution)/shard_map/convert_element_type | solution.py:441
  114.1 7.0 fusion
  123.4 2.3 slice.73.x_ref
  125.6 39.9 %gather.5 = bf16[8,2048,256]{2,1,0:T(8,128)(2,1)} custom-call(bf16[2048,256]{1,0:T(8,128)(2,1)} %slice.73.x_ref), custom_call_target="tpu_custom_call" | custom-call | bytes 83886080 | tf_op jit(solution)/shard_map/gather/pallas_call | solution.py:229
  165.6 11.7 %copy.113 = bf16[8,256,2048]{2,1,0:T(8,128)(2,1)} copy(bf16[8,256,2048]{1,2,0:T(8,128)(2,1)} %bitcast.155) | data formatting | bytes 16777216 | tf_op jit(solution)/shard_map/tk,skn->tsn/dot_general | solution.py:460
  177.3 5.1 fusion.2
  182.4 3.3 copy-done.9
  185.7 3.6 convolution_convert_fusion.10
  189.7 6.3 convolution_convert_fusion.9
  196.3 6.2 convolution_convert_fusion.6
  202.5 10.8 %attend.1.att_ref = bf16[2,1024,256]{2,1,0:T(8,128)(2,1)S(1)} custom-call(bf16[2,1024,32]{2,1,0:T(8,128)(2,1)S(1)} %bitcast.140, bf16[2,1024,32]{2,1,0:T(8,128)(2,1)S(1)} %bitcast.142, bf16[2,1024,256]{2,1,0:T(8,128)(2,1)S(1)} %bitcast.144, s32[2,1024,1]{2,1,0:T(8,128)S(1)} %copy.110.first_ref), custom_call_target="tpu_custom_call" | custom-call | tf_op jit(solution)/shard_map/attend/pallas_call | solution.py:61
  215.4 14.8 %exchange.4 = bf16[8,2,128,256]{3,2,1,0:T(8,128)(2,1)} custom-call(bf16[8,2,128,256]{3,2,1,0:T(8,128)(2,1)} %bitcast.181), custom_call_target="tpu_custom_call" | custom-call | bytes 20971520 | tf_op jit(solution)/shard_map/exchange/pallas_call | solution.py:341
  230.3 1.8 copy.112
  232.4 6.3 multiply_reduce_fusion.3
  241.2 39.7 %gather.6 = bf16[8,256,2048]{2,1,0:T(8,128)(2,1)} custom-call(bf16[256,2048]{1,0:T(8,128)(2,1)} %multiply_convert_fusion.1.x_ref), custom_call_target="tpu_custom_call" | custom-call | bytes 83886080 | tf_op jit(solution)/shard_map/gather/pallas_call | solution.py:229
  280.9 12.9 %fusion.9 = f32[2048,704]{0,1:T(8,128)} fusion(bf16[2048,2048]{1,0:T(8,128)(2,1)} %bitcast.164, bf16[2048,1408]{1,0:T(8,128)(2,1)} %all-gather.6.cloned.1.call-done), kind=kOutput, calls=%fused_computation.23 | convolution fusion | flops 5905580032 | bytes 17301504 | tf_op jit(solution)/shard_map/dot_general | solution.py:21
  293.8 8.2 fusion.13
  302.0 15.9 %fusion.6 = (bf16[2048,704]{0,1:T(8,128)(2,1)}, bf16[2048,704]{0,1:T(8,128)(2,1)S(1)}, bf16[2048,704]{0,1:T(8,128)(2,1)}) fusion(f32[2048,704]{0,1:T(8,128)} %fusion.13, f32[2048,704]{0,1:T(8,128)} %fusion.9, bf16[704,2048]{1,0:T(8,128)(2,1)} %all-gather.8.cloned.1.call-done, bf16[2048,2048]{1,0:T(8,128)(2,1)} %bitcast.162), kind=kOutput, calls=%fused_computation.15 | convolution fusion | flops 5927206912 | bytes 31457280 | tf_op jit(solution)/shard_map/dot_general | solution.py:25
  318.0 10.3 %fusion.11 = f32[2048,2048]{1,0:T(8,128)} fusion(bf16[2048,704]{0,1:T(8,128)(2,1)S(1)} %get-tuple-element.70, bf16[2048,1408]{1,0:T(8,128)(2,1)S(1)} %bitcast.198), kind=kOutput, calls=%fused_computation.25 | convolution fusion | flops 5905580032 | bytes 22806528 | tf_op jit(solution)/shard_map/dot_general | solution.py:25
  328.3 13.2 %add_convert_fusion.1 = bf16[2048,2048]{1,0:T(8,128)(2,1)S(1)} fusion(f32[2048,2048]{1,0:T(8,128)} %fusion.11, bf16[2048,704]{0,1:T(8,128)(2,1)} %get-tuple-element.69, bf16[2048,1408]{1,0:T(8,128)(2,1)} %all-gather.6.cloned.1.call-done), kind=kOutput, calls=%fused_computation.6 | convolution fusion | flops 5913968640 | bytes 31195136 | tf_op jit(solution)/shard_map/dot_general | solution.py:25
  341.4 40.0 %scatter.5 = f32[256,2048]{1,0:T(8,128)S(1)} custom-call(bf16[8,256,2048]{2,1,0:T(8,128)(2,1)S(1)} %bitcast.138), custom_call_target="tpu_custom_call" | custom-call | bytes 83886080 | tf_op jit(solution)/shard_map/scatter/pallas_call | solution.py:299
  383.9 5.6 convolution_convert_fusion
  389.5 2.4 fusion.18
  393.4 15.2 %exchange.5 = bf16[8,2,128,256]{3,2,1,0:T(8,128)(2,1)} custom-call(bf16[8,2,128,256]{3,2,1,0:T(8,128)(2,1)} %bitcast.179), custom_call_target="tpu_custom_call" | custom-call | bytes 20971520 | tf_op jit(solution)/shard_map/exchange/pallas_call | solution.py:341
  408.6 2.3 copy.116
  410.8 24.7 %attend_back.1 = (bf16[2,1024,32]{2,1,0:T(8,128)(2,1)}, bf16[2,1024,32]{2,1,0:T(8,128)(2,1)}, bf16[2,1024,256]{2,1,0:T(8,128)(2,1)}) custom-call(bf16[2,1024,32]{2,1,0:T(8,128)(2,1)} %bitcast.141, bf16[2,1024,32]{2,1,0:T(8,128)(2,1)} %bitcast.143, bf16[2,1024,256]{2,1,0:T(8,128)(2,1)} %bitcast.145, s32[2,1024,1]{2,1,0:T(8,128)} %copy-done.4, ...), custom_call_target="tpu_custom_call" | custom-call | tf_op jit(solution)/shard_map/attend_back/pallas_call | solution.py:122
  435.5 8.3 copy.123
  443.8 3.4 copy-done
  447.2 38.3 %scatter.7 = f32[256,2048]{1,0:T(8,128)S(1)} custom-call(bf16[8,256,2048]{2,1,0:T(8,128)(2,1)S(1)} %bitcast.135), custom_call_target="tpu_custom_call" | custom-call | bytes 83886080 | tf_op jit(solution)/shard_map/scatter/pallas_call | solution.py:299
  487.1 9.7 %fusion.26 = f32[2048,2048]{1,0:T(8,128)} fusion(bf16[2048,256]{1,0:T(8,128)(2,1)} %bitcast.189, bf16[2048,578]{1,0:T(8,128)(2,1)} %all-gather.4.cloned.1.call-done), kind=kOutput, calls=%fused_computation.60 | convolution fusion | flops 2147483648 | bytes 18874368 | tf_op jit(solution)/shard_map/dot_general | solution.py:25
  496.9 9.1 %fusion.31 = f32[2048,2048]{1,0:T(8,128)} fusion(bf16[2048,32]{1,0:T(8,128)(2,1)S(1)} %bitcast.182, bf16[2048,578]{1,0:T(8,128)(2,1)} %all-gather.4.cloned.1.call-done), kind=kOutput, calls=%fused_computation.67 | convolution fusion | flops 268435456 | bytes 17432576 | tf_op jit(solution)/shard_map/dot_general | solution.py:25
  506.0 16.7 %add_convert_fusion = bf16[2048,2048]{1,0:T(8,128)(2,1)} fusion(f32[2048,2048]{1,0:T(8,128)} %fusion.26, f32[2048,2048]{1,0:T(8,128)} %fusion.31, bf16[2048,32]{1,0:T(8,128)(2,1)} %bitcast.184, bf16[2048,578]{1,0:T(8,128)(2,1)} %all-gather.4.cloned.1.call-done), kind=kOutput, calls=%fused_computation.5 | convolution fusion | flops 281018368 | bytes 42991616 | tf_op jit(solution)/shard_map/dot_general | solution.py:25
  522.7 8.3 copy.118
  531.0 3.4 copy-done.1
  534.4 40.4 %scatter.6 = f32[256,2048]{1,0:T(8,128)S(1)} custom-call(bf16[8,256,2048]{2,1,0:T(8,128)(2,1)S(1)} %bitcast.136), custom_call_target="tpu_custom_call" | custom-call | bytes 83886080 | tf_op jit(solution)/shard_map/scatter/pallas_call | solution.py:299
  575.5 6.0 convolution_convert_fusion.8
  583.1 3.3 convolution_convert_fusion.5
  586.4 7.1 concatenate.14
  593.7 10.6 %convolution_convert_fusion.4 = bf16[704,2048]{1,0:T(8,128)(2,1)} fusion(bf16[2048,704]{0,1:T(8,128)(2,1)} %get-tuple-element.71, bf16[2048,2048]{1,0:T(8,128)(2,1)} %bitcast.163), kind=kOutput, calls=%fused_computation.21 | convolution fusion | flops 5907021824 | bytes 14155776 | tf_op jit(solution)/shard_map/dot_general | solution.py:25
  604.3 9.8 %convolution_convert_fusion.2 = bf16[2048,704]{0,1:T(8,128)(2,1)S(1)} fusion(bf16[2048,704]{0,1:T(8,128)(2,1)} %get-tuple-element.69, bf16[2048,2048]{1,0:T(8,128)(2,1)} %bitcast.165), kind=kOutput, calls=%fused_computation.19 | convolution fusion | flops 5907021824 | bytes 14155776 | tf_op jit(solution)/shard_map/dot_general | solution.py:25
  614.1 8.6 %convolution_convert_fusion.3 = bf16[2048,704]{0,1:T(8,128)(2,1)S(1)} fusion(bf16[2048,704]{0,1:T(8,128)(2,1)S(1)} %copy-done.30, bf16[2048,2048]{1,0:T(8,128)(2,1)} %bitcast.166), kind=kOutput, calls=%fused_computation.20 | convolution fusion | flops 5907021824 | bytes 14155776 | tf_op jit(solution)/shard_map/dot_general | solution.py:25
  622.7 3.2 pad_maximum_fusion
  626.0 9.3 %convolution_convert_fusion.1 = bf16[2048,2048]{1,0:T(8,128)(2,1)S(1)} fusion(bf16[2048,704]{0,1:T(8,128)(2,1)} %get-tuple-element.71, bf16[704,2048]{1,0:T(8,128)(2,1)} %all-gather.8.cloned.1.call-done), kind=kOutput, calls=%fused_computation.8 | convolution fusion | flops 5909774336 | bytes 14155776 | tf_op jit(solution)/shard_map/dot_general | solution.py:21
  635.3 40.0 %scatter.4 = f32[256,2048]{1,0:T(8,128)S(1)} custom-call(bf16[8,256,2048]{2,1,0:T(8,128)(2,1)S(1)} %bitcast.139), custom_call_target="tpu_custom_call" | custom-call | bytes 83886080 | tf_op jit(solution)/shard_map/scatter/pallas_call | solution.py:299
  675.3 2.9 fusion.22
  678.2 1.8 convert_element_type.156
  680.0 1.9 copy.119
  681.9 7.9 exchange.6
  694.4 2.4 convert_element_type.161
  696.8 90.5 %reduce-scatter.9.cloned.1.call-done = bf16[512,1408]{0,1:T(8,128)(2,1)} async-done(((bf16[2048,1408]{0,1:T(8,128)(2,1)}), bf16[512,1408]{0,1:T(8,128)(2,1)}) %reduce-scatter.9.cloned.1.call-update) | async-done | bytes 1441808 | tf_op jit(solution)/shard_map/reduce_scatter | solution.py:482
  787.2 2.5 copy.124
  789.8 19.8 %exchange.7 = bf16[8,64,1408]{2,1,0:T(8,128)(2,1)} custom-call(bf16[8,64,1408]{2,1,0:T(8,128)(2,1)} %bitcast.171), custom_call_target="tpu_custom_call" | custom-call | bytes 28835840 | tf_op jit(solution)/shard_map/exchange/pallas_call | solution.py:341
  809.6 3.5 fusion.35
  813.1 3.0 reshape.224
  816.1 2.5 copy.126
  818.6 3.3 reshape.225
  821.9 3.0 reshape.222
  824.9 2.5 copy.125
  827.5 3.3 reshape.223
  (135 shorter events, 26.9 us)
Async XLA Ops:
  7.2 114.0 %all-gather.4.cloned.1.call-start = ((), (), s32[]{:S(2)}) async-start(), calls=%async_computation.4 | async-start | bytes 3276800 | tf_op jit(solution)/shard_map/all_gather | solution.py:417
  12.2 268.7 %all-gather.6.cloned.1.call-start = ((), (), s32[]{:S(2)}) async-start(), calls=%async_computation.5 | async-start | bytes 7208960 | tf_op jit(solution)/shard_map/all_gather | solution.py:417
  15.1 4.6 copy-start.27
  15.2 4.8 copy-start.13
  17.6 284.5 %all-gather.8.cloned.1.call-start = ((), (), s32[]{:S(2)}) async-start(), calls=%async_computation.6 | async-start | bytes 3604480 | tf_op jit(solution)/shard_map/all_gather | solution.py:417
  19.7 658.5 %reduce-scatter.7.cloned.1.call-start = ((), (), s32[]{:S(2)}) async-start(), calls=%async_computation.8 | async-start | bytes 1310720 | tf_op jit(solution)/shard_map/reduce_scatter | solution.py:525
  21.3 181.2 %copy-start.4 = (s32[2,1024,1]{2,1,0:T(8,128)}, s32[2,1024,1]{2,1,0:T(8,128)S(1)}, u32[]{:S(2)}) copy-start(s32[2,1024,1]{2,1,0:T(8,128)S(1)} %copy.110.first_ref) | copy-start | bytes 24580
  123.4 53.9 %copy-start.24 = (f32[2048]{0:T(1024)}, f32[2048]{0:T(1024)S(1)}, u32[]{:S(2)}) copy-start(f32[2048]{0:T(1024)S(1)} %get-tuple-element.66) | copy-start | bytes 24580
  182.4 3.4 copy-start.9
  189.7 12.8 %copy-start.6 = (bf16[2048,32]{1,0:T(8,128)(2,1)}, bf16[2048,32]{1,0:T(8,128)(2,1)S(1)}, u32[]{:S(2)}) copy-start(bf16[2048,32]{1,0:T(8,128)(2,1)S(1)} %copy.108) | copy-start | bytes 393220
  196.3 6.3 copy-start.7
  202.5 12.9 %copy-start.8 = (bf16[2048,256]{1,0:T(8,128)(2,1)}, bf16[2048,256]{1,0:T(8,128)(2,1)S(1)}, u32[]{:S(2)}) copy-start(bf16[2048,256]{1,0:T(8,128)(2,1)S(1)} %convolution_convert_fusion.6) | copy-start | bytes 3145732
  213.4 1.0 copy-start.5
  215.4 17.0 %copy-start.14 = (bf16[1,2,128,2048]{3,2,1,0:T(8,128)(2,1)S(1)}, bf16[1,2,128,2048]{3,2,1,0:T(8,128)(2,1)}, u32[]{:S(2)}) copy-start(bf16[1,2,128,2048]{3,2,1,0:T(8,128)(2,1)} %param.12) | copy-start | bytes 3145732
  232.4 6.3 copy-start.18
  238.7 1.3 copy-start.10
  280.9 12.9 %copy-start.17 = (bf16[8,256,2048]{2,1,0:T(8,128)(2,1)S(1)}, bf16[8,256,2048]{2,1,0:T(8,128)(2,1)}, u32[]{:S(2)}) copy-start(bf16[8,256,2048]{2,1,0:T(8,128)(2,1)} %gather.6) | copy-start | bytes 25165828
  280.9 12.9 %copy-start.28 = (bf16[2048,1408]{1,0:T(8,128)(2,1)S(1)}, bf16[2048,1408]{1,0:T(8,128)(2,1)}, u32[]{:S(2)}) copy-start(bf16[2048,1408]{1,0:T(8,128)(2,1)} %all-gather.6.cloned.1.call-done) | copy-start | bytes 17301508
  293.8 24.1 %slice-start.4 = ((s8[5767168]{0:T(1024)(128)(4,1)}), s8[1572864]{0:T(1024)(128)(4,1)S(1)}, s32[]{:S(2)}) async-start(s8[5767168]{0:T(1024)(128)(4,1)} %bitcast.197), calls=%async_computation.15 | async-start | bytes 3145728
  302.0 15.9 %slice-start.5 = ((s8[5767168]{0:T(1024)(128)(4,1)}), s8[4194304]{0:T(1024)(128)(4,1)S(1)}, s32[]{:S(2)}) async-start(s8[5767168]{0:T(1024)(128)(4,1)} %bitcast.197), calls=%async_computation.16 | async-start | bytes 8388608
  318.0 10.3 %copy-start.29 = (bf16[2048,704]{0,1:T(8,128)(2,1)}, bf16[2048,704]{0,1:T(8,128)(2,1)S(1)}, u32[]{:S(2)}) copy-start(bf16[2048,704]{0,1:T(8,128)(2,1)S(1)} %get-tuple-element.70) | copy-start | bytes 8650756
  341.4 40.0 %copy-start.11 = (f32[256,2048]{1,0:T(8,128)S(1)}, f32[256,2048]{1,0:T(8,128)}, u32[]{:S(2)}) copy-start(f32[256,2048]{1,0:T(8,128)} %copy-done.10) | copy-start | bytes 6291460
  381.4 1.2 copy-start.15
  382.6 1.2 copy-start.19
  382.6 6.9 slice-start.2
  383.9 5.6 slice-start.3
  443.8 3.4 copy-start
  486.7 193.3 %reduce-scatter.5.cloned.1.call-start = ((), (), s32[]{:S(2)}) async-start(), calls=%async_computation.7 | async-start | bytes 1679360 | tf_op jit(solution)/shard_map/reduce_scatter | solution.py:536
  487.1 9.7 %copy-start.20 = (bf16[2,1024,32]{2,1,0:T(8,128)(2,1)S(1)}, bf16[2,1024,32]{2,1,0:T(8,128)(2,1)}, u32[]{:S(2)}) copy-start(bf16[2,1024,32]{2,1,0:T(8,128)(2,1)} %get-tuple-element.15) | copy-start | bytes 393220
  531.0 3.4 copy-start.1
  534.4 40.4 %copy-start.25 = (f32[2048]{0:T(1024)S(1)}, f32[2048]{0:T(1024)}, u32[]{:S(2)}) copy-start(f32[2048]{0:T(1024)} %copy-done.24) | copy-start | bytes 24580
  534.4 40.4 %copy-start.26 = (f32[256]{0:T(256)S(1)}, f32[256]{0:T(256)}, u32[]{:S(2)}) copy-start(f32[256]{0:T(256)} %rsqrt_bitcast_fusion) | copy-start | bytes 3076
  534.4 41.1 %copy-start.21 = (bf16[2,1024,32]{2,1,0:T(8,128)(2,1)S(1)}, bf16[2,1024,32]{2,1,0:T(8,128)(2,1)}, u32[]{:S(2)}) copy-start(bf16[2,1024,32]{2,1,0:T(8,128)(2,1)} %get-tuple-element.15) | copy-start | bytes 393220
  534.4 47.1 %slice-start = ((s8[8388608]{0:T(1024)(128)(4,1)}), s8[4194304]{0:T(1024)(128)(4,1)S(1)}, s32[]{:S(2)}) async-start(s8[8388608]{0:T(1024)(128)(4,1)} %bitcast.150), calls=%async_computation.11 | async-start | bytes 8388608
  574.8 6.7 copy-start.2
  574.8 6.7 slice-start.1
  575.5 6.0 copy-start.22
  581.5 1.6 copy-start.23
  593.6 100.8 %reduce-scatter.11.cloned.1.call-start = ((), (), s32[]{:S(2)}) async-start(), calls=%async_computation.10 | async-start | bytes 3604480 | tf_op jit(solution)/shard_map/reduce_scatter | solution.py:479
  604.2 183.0 %reduce-scatter.9.cloned.1.call-start = ((), (), s32[]{:S(2)}) async-start(), calls=%async_computation.9 | async-start | bytes 7208960 | tf_op jit(solution)/shard_map/reduce_scatter | solution.py:482
  604.3 9.8 %copy-start.30 = (bf16[2048,704]{0,1:T(8,128)(2,1)S(1)}, bf16[2048,704]{0,1:T(8,128)(2,1)}, u32[]{:S(2)}) copy-start(bf16[2048,704]{0,1:T(8,128)(2,1)} %copy-done.29) | copy-start | bytes 8650756
  635.2 40.0 %copy-start.3 = (f32[256,2048]{1,0:T(8,128)S(1)}, f32[256,2048]{1,0:T(8,128)}, u32[]{:S(2)}) copy-start(f32[256,2048]{1,0:T(8,128)} %copy-done.2) | copy-start | bytes 6291460
  635.2 40.0 %copy-start.12 = (f32[256,2048]{1,0:T(8,128)S(1)}, f32[256,2048]{1,0:T(8,128)}, u32[]{:S(2)}) copy-start(f32[256,2048]{1,0:T(8,128)} %copy-done.10) | copy-start | bytes 6291460
  635.2 40.0 %copy-start.16 = (bf16[1,2,128,2048]{3,2,1,0:T(8,128)(2,1)S(1)}, bf16[1,2,128,2048]{3,2,1,0:T(8,128)(2,1)}, u32[]{:S(2)}) copy-start(bf16[1,2,128,2048]{3,2,1,0:T(8,128)(2,1)} %param.23) | copy-start | bytes 3145732
Sparse Core Ops, SparseCore 0:
  12.3 56.8 all-gather.3
  71.3 105.7 all-gather.5
  178.7 57.2 all-gather.7
  486.8 28.0 reduce-scatter.6
  593.7 31.4 reduce-scatter.4
  627.4 54.9 reduce-scatter.10
  684.9 102.3 reduce-scatter.8

commit v3 on v2

--- a/solution.py
+++ b/solution.py
@@ -354,6 +354,328 @@
     )(x)
 
 
+def ffn_kernel(
+    h_ref,
+    c_ref,
+    wg_ref,
+    wu_ref,
+    wd_ref,
+    h_all,
+    out_part,
+    gh_ref,
+    dg_ref,
+    du_ref,
+    dd_ref,
+    h_buf,
+    c_buf,
+    o_buf,
+    beside,
+    held,
+    got,
+    one,
+    two,
+    sum_g,
+    sum_u,
+    sum_d,
+    emit,
+    send,
+    recv,
+    load_sem,
+    out_sem,
+    emit_sem,
+):
+    me, sib, xn, yn = partners()
+    diag = xn + yn - me
+    flip = sib - me
+    rows = h_ref.shape[0]
+    half = rows // 2
+    upper, lower = pl.ds(0, half), pl.ds(half, half)
+    copy = functools.partial(remote, send, recv)
+
+    xa = copy(0, h_ref.at[upper], h_all.at[me, upper], xn)
+    yb = copy(1, h_ref.at[lower], h_all.at[me, lower], yn)
+    xb = copy(2, h_ref.at[lower], h_all.at[me, lower], xn)
+    ya = copy(3, h_ref.at[upper], h_all.at[me, upper], yn)
+    s0 = copy(4, h_ref, h_all.at[me], sib)
+
+    def pass_on(k, origin, part, to):
+        return copy(k, h_all.at[origin, part], h_all.at[origin, part], to)
+
+    fy = pass_on(5, xn, upper, yn)
+    fx = pass_on(6, yn, lower, xn)
+    s1 = pass_on(7, xn, upper, sib)
+    s2 = pass_on(8, yn, lower, sib)
+    s3 = pass_on(9, xn, lower, sib)
+    s4 = pass_on(10, yn, upper, sib)
+    s5 = pass_on(11, diag, upper, sib)
+    s6 = pass_on(12, diag, lower, sib)
+    b0 = copy(13, beside.at[0], got.at[0], sib)
+    b1 = copy(14, beside.at[1], got.at[1], sib)
+    b2 = copy(15, beside.at[0], got.at[2], sib)
+    b3 = copy(16, beside.at[1], got.at[3], sib)
+    x0 = copy(17, held.at[2, upper], one.at[0], xn)
+    y0 = copy(18, held.at[2, lower], one.at[1], yn)
+    x1 = copy(19, held.at[1, upper], one.at[2], xn)
+    y1 = copy(20, held.at[3, lower], one.at[3], yn)
+    y2 = copy(21, held.at[3, upper], two.at[0], yn)
+    x2 = copy(22, held.at[1, lower], two.at[1], xn)
+
+    def owner_of(step):
+        chip = jnp.where(step < 4, xn, jnp.where(step < 6, diag, yn))
+        later = chip + jnp.where(lax.rem(step, 2) == 0, flip, 0)
+        return jnp.where(step == 0, me, jnp.where(step == 1, sib, later))
+
+    def loads(step):
+        slot = lax.rem(step, 2)
+        owner = owner_of(step)
+        return (
+            pltpu.make_async_copy(h_all.at[owner], h_buf.at[slot], load_sem.at[0, slot]),
+            pltpu.make_async_copy(c_ref.at[owner], c_buf.at[slot], load_sem.at[1, slot]),
+        )
+
+    def out_copy(step):
+        slot = lax.rem(step, 2)
+        return pltpu.make_async_copy(o_buf.at[slot], out_part.at[owner_of(step)], out_sem.at[slot])
+
+    greet((sib, xn, yn))
+    for c in (xa, yb, xb, ya, s0):
+        c.start()
+    first = (
+        pltpu.make_async_copy(h_ref, h_buf.at[0], load_sem.at[0, 0]),
+        pltpu.make_async_copy(c_ref.at[me], c_buf.at[0], load_sem.at[1, 0]),
+    )
+    for c in first:
+        c.start()
+    for total in (sum_g, sum_u, sum_d):
+        total[...] = jnp.zeros_like(total)
+
+    def arrive(step):
+        @pl.when(step == 1)
+        def _():
+            s0.wait_recv()
+
+        @pl.when(step == 2)
+        def _():
+            xa.wait_recv()
+            yb.wait_recv()
+            for c in (fy, fx, s1, s2):
+                c.start()
+            xb.wait_recv()
+            ya.wait_recv()
+            s3.start()
+            s4.start()
+            s1.wait_recv()
+            s3.wait_recv()
+
+        @pl.when(step == 4)
+        def _():
+            fy.wait_recv()
+            fx.wait_recv()
+            s5.start()
+            s6.start()
+            s5.wait_recv()
+            s6.wait_recv()
+
+        @pl.when(step == 6)
+        def _():
+            s2.wait_recv()
+            s4.wait_recv()
+
+        @pl.when(step == 7)
+        def _():
+            y0.wait_recv()
+            held[1, half:] = held[1, half:] + one[1]
+            x2.start()
+
+    def body(step, carry):
+        slot = lax.rem(step, 2)
+        for c in loads(step):
+            c.wait()
+        h, c = h_buf[slot], c_buf[slot]
+        gate = dot(h, wg_ref[...])
+        up = dot(h, wu_ref[...])
+        g_act = contract(c, wd_ref[...], 1, 1)
+        sigmoid = jax.nn.sigmoid(gate)
+        silu = gate * sigmoid
+        act = (silu * up).astype(LOW)
+        g_gate = (g_act * up * sigmoid * (1.0 + gate * (1.0 - sigmoid))).astype(LOW)
+        g_up = (g_act * silu).astype(LOW)
+        part = (contract(g_gate, wg_ref[...], 1, 1) + contract(g_up, wu_ref[...], 1, 1)).astype(LOW)
+
+        for k, place, sent in ((1, 0, b0), (2, 1, b1), (4, 0, b2), (6, 1, b3)):
+
+            @pl.when(step == k)
+            def _(k=k, place=place, sent=sent):
+                if k == 4:
+                    b0.wait_send()
+                if k == 6:
+                    b1.wait_send()
+                beside[place] = part
+                sent.start()
+
+        for k, place, arrived in ((0, 0, None), (3, 1, b1), (5, 2, b2), (7, 3, b3)):
+
+            @pl.when(step == k)
+            def _(k=k, place=place, arrived=arrived):
+                if arrived is None:
+                    held[place] = part
+                else:
+                    arrived.wait_recv()
+                    held[place] = part + got[place]
+                if k == 3:
+                    x1.start()
+                if k == 5:
+                    x0.start()
+                    y0.start()
+                if k == 7:
+                    y1.start()
+                    x0.wait_recv()
+                    held[3, :half] = held[3, :half] + one[0]
+                    y2.start()
+
+        @pl.when(step >= 2)
+        def _():
+            out_copy(step - 2).wait()
+
+        o_buf[slot] = dot(act, wd_ref[...]).astype(LOW)
+        out_copy(step).start()
+        arrive(step + 1)
+
+        @pl.when(step < 7)
+        def _():
+            for c in loads(step + 1):
+                c.start()
+
+        sum_g[...] += contract(h, g_gate, 0, 0)
+        sum_u[...] += contract(h, g_up, 0, 0)
+        sum_d[...] += contract(act, c, 0, 0)
+        return carry
+
+    lax.fori_loop(0, 8, body, 0)
+    out_copy(6).wait()
+    out_copy(7).wait()
+
+    pending = [None, None]
+    count = 0
+    for total, target in ((sum_g, dg_ref), (sum_u, du_ref)):
+        block = emit.shape[1]
+        for start in range(0, total.shape[0], block):
+            slot = count % 2
+            if pending[slot] is not None:
+                pending[slot].wait()
+            emit[slot] = total[start : start + block].astype(LOW)
+            pending[slot] = pltpu.make_async_copy(
+                emit.at[slot], target.at[pl.ds(start, block)], emit_sem.at[slot]
+            )
+            pending[slot].start()
+            count += 1
+    hidden = sum_d.shape[0]
+    downs = []
+    for slot, start in enumerate(range(0, hidden, rows)):
+        size = min(rows, hidden - start)
+        if slot >= 2:
+            downs[slot - 2].wait()
+        o_buf[slot % 2, :size] = sum_d[start : start + size].astype(LOW)
+        downs.append(
+            pltpu.make_async_copy(
+                o_buf.at[slot % 2, pl.ds(0, size)],
+                dd_ref.at[pl.ds(start, size)],
+                out_sem.at[slot % 2],
+            )
+        )
+        downs[-1].start()
+
+    b0.wait_recv()
+    wide = jnp.float32
+    x1.wait_recv()
+    y1.wait_recv()
+    y2.wait_recv()
+    own = held[0, :half].astype(wide) + got[0, :half].astype(wide)
+    gh_ref[:half] = own + one[2].astype(wide) + two[0].astype(wide)
+    x2.wait_recv()
+    own = held[0, half:].astype(wide) + got[0, half:].astype(wide)
+    gh_ref[half:] = own + one[3].astype(wide) + two[1].astype(wide)
+    for c in downs[-2:]:
+        c.wait()
+    for c in pending:
+        c.wait()
+    for c in (xa, yb, xb, ya, s0, fy, fx, s1, s2, s3, s4, s5, s6, b2, b3, x0, y0, x1, y1, y2, x2):
+        c.wait_send()
+
+
+def ffn_plane(h_two, cot_all, gate_full, up_full, down_full):
+    rows, width = h_two.shape
+    hidden = gate_full.shape[1]
+    anywhere = pl.BlockSpec(memory_space=pl.ANY)
+    in_vmem = pl.BlockSpec(memory_space=pltpu.VMEM)
+    emit_rows = 256
+    shape = jax.ShapeDtypeStruct
+    unused, out_part, g_h_two, d_gate, d_up, d_down = pl.pallas_call(
+        ffn_kernel,
+        out_shape=[
+            shape((8, rows, width), LOW),
+            shape((8, rows, width), LOW),
+            shape((rows, width), jnp.float32),
+            shape((width, hidden), LOW),
+            shape((width, hidden), LOW),
+            shape((hidden, width), LOW),
+        ],
+        in_specs=[anywhere, anywhere, in_vmem, in_vmem, in_vmem],
+        out_specs=[anywhere, anywhere, in_vmem, anywhere, anywhere, anywhere],
+        scratch_shapes=[
+            pltpu.VMEM((2, rows, width), LOW),
+            pltpu.VMEM((2, rows, width), LOW),
+            pltpu.VMEM((2, rows, width), LOW),
+            pltpu.VMEM((2, rows, width), LOW),
+            pltpu.VMEM((4, rows, width), LOW),
+            pltpu.VMEM((4, rows, width), LOW),
+            pltpu.VMEM((4, rows // 2, width), LOW),
+            pltpu.VMEM((2, rows // 2, width), LOW),
+            pltpu.VMEM((width, hidden), jnp.float32),
+            pltpu.VMEM((width, hidden), jnp.float32),
+            pltpu.VMEM((hidden, width), jnp.float32),
+            pltpu.VMEM((2, emit_rows, hidden), LOW),
+            pltpu.SemaphoreType.DMA((23,)),
+            pltpu.SemaphoreType.DMA((23,)),
+            pltpu.SemaphoreType.DMA((2, 2)),
+            pltpu.SemaphoreType.DMA((2,)),
+            pltpu.SemaphoreType.DMA((2,)),
+        ],
+        compiler_params=pltpu.CompilerParams(
+            collective_id=20, has_side_effects=True, vmem_limit_bytes=63 * MIB
+        ),
+        cost_estimate=pl.CostEstimate(
+            flops=6 * 3 * 8 * rows * width * hidden,
+            bytes_accessed=64 * rows * width,
+            transcendentals=0,
+        ),
+        name="ffn",
+    )(h_two, cot_all, gate_full, up_full, down_full)
+    return out_part, g_h_two, d_gate, d_up, d_down
+
+
+def ffn_lax(h_two, cot_all, gate_full, up_full, down_full):
+    pieces, rows, width = cot_all.shape
+    h_two_all = gather_plane(h_two, 5).reshape(-1, width)
+    cot_all = cot_all.reshape(-1, width)
+    gate = dot(h_two_all, gate_full)
+    up = dot(h_two_all, up_full)
+    g_act = contract(cot_all, down_full, 1, 1)
+    sigmoid = jax.nn.sigmoid(gate)
+    silu = gate * sigmoid
+    act = (silu * up).astype(LOW)
+    g_gate = (g_act * up * sigmoid * (1.0 + gate * (1.0 - sigmoid))).astype(LOW)
+    g_up = (g_act * silu).astype(LOW)
+    part = (contract(g_gate, gate_full, 1, 1) + contract(g_up, up_full, 1, 1)).astype(LOW)
+    return (
+        dot(act, down_full).astype(LOW).reshape(pieces, rows, width),
+        scatter_plane(part.reshape(pieces, rows, width), 7),
+        contract(h_two_all, g_gate, 0, 0).astype(LOW),
+        contract(h_two_all, g_up, 0, 0).astype(LOW),
+        contract(act, cot_all, 0, 0).astype(LOW),
+    )
+
+
 def norm_scale(rows):
     return lax.rsqrt(jnp.mean(rows * rows, axis=-1, keepdims=True) + epsilon)
 
@@ -464,32 +786,18 @@
     plain_two = mid * inverse_two
     h_two = (plain_two * gain_two).astype(LOW)
 
-    h_two_all = gather_plane(h_two, 5).reshape(-1, D)
-    cot_all = gather_plane(cot, 6).reshape(-1, D)
-    gate = dot(h_two_all, gate_full)
-    up = dot(h_two_all, up_full)
-    g_act = contract(cot_all, down_full, 1, 1)
-    sigmoid = jax.nn.sigmoid(gate)
-    silu = gate * sigmoid
-    act = (silu * up).astype(LOW)
-    g_gate = (g_act * up * sigmoid * (1.0 + gate * (1.0 - sigmoid))).astype(LOW)
-    g_up = (g_act * silu).astype(LOW)
-    g_h_two_part = (contract(g_gate, gate_full, 1, 1) + contract(g_up, up_full, 1, 1)).astype(LOW)
-    g_h_two = scatter_plane(g_h_two_part.reshape(pieces, mine, D), 7)
-    grad_down = lax.psum_scatter(
-        contract(act, cot_all, 0, 0).astype(LOW), "dp", scatter_dimension=0, tiled=True
-    ).astype(jnp.float32)
-    grad_ffn = lax.psum_scatter(
-        jnp.concatenate(
-            [contract(h_two_all, g_gate, 0, 0).astype(LOW), contract(h_two_all, g_up, 0, 0).astype(LOW)],
-            axis=1,
-        ),
-        "dp",
-        scatter_dimension=0,
-        tiled=True,
-    )
-    out_part = dot(act, down_full).astype(LOW)
-    output = (mid + scatter_plane(out_part.reshape(pieces, mine, D), 8)).astype(LOW)
+    cot_all = gather_plane(cot, 6)
+    feed_forward = ffn_plane if pieces == 8 else ffn_lax
+    out_part, g_h_two, d_gate, d_up, d_down = feed_forward(
+        h_two, cot_all, gate_full, up_full, down_full
+    )
+
+    def scatter_dp(part):
+        return lax.psum_scatter(part, "dp", scatter_dimension=0, tiled=True)
+
+    grad_ffn = scatter_dp(jnp.concatenate([d_gate, d_up], axis=1))
+    grad_down = scatter_dp(d_down).astype(jnp.float32)
+    output = (mid + scatter_plane(out_part, 8)).astype(LOW)
 
     g_mid = cot.astype(jnp.float32) + norm_backward(g_h_two, plain_two, inverse_two, gain_two)
     g_mid_low = g_mid.astype(LOW)
@@ -522,7 +830,7 @@
     grad_out = contract(attended, g_mid_low, 0, 0).astype(LOW)
     grad_out = grad_out.reshape(groups, pieces, own, D).transpose(1, 0, 2, 3)
     grad_out = scatter_plane(grad_out.reshape(pieces, groups * own, D), 10).astype(LOW)
-    grad_out = lax.psum_scatter(grad_out, "dp", scatter_dimension=0, tiled=True)
+    grad_out = scatter_dp(grad_out)
     grad_attn = jnp.concatenate(
         [
             contract(h_flat, g_value, 0, 0).astype(LOW),
@@ -533,7 +841,7 @@
         ],
         axis=1,
     )
-    grad_attn = lax.psum_scatter(grad_attn, "dp", scatter_dimension=0, tiled=True)
+    grad_attn = scatter_dp(grad_attn)
     ffn_got = exchange_plane(grad_ffn.reshape(pieces, own, 2 * hidden), 11).astype(jnp.float32)
     attn_got = exchange_plane(grad_attn.reshape(pieces, own, -1), 12).astype(jnp.float32)
     grad_gains = jnp.sum(attn_got[:, :, wide + 2 * qk :], axis=0)

time: 845 us -> 828 us (0.980)
  matrix products: 175 us -> 76.1 us
  Pallas kernels: 413 us -> 449 us
  waiting for transfers between devices: 90.6 us -> 122 us
  other arithmetic: 41.5 us -> 52.3 us
    pallas_call x0 -> x1, Pallas kernels: none -> 115 us  [ffn_plane(): pl.pallas_call(ffn_kernel, out_shape=[shape((8, rows, width), LOW), shape...]
    dot_general x13 -> x7, matrix products: 120 us -> 48.9 us  [contract(): lax.dot_general(left, right, (((left_dim,), (right_dim,)), ((), ())), pre...]
    pallas_call x4 -> x3, Pallas kernels: 161 us -> 121 us  [gather_plane(): pl.pallas_call(gather_kernel, out_shape=jax.ShapeDtypeStruct((8,) + x.sha...]
    pallas_call x4 -> x3, Pallas kernels: 159 us -> 119 us  [scatter_plane(): pl.pallas_call(scatter_kernel, out_shape=jax.ShapeDtypeStruct((rows, colu...]
    reduce_scatter x4, waiting for transfers between devices: 90.5 us -> 121 us  [scatter_dp(): return lax.psum_scatter(part, 'dp', scatter_dimension=0, tiled=True)]
    dot_general x6 -> x3, matrix products: 46.4 us -> 18.7 us  [dot(): return jnp.dot(left, right, preferred_element_type=jnp.float32)]
  transfers between devices with their start and end apart: 7 -> 7, of which waited for: 1 -> 2; matrix products, arithmetic and copies ran while one was open for 26% -> 21% of each run, Pallas kernels for 33% -> 29%
where the time goes in v3:
time: 828 us; the launch traced here: 821 us
  Pallas kernels  449 us (54%)
  waiting for transfers between devices  122 us (15%)
  local copies, waits for them, and re-layouts  106 us (13%)
  matrix products  76.1 us (9%)
  other arithmetic  52.3 us (6%)
  between operations  15 us (2%)
    pallas_call x3, Pallas kernels, gather_plane(): pl.pallas_call(gather_kernel, out_shape=jax.ShapeDtypeStruct((8,) + x.sha...  121 us
    reduce_scatter x4, waiting for transfers between devices, scatter_dp(): return lax.psum_scatter(part, 'dp', scatter_dimension=0, tiled=True)  121 us
    pallas_call x3, Pallas kernels, scatter_plane(): pl.pallas_call(scatter_kernel, out_shape=jax.ShapeDtypeStruct((rows, colu...  119 us
    pallas_call x1, Pallas kernels, ffn_plane(): pl.pallas_call(ffn_kernel, out_shape=[shape((8, rows, width), LOW), shape...  115 us
    pallas_call x4, Pallas kernels, exchange_plane(): pl.pallas_call(exchange_kernel, out_shape=jax.ShapeDtypeStruct(x.shape, x...  58 us
    dot_general x7, matrix products, contract(): lax.dot_general(left, right, (((left_dim,), (right_dim,)), ((), ())), pre...  48.9 us
    pallas_call x1, Pallas kernels, attend_back(): pl.pallas_call(functools.partial(attend_back_kernel, heads), grid=(stream...  24.6 us
    dot_general x3, matrix products, dot(): return jnp.dot(left, right, preferred_element_type=jnp.float32)  18.7 us
  transfers between devices with their start and end apart: 7, of which 2 were waited for; matrix products, arithmetic and copies ran while one was open for 21% of the time, Pallas kernels for 29%

profile of v3, /device:TPU:1, one launch (start us, length us, event | category | flops | bytes accessed | tf_op | source)
XLA Modules:
  0.0 820.9 jit_solution(2524150932868004812)
XLA Ops:
  8.9 1.1 constant_dynamic-slice_fusion.9
  12.2 2.9 constant_dynamic-slice_fusion.1
  15.1 2.4 concatenate.13
  17.6 2.2 constant_dynamic-slice_fusion
  21.4 41.6 %gather.3 = bf16[8,256,2048]{2,1,0:T(8,128)(2,1)} custom-call(bf16[256,2048]{1,0:T(8,128)(2,1)} %bitcast.128), custom_call_target="tpu_custom_call" | custom-call | bytes 83886080 | tf_op jit(solution)/shard_map/gather/pallas_call | solution.py:229
  63.0 39.9 %gather.5.c_ref = bf16[8,256,2048]{2,1,0:T(8,128)(2,1)} custom-call(bf16[256,2048]{1,0:T(8,128)(2,1)} %bitcast.130), custom_call_target="tpu_custom_call" | custom-call | bytes 83886080 | tf_op jit(solution)/shard_map/gather/pallas_call | solution.py:229
  102.9 11.3 %bitcast_convert_fusion = f32[8,2,128,2048]{3,2,1,0:T(8,128)} fusion(bf16[8,256,2048]{2,1,0:T(8,128)(2,1)} %gather.3), kind=kLoop, calls=%fused_computation.74 | loop fusion | flops 4194304 | bytes 25165824 | tf_op jit(solution)/shard_map/convert_element_type | solution.py:763
  114.2 7.0 fusion
  121.3 1.2 slice_convert_fusion
  123.5 8.1 fusion.2
  131.6 2.3 slice.73.x_ref
  133.9 39.9 %gather.4 = bf16[8,2048,256]{2,1,0:T(8,128)(2,1)} custom-call(bf16[2048,256]{1,0:T(8,128)(2,1)} %slice.73.x_ref), custom_call_target="tpu_custom_call" | custom-call | bytes 83886080 | tf_op jit(solution)/shard_map/gather/pallas_call | solution.py:229
  173.8 11.5 %copy.109 = bf16[8,256,2048]{2,1,0:T(8,128)(2,1)} copy(bf16[8,256,2048]{1,2,0:T(8,128)(2,1)} %bitcast.124) | data formatting | bytes 16777216 | tf_op jit(solution)/shard_map/tk,skn->tsn/dot_general | solution.py:782
  185.3 6.2 convolution_convert_fusion.6
  191.8 6.3 convolution_convert_fusion.5
  198.4 6.2 convolution_convert_fusion.2
  204.7 11.0 %attend.1.att_ref = bf16[2,1024,256]{2,1,0:T(8,128)(2,1)S(1)} custom-call(bf16[2,1024,32]{2,1,0:T(8,128)(2,1)S(1)} %bitcast.109, bf16[2,1024,32]{2,1,0:T(8,128)(2,1)S(1)} %bitcast.111, bf16[2,1024,256]{2,1,0:T(8,128)(2,1)S(1)} %bitcast.113, s32[2,1024,1]{2,1,0:T(8,128)S(1)} %copy.106.first_ref), custom_call_target="tpu_custom_call" | custom-call | tf_op jit(solution)/shard_map/attend/pallas_call | solution.py:61
  217.7 15.0 %exchange.4 = bf16[8,2,128,256]{3,2,1,0:T(8,128)(2,1)} custom-call(bf16[8,2,128,256]{3,2,1,0:T(8,128)(2,1)} %bitcast.143), custom_call_target="tpu_custom_call" | custom-call | bytes 20971520 | tf_op jit(solution)/shard_map/exchange/pallas_call | solution.py:341
  232.7 1.9 copy.108
  234.9 6.3 multiply_reduce_fusion.3
  241.2 1.3 copy-done.8
  242.5 1.2 multiply_convert_fusion.h_ref
  243.8 7.2 fusion.23
  251.0 114.6 %ffn.1 = (bf16[8,256,2048]{2,1,0:T(8,128)(2,1)}, bf16[8,256,2048]{2,1,0:T(8,128)(2,1)}, f32[256,2048]{1,0:T(8,128)}, bf16[2048,704]{1,0:T(8,128)(2,1)}, bf16[204...) custom-call(bf16[256,2048]{1,0:T(8,128)(2,1)} %multiply_convert_fusion.h_ref, bf16[8,256,2048]{2,1,0:T(8,128)(2,1)} %gather.5.c_ref, ...), custom_call_target="tpu_custom_call" | custom-call | flops 53150220288 | bytes 33554432 | tf_op jit(solution)/shard_map/ffn/pallas_call | solution.py:613
  365.7 2.9 multiply_reduce_fusion
  369.1 2.1 fusion.22
  371.2 5.6 convolution_convert_fusion
  376.9 2.4 fusion.6
  379.6 1.2 copy.136
  380.8 15.3 %exchange.5 = bf16[8,2,128,256]{3,2,1,0:T(8,128)(2,1)} custom-call(bf16[8,2,128,256]{3,2,1,0:T(8,128)(2,1)} %bitcast.141), custom_call_target="tpu_custom_call" | custom-call | bytes 20971520 | tf_op jit(solution)/shard_map/exchange/pallas_call | solution.py:341
  396.1 2.3 copy.112
  398.4 24.6 %attend_back.1 = (bf16[2,1024,32]{2,1,0:T(8,128)(2,1)}, bf16[2,1024,32]{2,1,0:T(8,128)(2,1)}, bf16[2,1024,256]{2,1,0:T(8,128)(2,1)}) custom-call(bf16[2,1024,32]{2,1,0:T(8,128)(2,1)} %bitcast.110, bf16[2,1024,32]{2,1,0:T(8,128)(2,1)} %bitcast.112, bf16[2,1024,256]{2,1,0:T(8,128)(2,1)} %bitcast.114, s32[2,1024,1]{2,1,0:T(8,128)} %copy-done.2, ...), custom_call_target="tpu_custom_call" | custom-call | tf_op jit(solution)/shard_map/attend_back/pallas_call | solution.py:122
  423.0 8.3 %copy.119 = bf16[4,8,64,2048]{3,2,0,1:T(8,128)(2,1)} copy(bf16[4,8,64,2048]{3,2,1,0:T(8,128)(2,1)} %bitcast.123) | data formatting | bytes 16777216 | tf_op jit(solution)/shard_map/reshape | solution.py:831
  431.3 3.4 copy-done
  434.7 38.1 %scatter.5 = f32[256,2048]{1,0:T(8,128)S(1)} custom-call(bf16[8,256,2048]{2,1,0:T(8,128)(2,1)S(1)} %bitcast.106), custom_call_target="tpu_custom_call" | custom-call | bytes 83886080 | tf_op jit(solution)/shard_map/scatter/pallas_call | solution.py:299
  472.8 1.1 convert_element_type.126
  474.9 9.4 %fusion.14 = f32[2048,2048]{1,0:T(8,128)} fusion(bf16[2048,256]{1,0:T(8,128)(2,1)} %bitcast.152, bf16[2048,578]{1,0:T(8,128)(2,1)S(1)} %copy-done.17), kind=kOutput, calls=%fused_computation.39 | convolution fusion | flops 2147483648 | bytes 18874368 | tf_op jit(solution)/shard_map/dot_general | solution.py:25
  484.3 8.1 fusion.19
  492.4 15.6 %add_convert_fusion = bf16[2048,2048]{1,0:T(8,128)(2,1)} fusion(f32[2048,2048]{1,0:T(8,128)} %fusion.14, f32[2048,2048]{1,0:T(8,128)} %fusion.19, bf16[2048,32]{1,0:T(8,128)(2,1)S(1)} %bitcast.146, bf16[2048,578]{1,0:T(8,128)(2,1)S(1)} %copy-done.17), kind=kOutput, calls=%fused_computation.5 | convolution fusion | flops 281018368 | bytes 42991616 | tf_op jit(solution)/shard_map/dot_general | solution.py:25
  507.9 8.3 %copy.114 = bf16[2,8,128,2048]{3,2,0,1:T(8,128)(2,1)} copy(bf16[2,8,128,2048]{3,2,1,0:T(8,128)(2,1)} %bitcast.127) | data formatting | bytes 16777216 | tf_op jit(solution)/shard_map/reshape | solution.py:820
  516.2 3.4 copy-done.1
  519.6 41.2 %scatter.4 = f32[256,2048]{1,0:T(8,128)S(1)} custom-call(bf16[8,256,2048]{2,1,0:T(8,128)(2,1)S(1)} %bitcast.107), custom_call_target="tpu_custom_call" | custom-call | bytes 83886080 | tf_op jit(solution)/shard_map/scatter/pallas_call | solution.py:299
  561.6 5.3 convolution_convert_fusion.4
  566.9 1.5 convolution_convert_fusion.3
  568.4 3.3 convolution_convert_fusion.1
  571.8 7.1 concatenate.14
  579.6 7.1 pad_maximum_fusion
  586.7 3.4 copy-done.4
  590.1 40.1 %scatter.3 = f32[256,2048]{1,0:T(8,128)S(1)} custom-call(bf16[8,256,2048]{2,1,0:T(8,128)(2,1)S(1)} %copy-done.4), custom_call_target="tpu_custom_call" | custom-call | bytes 83886080 | tf_op jit(solution)/shard_map/scatter/pallas_call | solution.py:299
  630.2 2.9 fusion.10
  633.2 1.8 convert_element_type.127
  634.9 1.9 copy.115
  636.8 7.8 exchange.6
  649.2 18.9 %reduce-scatter.11.cloned.1.call-done = bf16[176,2048]{1,0:T(8,128)(2,1)} async-done(((bf16[704,2048]{1,0:T(8,128)(2,1)}), bf16[176,2048]{1,0:T(8,128)(2,1)}) %reduce-scatter.11.cloned.1.call-update) | async-done | bytes 720912 | tf_op jit(solution)/shard_map/reduce_scatter | solution.py:796
  668.1 2.4 convert_element_type.129
  670.5 102.4 %reduce-scatter.9.cloned.1.call-done = bf16[512,1408]{1,0:T(8,128)(2,1)} async-done(((bf16[2048,1408]{1,0:T(8,128)(2,1)}), bf16[512,1408]{1,0:T(8,128)(2,1)}) %reduce-scatter.9.cloned.1.call-update) | async-done | bytes 1441808 | tf_op jit(solution)/shard_map/reduce_scatter | solution.py:796
  772.9 19.8 %exchange.7 = bf16[8,64,1408]{2,1,0:T(8,128)(2,1)} custom-call(bf16[8,64,1408]{2,1,0:T(8,128)(2,1)} %bitcast.150), custom_call_target="tpu_custom_call" | custom-call | bytes 28835840 | tf_op jit(solution)/shard_map/exchange/pallas_call | solution.py:341
  792.7 3.5 fusion.24
  796.2 3.0 reshape.208
  799.2 2.5 copy.121
  801.8 3.3 reshape.209
  805.0 3.0 reshape.206
  808.1 2.5 copy.120
  810.6 3.3 reshape.207
  (112 shorter events, 17.2 us)
Async XLA Ops:
  7.2 114.1 %all-gather.4.cloned.1.call-start = ((), (), s32[]{:S(2)}) async-start(), calls=%async_computation.4 | async-start | bytes 3276800 | tf_op jit(solution)/shard_map/all_gather | solution.py:739
  12.2 231.6 %all-gather.6.cloned.1.call-start = ((), (), s32[]{:S(2)}) async-start(), calls=%async_computation.5 | async-start | bytes 7208960 | tf_op jit(solution)/shard_map/all_gather | solution.py:739
  17.5 2.3 copy-start.26
  17.5 2.5 copy-start.13
  17.5 233.5 %all-gather.8.cloned.1.call-start = ((), (), s32[]{:S(2)}) async-start(), calls=%async_computation.6 | async-start | bytes 3604480 | tf_op jit(solution)/shard_map/all_gather | solution.py:739
  19.8 613.4 %reduce-scatter.7.cloned.1.call-start = ((), (), s32[]{:S(2)}) async-start(), calls=%async_computation.8 | async-start | bytes 1310720 | tf_op jit(solution)/shard_map/reduce_scatter | solution.py:796
  21.4 183.3 %copy-start.2 = (s32[2,1024,1]{2,1,0:T(8,128)}, s32[2,1024,1]{2,1,0:T(8,128)S(1)}, u32[]{:S(2)}) copy-start(s32[2,1024,1]{2,1,0:T(8,128)S(1)} %copy.106.first_ref) | copy-start | bytes 24580
  191.8 12.8 %copy-start.5 = (bf16[2048,32]{1,0:T(8,128)(2,1)}, bf16[2048,32]{1,0:T(8,128)(2,1)S(1)}, u32[]{:S(2)}) copy-start(bf16[2048,32]{1,0:T(8,128)(2,1)S(1)} %copy.104) | copy-start | bytes 393220
  198.4 6.2 copy-start.6
  204.6 13.0 %copy-start.7 = (bf16[2048,256]{1,0:T(8,128)(2,1)}, bf16[2048,256]{1,0:T(8,128)(2,1)S(1)}, u32[]{:S(2)}) copy-start(bf16[2048,256]{1,0:T(8,128)(2,1)S(1)} %convolution_convert_fusion.2) | copy-start | bytes 3145732
  215.6 1.0 copy-start.3
  232.7 2.2 copy-start.14
  234.9 6.3 copy-start.18
  241.2 1.3 copy-start.8
  365.7 3.0 copy-start.9
  365.7 3.5 copy-start.11
  369.1 2.1 copy-start.19
  369.1 7.7 slice-start.2
  371.2 5.7 slice-start.3
  431.3 3.4 copy-start
  472.8 2.1 copy-start.17
  473.9 161.0 %reduce-scatter.5.cloned.1.call-start = ((), (), s32[]{:S(2)}) async-start(), calls=%async_computation.7 | async-start | bytes 1679360 | tf_op jit(solution)/shard_map/reduce_scatter | solution.py:796
  474.9 9.4 %copy-start.20 = (bf16[2,1024,32]{2,1,0:T(8,128)(2,1)S(1)}, bf16[2,1024,32]{2,1,0:T(8,128)(2,1)}, u32[]{:S(2)}) copy-start(bf16[2,1024,32]{2,1,0:T(8,128)(2,1)} %get-tuple-element.22) | copy-start | bytes 393220
  484.3 8.1 copy-start.22
  516.2 3.4 copy-start.1
  519.6 41.2 %copy-start.15 = (bf16[1,2,128,2048]{3,2,1,0:T(8,128)(2,1)S(1)}, bf16[1,2,128,2048]{3,2,1,0:T(8,128)(2,1)}, u32[]{:S(2)}) copy-start(bf16[1,2,128,2048]{3,2,1,0:T(8,128)(2,1)} %param.12) | copy-start | bytes 3145732
  519.6 41.2 %copy-start.25 = (f32[256]{0:T(256)S(1)}, f32[256]{0:T(256)}, u32[]{:S(2)}) copy-start(f32[256]{0:T(256)} %rsqrt_bitcast_fusion) | copy-start | bytes 3076
  519.6 41.9 %copy-start.21 = (bf16[2,1024,32]{2,1,0:T(8,128)(2,1)S(1)}, bf16[2,1024,32]{2,1,0:T(8,128)(2,1)}, u32[]{:S(2)}) copy-start(bf16[2,1024,32]{2,1,0:T(8,128)(2,1)} %get-tuple-element.22) | copy-start | bytes 393220
  519.6 47.2 %slice-start = ((s8[8388608]{0:T(1024)(128)(4,1)}), s8[4194304]{0:T(1024)(128)(4,1)S(1)}, s32[]{:S(2)}) async-start(s8[8388608]{0:T(1024)(128)(4,1)} %bitcast.119), calls=%async_computation.11 | async-start | bytes 8388608
  560.9 6.0 slice-start.1
  561.6 5.3 copy-start.23
  566.9 1.6 copy-start.24
  579.0 89.2 %reduce-scatter.11.cloned.1.call-start = ((), (), s32[]{:S(2)}) async-start(), calls=%async_computation.10 | async-start | bytes 3604480 | tf_op jit(solution)/shard_map/reduce_scatter | solution.py:796
  579.5 193.3 %reduce-scatter.9.cloned.1.call-start = ((), (), s32[]{:S(2)}) async-start(), calls=%async_computation.9 | async-start | bytes 7208960 | tf_op jit(solution)/shard_map/reduce_scatter | solution.py:796
  586.7 3.4 copy-start.4
  590.1 40.1 %copy-start.10 = (f32[256,2048]{1,0:T(8,128)S(1)}, f32[256,2048]{1,0:T(8,128)}, u32[]{:S(2)}) copy-start(f32[256,2048]{1,0:T(8,128)} %copy-done.8) | copy-start | bytes 6291460
  590.1 40.1 %copy-start.12 = (f32[256,2048]{1,0:T(8,128)S(1)}, f32[256,2048]{1,0:T(8,128)}, u32[]{:S(2)}) copy-start(f32[256,2048]{1,0:T(8,128)} %get-tuple-element.20) | copy-start | bytes 6291460
  590.1 40.1 %copy-start.16 = (bf16[1,2,128,2048]{3,2,1,0:T(8,128)(2,1)S(1)}, bf16[1,2,128,2048]{3,2,1,0:T(8,128)(2,1)}, u32[]{:S(2)}) copy-start(bf16[1,2,128,2048]{3,2,1,0:T(8,128)(2,1)} %param.23) | copy-start | bytes 3145732
Sparse Core Ops, SparseCore 0:
  12.3 56.8 all-gather.3
  71.3 105.7 all-gather.5
  178.7 57.2 all-gather.7
  474.0 28.3 reduce-scatter.6
  579.1 31.6 reduce-scatter.4
  613.0 55.0 reduce-scatter.10
  670.5 102.3 reduce-scatter.8

commit v4 on v3

--- a/solution.py
+++ b/solution.py
@@ -795,8 +795,7 @@
     def scatter_dp(part):
         return lax.psum_scatter(part, "dp", scatter_dimension=0, tiled=True)
 
-    grad_ffn = scatter_dp(jnp.concatenate([d_gate, d_up], axis=1))
-    grad_down = scatter_dp(d_down).astype(jnp.float32)
+    sum_gate, sum_up, sum_down = scatter_dp(d_gate), scatter_dp(d_up), scatter_dp(d_down)
     output = (mid + scatter_plane(out_part, 8)).astype(LOW)
 
     g_mid = cot.astype(jnp.float32) + norm_backward(g_h_two, plain_two, inverse_two, gain_two)
@@ -830,6 +829,9 @@
     grad_out = contract(attended, g_mid_low, 0, 0).astype(LOW)
     grad_out = grad_out.reshape(groups, pieces, own, D).transpose(1, 0, 2, 3)
     grad_out = scatter_plane(grad_out.reshape(pieces, groups * own, D), 10).astype(LOW)
+    grad_out, sum_gate, sum_up, sum_down = lax.optimization_barrier(
+        (grad_out, sum_gate, sum_up, sum_down)
+    )
     grad_out = scatter_dp(grad_out)
     grad_attn = jnp.concatenate(
         [
@@ -841,8 +843,10 @@
         ],
         axis=1,
     )
+    grad_attn, grad_out = lax.optimization_barrier((grad_attn, grad_out))
     grad_attn = scatter_dp(grad_attn)
-    ffn_got = exchange_plane(grad_ffn.reshape(pieces, own, 2 * hidden), 11).astype(jnp.float32)
+    gate_got = exchange_plane(sum_gate.reshape(pieces, own, hidden), 11)
+    up_got = exchange_plane(sum_up.reshape(pieces, own, hidden), 13)
     attn_got = exchange_plane(grad_attn.reshape(pieces, own, -1), 12).astype(jnp.float32)
     grad_gains = jnp.sum(attn_got[:, :, wide + 2 * qk :], axis=0)
     attn_got = jnp.sum(attn_got.reshape(pieces // sharers, sharers, own, -1), axis=1)
@@ -851,7 +855,8 @@
         return block.transpose(1, 0, 2).reshape(own, -1)
 
     def by_hidden(block):
-        return block.reshape(pieces, own, groups, share).transpose(1, 2, 0, 3).reshape(own, FF)
+        block = block.astype(jnp.float32).reshape(pieces, own, groups, share)
+        return block.transpose(1, 2, 0, 3).reshape(own, FF)
 
     return (
         output.reshape(tokens.shape),
@@ -860,9 +865,9 @@
         by_rows(attn_got[:, :, wide + qk : wide + 2 * qk]),
         by_rows(attn_got[:, :, :wide]),
         grad_out.astype(jnp.float32),
-        by_hidden(ffn_got[:, :, :hidden]),
-        by_hidden(ffn_got[:, :, hidden:]),
-        grad_down,
+        by_hidden(gate_got),
+        by_hidden(up_got),
+        sum_down.astype(jnp.float32),
         grad_gains[:, 0],
         grad_gains[:, 1],
     )

time: 828 us -> 708 us (0.86)
  waiting for transfers between devices: 122 us -> 7.69 us
  other arithmetic: 52.3 us -> 38.3 us
    reduce_scatter x4 -> x5, waiting for transfers between devices: 121 us -> 6.53 us  [scatter_dp(): return lax.psum_scatter(part, 'dp', scatter_dimension=0, tiled=True)]
    reshape x4 -> x6, local copies, waits for them, and re-layouts: 12.6 us -> 18.9 us  [by_hidden(): return block.transpose(1, 2, 0, 3).reshape(own, FF)]
    pallas_call x4 -> x5, Pallas kernels: 58 us -> 62.7 us  [exchange_plane(): pl.pallas_call(exchange_kernel, out_shape=jax.ShapeDtypeStruct(x.shape, x...]
    unnamed x67 -> x71, local copies, waits for them, and re-layouts: 16 us -> 19.7 us
  transfers between devices with their start and end apart: 7 -> 8, of which waited for: 2 -> 1; matrix products, arithmetic and copies ran while one was open for 21% -> 28% of each run, Pallas kernels for 29% -> 47%
where the time goes in v4:
time: 708 us; the launch traced here: 701 us
  Pallas kernels  450 us (64%)
  local copies, waits for them, and re-layouts  109 us (15%)
  matrix products  81.5 us (12%)
  other arithmetic  38.3 us (5%)
  between operations  15.1 us (2%)
  waiting for transfers between devices  7.69 us (1%)
    pallas_call x3, Pallas kernels, gather_plane(): pl.pallas_call(gather_kernel, out_shape=jax.ShapeDtypeStruct((8,) + x.sha...  121 us
    pallas_call x3, Pallas kernels, scatter_plane(): pl.pallas_call(scatter_kernel, out_shape=jax.ShapeDtypeStruct((rows, colu...  121 us
    pallas_call x1, Pallas kernels, ffn_plane(): pl.pallas_call(ffn_kernel, out_shape=[shape((8, rows, width), LOW), shape...  109 us
    pallas_call x5, Pallas kernels, exchange_plane(): pl.pallas_call(exchange_kernel, out_shape=jax.ShapeDtypeStruct(x.shape, x...  62.7 us
    dot_general x7, matrix products, contract(): lax.dot_general(left, right, (((left_dim,), (right_dim,)), ((), ())), pre...  53.3 us
    pallas_call x1, Pallas kernels, attend_back(): pl.pallas_call(functools.partial(attend_back_kernel, heads), grid=(stream...  24.8 us
    unnamed x71, local copies, waits for them, and re-layouts  19.7 us
    reshape x6, local copies, waits for them, and re-layouts, by_hidden(): return block.transpose(1, 2, 0, 3).reshape(own, FF)  18.9 us
  transfers between devices with their start and end apart: 8, of which 1 were waited for; matrix products, arithmetic and copies ran while one was open for 28% of the time, Pallas kernels for 47%

profile of v4, /device:TPU:1, one launch (start us, length us, event | category | flops | bytes accessed | tf_op | source)
XLA Modules:
  0.0 701.3 jit_solution(18396321576002258104)
XLA Ops:
  8.9 1.1 constant_dynamic-slice_fusion.11
  9.9 1.1 constant_dynamic-slice_fusion.9
  11.1 1.1 concatenate.9
  12.2 2.9 constant_dynamic-slice_fusion.1
  15.1 2.4 concatenate.10
  17.6 2.1 constant_dynamic-slice_fusion
  19.7 41.6 %gather.3 = bf16[8,256,2048]{2,1,0:T(8,128)(2,1)} custom-call(bf16[256,2048]{1,0:T(8,128)(2,1)} %bitcast.127), custom_call_target="tpu_custom_call" | custom-call | bytes 83886080 | tf_op jit(solution)/shard_map/gather/pallas_call | solution.py:229
  61.4 11.2 %bitcast_convert_fusion = f32[8,2,128,2048]{3,2,1,0:T(8,128)} fusion(bf16[8,256,2048]{2,1,0:T(8,128)(2,1)} %gather.3), kind=kLoop, calls=%fused_computation.73 | loop fusion | flops 4194304 | bytes 25165824 | tf_op jit(solution)/shard_map/convert_element_type | solution.py:763
  72.6 7.4 %fusion = f32[2,8,128]{2,1,0:T(8,128)S(1)} fusion(f32[8,2,128,2048]{3,2,1,0:T(8,128)} %bitcast_convert_fusion), kind=kLoop, calls=%fused_computation.2 | loop fusion | flops 8386560 | bytes 16785408 | tf_op jit(solution)/shard_map/reduce_sum | solution.py:680
  80.8 39.9 %gather.5.c_ref = bf16[8,256,2048]{2,1,0:T(8,128)(2,1)} custom-call(bf16[256,2048]{1,0:T(8,128)(2,1)} %bitcast.129), custom_call_target="tpu_custom_call" | custom-call | bytes 83886080 | tf_op jit(solution)/shard_map/gather/pallas_call | solution.py:229
  120.7 1.2 slice_convert_fusion
  122.9 5.5 fusion.2
  128.4 3.2 copy-done.8
  131.6 3.7 convolution_convert_fusion.5
  135.6 6.2 convolution_convert_fusion.6
  142.1 6.1 convolution_convert_fusion.2
  148.3 10.4 %attend.1.att_ref = bf16[2,1024,256]{2,1,0:T(8,128)(2,1)S(1)} custom-call(bf16[2,1024,32]{2,1,0:T(8,128)(2,1)S(1)} %bitcast.112, bf16[2,1024,32]{2,1,0:T(8,128)(2,1)S(1)} %bitcast.110, bf16[2,1024,256]{2,1,0:T(8,128)(2,1)S(1)} %bitcast.114, s32[2,1024,1]{2,1,0:T(8,128)S(1)} %copy.106.first_ref), custom_call_target="tpu_custom_call" | custom-call | tf_op jit(solution)/shard_map/attend/pallas_call | solution.py:61
  159.7 1.1 copy.137
  160.8 14.7 %exchange.5 = bf16[8,2,128,256]{3,2,1,0:T(8,128)(2,1)} custom-call(bf16[8,2,128,256]{3,2,1,0:T(8,128)(2,1)} %bitcast.142), custom_call_target="tpu_custom_call" | custom-call | bytes 20971520 | tf_op jit(solution)/shard_map/exchange/pallas_call | solution.py:341
  175.5 1.8 copy.108
  177.6 2.6 slice.65.x_ref
  180.3 39.8 %gather.4 = bf16[8,2048,256]{2,1,0:T(8,128)(2,1)} custom-call(bf16[2048,256]{1,0:T(8,128)(2,1)} %slice.65.x_ref), custom_call_target="tpu_custom_call" | custom-call | bytes 83886080 | tf_op jit(solution)/shard_map/gather/pallas_call | solution.py:229
  220.1 12.1 %copy.109 = bf16[8,256,2048]{2,1,0:T(8,128)(2,1)} copy(bf16[8,256,2048]{1,2,0:T(8,128)(2,1)} %bitcast.125) | data formatting | bytes 16777216 | tf_op jit(solution)/shard_map/tk,skn->tsn/dot_general | solution.py:782
  232.3 5.9 multiply_reduce_fusion.3
  238.2 1.3 copy-done.9
  239.5 1.3 multiply_convert_fusion.h_ref
  240.7 7.1 %fusion.23 = (bf16[2048,704]{1,0:T(8,128)(2,1)}, bf16[2048,704]{1,0:T(8,128)(2,1)}) fusion(bf16[2048,1408]{1,0:T(8,128)(2,1)} %all-gather.6.cloned.1.call-done), kind=kLoop, calls=%fused_computation.76 | loop fusion | bytes 11534336 | tf_op jit(solution)/shard_map/slice | solution.py:749
  247.9 109.3 %ffn.1 = (bf16[8,256,2048]{2,1,0:T(8,128)(2,1)}, bf16[8,256,2048]{2,1,0:T(8,128)(2,1)}, f32[256,2048]{1,0:T(8,128)}, bf16[2048,704]{1,0:T(8,128)(2,1)}, bf16[204...) custom-call(bf16[256,2048]{1,0:T(8,128)(2,1)} %multiply_convert_fusion.h_ref, bf16[8,256,2048]{2,1,0:T(8,128)(2,1)} %gather.5.c_ref, ...), custom_call_target="tpu_custom_call" | custom-call | flops 53150220288 | bytes 33554432 | tf_op jit(solution)/shard_map/ffn/pallas_call | solution.py:613
  359.5 2.3 multiply_reduce_fusion
  363.0 5.7 convolution_convert_fusion
  368.7 8.3 %copy.115 = bf16[4,8,64,2048]{3,2,0,1:T(8,128)(2,1)} copy(bf16[4,8,64,2048]{3,2,1,0:T(8,128)(2,1)} %bitcast.124) | data formatting | bytes 16777216 | tf_op jit(solution)/shard_map/reshape | solution.py:830
  377.0 3.5 copy-done
  380.4 42.4 %scatter.5 = f32[256,2048]{1,0:T(8,128)S(1)} custom-call(bf16[8,256,2048]{2,1,0:T(8,128)(2,1)S(1)} %bitcast.107), custom_call_target="tpu_custom_call" | custom-call | bytes 83886080 | tf_op jit(solution)/shard_map/scatter/pallas_call | solution.py:299
  422.8 1.2 convert_element_type.124
  424.4 6.3 fusion.6
  431.0 1.2 copy.136
  432.2 15.4 %exchange.6 = bf16[8,2,128,256]{3,2,1,0:T(8,128)(2,1)} custom-call(bf16[8,2,128,256]{3,2,1,0:T(8,128)(2,1)} %bitcast.140), custom_call_target="tpu_custom_call" | custom-call | bytes 20971520 | tf_op jit(solution)/shard_map/exchange/pallas_call | solution.py:341
  447.6 2.3 copy.112
  449.9 24.8 %attend_back.1 = (bf16[2,1024,32]{2,1,0:T(8,128)(2,1)}, bf16[2,1024,32]{2,1,0:T(8,128)(2,1)}, bf16[2,1024,256]{2,1,0:T(8,128)(2,1)}) custom-call(bf16[2,1024,32]{2,1,0:T(8,128)(2,1)} %bitcast.113, bf16[2,1024,32]{2,1,0:T(8,128)(2,1)} %bitcast.111, bf16[2,1024,256]{2,1,0:T(8,128)(2,1)} %bitcast.115, s32[2,1024,1]{2,1,0:T(8,128)} %copy-done.2, ...), custom_call_target="tpu_custom_call" | custom-call | tf_op jit(solution)/shard_map/attend_back/pallas_call | solution.py:122
  474.8 9.2 %fusion.19 = f32[2048,2048]{1,0:T(8,128)} fusion(bf16[2048,32]{1,0:T(8,128)(2,1)} %bitcast.143, bf16[2048,578]{1,0:T(8,128)(2,1)S(1)} %copy-done.18), kind=kOutput, calls=%fused_computation.45 | convolution fusion | flops 268435456 | bytes 17432576 | tf_op jit(solution)/shard_map/dot_general | solution.py:25
  483.9 8.5 %fusion.14 = f32[2048,2048]{1,0:T(8,128)} fusion(bf16[2048,256]{1,0:T(8,128)(2,1)S(1)} %bitcast.150, bf16[2048,578]{1,0:T(8,128)(2,1)S(1)} %copy-done.18), kind=kOutput, calls=%fused_computation.38 | convolution fusion | flops 2147483648 | bytes 18874368 | tf_op jit(solution)/shard_map/dot_general | solution.py:25
  492.5 16.1 %add_convert_fusion = bf16[2048,2048]{1,0:T(8,128)(2,1)} fusion(f32[2048,2048]{1,0:T(8,128)} %fusion.14, f32[2048,2048]{1,0:T(8,128)} %fusion.19, bf16[2048,32]{1,0:T(8,128)(2,1)S(1)} %bitcast.145, bf16[2048,578]{1,0:T(8,128)(2,1)} %all-gather.4.cloned.1.call-done), kind=kOutput, calls=%fused_computation.5 | convolution fusion | flops 281018368 | bytes 42598400 | tf_op jit(solution)/shard_map/dot_general | solution.py:25
  508.6 8.3 %copy.114 = bf16[2,8,128,2048]{3,2,0,1:T(8,128)(2,1)} copy(bf16[2,8,128,2048]{3,2,1,0:T(8,128)(2,1)} %bitcast.126) | data formatting | bytes 16777216 | tf_op jit(solution)/shard_map/reshape | solution.py:819
  516.9 3.5 copy-done.1
  520.4 38.0 %scatter.4 = f32[256,2048]{1,0:T(8,128)S(1)} custom-call(bf16[8,256,2048]{2,1,0:T(8,128)(2,1)S(1)} %bitcast.108), custom_call_target="tpu_custom_call" | custom-call | bytes 83886080 | tf_op jit(solution)/shard_map/scatter/pallas_call | solution.py:299
  559.6 5.1 convolution_convert_fusion.3
  564.8 5.3 convolution_convert_fusion.4
  570.1 3.3 convolution_convert_fusion.1
  573.5 7.3 %concatenate.11 = bf16[2048,322]{0,1:T(8,128)(2,1)} concatenate(bf16[2048,256]{0,1:T(8,128)(2,1)} %convolution_convert_fusion.1, bf16[2048,32]{0,1:T(8,128)(2,1)S(1)} %convolution_convert_fusion.4, bf16[2048,32]{0,1:T(8,128)(2,1)S(1)} %convolution_convert_fusion.3, bf16[2048,1]{0,1:T(2,128)(2,1)S(1)} %convert_element_type.120, bf16[2048,1]{0,1:T(2,128)(2,1)S(1)} %convert_element_type.122), dimensions={1} | concatenate | bytes 2637824 | tf_op jit(solution)/shard_map/concatenate | solution.py:836
  580.7 6.5 reduce-scatter.12.cloned.1.call-done
  587.2 3.4 copy-done.4
  590.6 40.6 %scatter.3 = f32[256,2048]{1,0:T(8,128)S(1)} custom-call(bf16[8,256,2048]{2,1,0:T(8,128)(2,1)S(1)} %copy-done.4), custom_call_target="tpu_custom_call" | custom-call | bytes 83886080 | tf_op jit(solution)/shard_map/scatter/pallas_call | solution.py:299
  631.2 2.9 fusion.10
  634.1 12.3 %exchange.8 = bf16[8,64,704]{2,1,0:T(8,128)(2,1)} custom-call(bf16[8,64,704]{2,1,0:T(8,128)(2,1)} %bitcast.153), custom_call_target="tpu_custom_call" | custom-call | bytes 14417920 | tf_op jit(solution)/shard_map/exchange/pallas_call | solution.py:341
  646.5 3.9 reshape.232
  650.3 2.8 copy.120
  653.2 2.6 reshape.225
  655.8 12.2 %exchange.9 = bf16[8,64,704]{2,1,0:T(8,128)(2,1)} custom-call(bf16[8,64,704]{2,1,0:T(8,128)(2,1)} %bitcast.154), custom_call_target="tpu_custom_call" | custom-call | bytes 14417920 | tf_op jit(solution)/shard_map/exchange/pallas_call | solution.py:341
  668.0 4.1 reshape.234
  672.1 2.8 copy.121
  674.9 2.7 reshape.227
  677.6 1.3 convert_element_type.127
  679.7 1.9 copy.116
  681.6 8.0 %exchange.7 = bf16[8,64,322]{2,1,0:T(8,128)(2,1)} custom-call(bf16[8,64,322]{2,1,0:T(8,128)(2,1)} %bitcast.148), custom_call_target="tpu_custom_call" | custom-call | bytes 6594560 | tf_op jit(solution)/shard_map/exchange/pallas_call | solution.py:341
  (117 shorter events, 16.0 us)
Async XLA Ops:
  7.2 113.6 %all-gather.4.cloned.1.call-start = ((), (), s32[]{:S(2)}) async-start(), calls=%async_computation.5 | async-start | bytes 3276800 | tf_op jit(solution)/shard_map/all_gather | solution.py:739
  12.2 228.5 %all-gather.6.cloned.1.call-start = ((), (), s32[]{:S(2)}) async-start(), calls=%async_computation.6 | async-start | bytes 7208960 | tf_op jit(solution)/shard_map/all_gather | solution.py:739
  17.5 230.3 %all-gather.8.cloned.1.call-start = ((), (), s32[]{:S(2)}) async-start(), calls=%async_computation.7 | async-start | bytes 3604480 | tf_op jit(solution)/shard_map/all_gather | solution.py:739
  19.7 538.8 %reduce-scatter.10.cloned.1.call-start = ((), (), s32[]{:S(2)}) async-start(), calls=%async_computation.10 | async-start | bytes 3604480 | tf_op jit(solution)/shard_map/reduce_scatter | solution.py:796
  72.6 7.5 %copy-start.30 = (s32[1,2,8]{2,1,0:T(2,128)S(1)}, s32[1,2,8]{2,1,0:T(2,128)}, u32[]{:S(2)}) copy-start(s32[1,2,8]{2,1,0:T(2,128)} %param.13) | copy-start | bytes 196
  80.8 67.5 %copy-start.2 = (s32[2,1024,1]{2,1,0:T(8,128)}, s32[2,1024,1]{2,1,0:T(8,128)S(1)}, u32[]{:S(2)}) copy-start(s32[2,1024,1]{2,1,0:T(8,128)S(1)} %copy.106.first_ref) | copy-start | bytes 24580
  128.4 3.2 copy-start.8
  135.6 12.7 %copy-start.5 = (bf16[2048,32]{1,0:T(8,128)(2,1)}, bf16[2048,32]{1,0:T(8,128)(2,1)S(1)}, u32[]{:S(2)}) copy-start(bf16[2048,32]{1,0:T(8,128)(2,1)S(1)} %copy.105) | copy-start | bytes 393220
  142.1 6.2 copy-start.6
  148.2 12.5 %copy-start.7 = (bf16[2048,256]{1,0:T(8,128)(2,1)}, bf16[2048,256]{1,0:T(8,128)(2,1)S(1)}, u32[]{:S(2)}) copy-start(bf16[2048,256]{1,0:T(8,128)(2,1)S(1)} %convolution_convert_fusion.2) | copy-start | bytes 3145732
  158.7 1.0 copy-start.3
  177.6 54.6 %copy-start.19 = (bf16[32,8,8,256]{3,1,2,0:T(8,128)(2,1)}, bf16[32,8,8,256]{3,1,2,0:T(8,128)(2,1)S(1)}, u32[]{:S(2)}) copy-start(bf16[32,8,8,256]{3,1,2,0:T(8,128)(2,1)S(1)} %copy.126) | copy-start | bytes 3145732
  220.1 12.2 %copy-start.14 = (bf16[1,2,128,2048]{3,2,1,0:T(8,128)(2,1)S(1)}, bf16[1,2,128,2048]{3,2,1,0:T(8,128)(2,1)}, u32[]{:S(2)}) copy-start(bf16[1,2,128,2048]{3,2,1,0:T(8,128)(2,1)} %param.12) | copy-start | bytes 3145732
  238.1 1.3 copy-start.9
  357.2 201.3 %reduce-scatter.6.cloned.1.call-start = ((), (), s32[]{:S(2)}) async-start(), calls=%async_computation.8 | async-start | bytes 3932160 | tf_op jit(solution)/shard_map/reduce_scatter | solution.py:796
  357.3 1.4 copy-start.15
  357.8 1.7 copy-start.10
  357.8 200.7 %reduce-scatter.8.cloned.1.call-start = ((), (), s32[]{:S(2)}) async-start(), calls=%async_computation.9 | async-start | bytes 3932160 | tf_op jit(solution)/shard_map/reduce_scatter | solution.py:796
  358.4 228.8 %reduce-scatter.12.cloned.1.call-start = ((), (), s32[]{:S(2)}) async-start(), calls=%async_computation.11 | async-start | bytes 1310720 | tf_op jit(solution)/shard_map/reduce_scatter | solution.py:796
  358.7 3.1 copy-start.12
  358.7 3.1 copy-start.16
  361.8 1.2 copy-start.20
  363.0 5.7 copy-start.21
  377.0 3.5 copy-start
  422.8 1.6 copy-start.22
  449.9 24.8 %copy-start.18 = (bf16[2048,578]{1,0:T(8,128)(2,1)S(1)}, bf16[2048,578]{1,0:T(8,128)(2,1)}, u32[]{:S(2)}) copy-start(bf16[2048,578]{1,0:T(8,128)(2,1)} %all-gather.4.cloned.1.call-done) | copy-start | bytes 7102468
  474.7 9.2 %copy-start.26 = (bf16[2,1024,256]{2,1,0:T(8,128)(2,1)S(1)}, bf16[2,1024,256]{2,1,0:T(8,128)(2,1)}, u32[]{:S(2)}) copy-start(bf16[2,1024,256]{2,1,0:T(8,128)(2,1)} %get-tuple-element.27) | copy-start | bytes 3145732
  483.9 8.5 %copy-start.24 = (bf16[2,1024,32]{2,1,0:T(8,128)(2,1)S(1)}, bf16[2,1024,32]{2,1,0:T(8,128)(2,1)}, u32[]{:S(2)}) copy-start(bf16[2,1024,32]{2,1,0:T(8,128)(2,1)} %get-tuple-element.29) | copy-start | bytes 393220
  516.9 3.5 copy-start.1
  558.5 121.2 %reduce-scatter.14.cloned.1.call-start = ((), (), s32[]{:S(2)}) async-start(), calls=%async_computation.12 | async-start | bytes 1679360 | tf_op jit(solution)/shard_map/reduce_scatter | solution.py:796
  558.6 1.0 copy-start.25
  559.6 5.1 copy-start.23
  559.6 10.4 %slice-start = ((s8[8388608]{0:T(1024)(128)(4,1)}), s8[4194304]{0:T(1024)(128)(4,1)S(1)}, s32[]{:S(2)}) async-start(s8[8388608]{0:T(1024)(128)(4,1)} %bitcast.121), calls=%async_computation.13 | async-start | bytes 8388608
  564.7 5.3 slice-start.1
  564.8 5.3 copy-start.27
  587.2 3.4 copy-start.4
  590.6 40.6 %copy-start.11 = (f32[256,2048]{1,0:T(8,128)S(1)}, f32[256,2048]{1,0:T(8,128)}, u32[]{:S(2)}) copy-start(f32[256,2048]{1,0:T(8,128)} %copy-done.9) | copy-start | bytes 6291460
  590.6 40.6 %copy-start.13 = (f32[256,2048]{1,0:T(8,128)S(1)}, f32[256,2048]{1,0:T(8,128)}, u32[]{:S(2)}) copy-start(f32[256,2048]{1,0:T(8,128)} %get-tuple-element.26) | copy-start | bytes 6291460
  590.6 40.6 %copy-start.17 = (bf16[1,2,128,2048]{3,2,1,0:T(8,128)(2,1)S(1)}, bf16[1,2,128,2048]{3,2,1,0:T(8,128)(2,1)}, u32[]{:S(2)}) copy-start(bf16[1,2,128,2048]{3,2,1,0:T(8,128)(2,1)} %param.23) | copy-start | bytes 3145732
  674.9 2.7 copy-start.28
  674.9 3.9 copy-start.29
Sparse Core Ops, SparseCore 0:
  12.3 56.8 all-gather.3
  71.3 105.7 all-gather.5
  178.7 57.1 all-gather.7
  357.3 59.5 reduce-scatter.9
  419.1 60.0 reduce-scatter.5
  481.3 60.2 reduce-scatter.7
  558.7 28.4 reduce-scatter.11
  589.6 30.3 reduce-scatter.13

commit v5 on v2

--- a/solution.py
+++ b/solution.py
@@ -354,6 +354,858 @@
     )(x)
 
 
+CHUNKS = (64, 64, 48)
+
+
+class PlaneGather:
+    def __init__(self, source, target, send, recv):
+        me, sib, xn, yn = partners()
+        diag = xn + yn - me
+        half = target.shape[1] // 2
+        upper, lower = pl.ds(0, half), pl.ds(half, half)
+        copy = functools.partial(remote, send, recv)
+
+        def direct(k, part, to):
+            return copy(k, source.at[part], target.at[me, part], to)
+
+        def pass_on(k, origin, part, to):
+            return copy(k, target.at[origin, part], target.at[origin, part], to)
+
+        self.xa, self.yb = direct(0, upper, xn), direct(1, lower, yn)
+        self.xb, self.ya = direct(2, lower, xn), direct(3, upper, yn)
+        self.s0 = copy(4, source, target.at[me], sib)
+        self.fy, self.fx = pass_on(5, xn, upper, yn), pass_on(6, yn, lower, xn)
+        self.s1, self.s2 = pass_on(7, xn, upper, sib), pass_on(8, yn, lower, sib)
+        self.s3, self.s4 = pass_on(9, xn, lower, sib), pass_on(10, yn, upper, sib)
+        self.s5, self.s6 = pass_on(11, diag, upper, sib), pass_on(12, diag, lower, sib)
+
+    def start(self):
+        for c in (self.xa, self.yb, self.xb, self.ya, self.s0):
+            c.start()
+
+    def forward_first(self):
+        self.xa.wait_recv()
+        self.yb.wait_recv()
+        for c in (self.fy, self.fx, self.s1, self.s2):
+            c.start()
+
+    def forward_second(self):
+        self.xb.wait_recv()
+        self.ya.wait_recv()
+        self.s3.start()
+        self.s4.start()
+
+    def forward_third(self):
+        self.fy.wait_recv()
+        self.fx.wait_recv()
+        self.s5.start()
+        self.s6.start()
+
+    def from_sibling(self, chip):
+        for c in {"own": (self.s0,), "x": (self.s1, self.s3), "y": (self.s2, self.s4), "diag": (self.s5, self.s6)}[chip]:
+            c.wait_recv()
+
+    def sent(self):
+        for c in (self.xa, self.yb, self.xb, self.ya, self.s0, self.fy, self.fx):
+            c.wait_send()
+        for c in (self.s1, self.s2, self.s3, self.s4, self.s5, self.s6):
+            c.wait_send()
+
+    def arrive(self, step):
+        @pl.when(step == 1)
+        def _():
+            self.from_sibling("own")
+
+        @pl.when(step == 2)
+        def _():
+            self.forward_first()
+            self.forward_second()
+            self.from_sibling("x")
+
+        @pl.when(step == 4)
+        def _():
+            self.from_sibling("y")
+
+        @pl.when(step == 6)
+        def _():
+            self.forward_third()
+            self.from_sibling("diag")
+
+
+class LineGather:
+    def __init__(self, item, source, block, send, recv, local):
+        z = lax.axis_index("dp")
+        self.z = z
+
+        def copy(k, src, owner, to):
+            return pltpu.make_async_remote_copy(
+                src_ref=src,
+                dst_ref=block(owner),
+                send_sem=send.at[item, k],
+                recv_sem=recv.at[item, owner],
+                device_id={"dp": to},
+                device_id_type=MESH,
+            )
+
+        self.sends = []
+        for k, d in enumerate((2, -2, 1, -1)):
+            to = z + d
+            valid = (to >= 0) & (to < 4)
+            self.sends.append((valid, copy(k, source, z, jnp.clip(to, 0, 3))))
+        inner = (z == 1) | (z == 2)
+        far = jnp.where(z == 1, 3, 0)
+        self.stop = (inner, copy(4, block(far), far, jnp.where(z == 1, 0, 3)))
+        others = [lax.rem(z + o, 4) for o in (1, 2, 3)]
+        self.blocks = [copy(0, source, other, other) for other in others]
+        self.own = pltpu.make_async_copy(source, block(z), local.at[item])
+
+    def start(self):
+        self.own.start()
+        for valid, c in self.sends:
+
+            @pl.when(valid)
+            def _(c=c):
+                c.start()
+
+    def forward(self):
+        inner, c = self.stop
+
+        @pl.when(inner)
+        def _():
+            self.blocks[1].wait_recv()
+            c.start()
+
+    def wait(self):
+        inner, unused = self.stop
+        self.blocks[0].wait_recv()
+        self.blocks[2].wait_recv()
+
+        @pl.when(jnp.logical_not(inner))
+        def _():
+            self.blocks[1].wait_recv()
+
+        self.own.wait()
+
+    def sent(self):
+        for valid, c in (*self.sends, self.stop):
+
+            @pl.when(valid)
+            def _(c=c):
+                c.wait_send()
+
+
+def nearest_first(step):
+    me, sib, xn, yn = partners()
+    chip = jnp.where(step < 4, xn, jnp.where(step < 6, yn, xn + yn - me))
+    later = chip + jnp.where(lax.rem(step, 2) == 0, sib - me, 0)
+    return jnp.where(step == 0, me, jnp.where(step == 1, sib, later))
+
+
+def farthest_first(step):
+    me, sib, xn, yn = partners()
+    chip = jnp.where(step < 4, xn, yn)
+    chip = jnp.where(step < 2, xn + yn - me, jnp.where(step < 6, chip, me))
+    return chip + jnp.where(lax.rem(step, 2) == 0, sib - me, 0)
+
+
+def layer_kernel(
+    x_ref,
+    c_ref,
+    wa_ref,
+    wo_ref,
+    wgu_ref,
+    wd_ref,
+    gain_ref,
+    first_ref,
+    x_all,
+    c_all,
+    h2_all,
+    wo_all,
+    h1_out,
+    q_out,
+    k_out,
+    v_out,
+    att_out,
+    tok_out,
+    mid_out,
+    wa_out,
+    gain_out,
+    out_part,
+    gh_ref,
+    dgu_out,
+    dd_out,
+    wa,
+    wgu,
+    wd,
+    gains,
+    q_s,
+    k_s,
+    v_s,
+    att_s,
+    tok,
+    mid,
+    act_s,
+    ggu_s,
+    sum_gu,
+    sum_d,
+    x_buf,
+    c_buf,
+    o_buf,
+    w_buf,
+    beside,
+    held,
+    got,
+    one,
+    two,
+    gsend,
+    grecv,
+    zsend,
+    zrecv,
+    zlocal,
+    esend,
+    erecv,
+    rsend,
+    rrecv,
+    load_sem,
+    out_sem,
+    h1_sem,
+    w_sem,
+    done_sem,
+    self_sem,
+):
+    me, sib, xn, yn = partners()
+    z = lax.axis_index("dp")
+    rows, width = x_ref.shape
+    span = rows // 2
+    wide, qk = v_s.shape[2], q_s.shape[2]
+    share = CHUNKS[0] + CHUNKS[1] + CHUNKS[2]
+    half = rows // 2
+    upper, lower = pl.ds(0, half), pl.ds(half, half)
+
+    barrier = pltpu.get_barrier_semaphore()
+    for i in range(1, 8):
+        pl.semaphore_signal(
+            barrier, inc=1, device_id={"seq": lax.rem(me + i, 8)}, device_id_type=MESH
+        )
+    for i in range(1, 4):
+        pl.semaphore_signal(
+            barrier, inc=1, device_id={"dp": lax.rem(z + i, 4)}, device_id_type=MESH
+        )
+    pl.semaphore_wait(barrier, 10)
+
+    tokens = PlaneGather(x_ref, x_all, gsend.at[0], grecv.at[0])
+    out_w = PlaneGather(wo_all.at[me], wo_all, gsend.at[1], grecv.at[1])
+    cots = PlaneGather(c_ref, c_all, gsend.at[2], grecv.at[2])
+    hidden_in = PlaneGather(held.at[0], h2_all, gsend.at[3], grecv.at[3])
+
+    def line(item, source, block):
+        return LineGather(item, source, block, zsend, zrecv, zlocal)
+
+    depth = wa_ref.shape[0]
+
+    def rows_of(ref, count, columns=None):
+        def block(owner):
+            if columns is None:
+                return ref.at[pl.ds(owner * count, count)]
+            return ref.at[pl.ds(owner * count, count), columns]
+
+        return block
+
+    z_gain = line(
+        0, gain_ref, lambda owner: gains.at[:, pl.ds(pl.multiple_of(owner * depth, 128), depth)]
+    )
+    z_attn = line(1, wa_ref, rows_of(wa, depth))
+    z_out = line(
+        2,
+        wo_ref.at[:, pl.ds(pl.multiple_of(me * wide, 128), wide)],
+        lambda owner: wo_all.at[me, pl.ds(owner * depth, depth)],
+    )
+    z_up, z_down = [], []
+    column, before = 0, 0
+    columns, hiddens = [], []
+    for k, count in enumerate(CHUNKS):
+        part = pl.ds(column, 8 * count)
+        z_up.append(line(3 + k, wgu_ref.at[:, part], rows_of(wgu, depth, part)))
+        z_down.append(
+            line(
+                6 + k,
+                wd_ref.at[pl.ds(me * share + before, count)],
+                lambda owner, base=4 * before, count=count: wd.at[
+                    pl.ds(base + owner * count, count)
+                ],
+            )
+        )
+        columns.append(column)
+        hiddens.append(4 * before)
+        column += 8 * count
+        before += count
+
+    tokens.start()
+    for g in (z_gain, z_attn, z_out):
+        g.start()
+
+    def loads(order, step, sources):
+        slot = lax.rem(step, 2)
+        owner = order(step)
+        return [
+            pltpu.make_async_copy(source.at[owner], buf.at[slot], load_sem.at[i, slot])
+            for i, (source, buf) in enumerate(sources)
+        ]
+
+    first_load = pltpu.make_async_copy(x_ref, x_buf.at[0], load_sem.at[0, 0])
+    first_load.start()
+    tokens.forward_first()
+    z_gain.forward()
+    z_attn.forward()
+    tokens.forward_second()
+    z_gain.wait()
+    z_attn.wait()
+    for g in (z_up[0], z_down[0]):
+        g.start()
+
+    def h1_copies(step):
+        slot = lax.rem(step, 2)
+        owner = nearest_first(step)
+        return [
+            pltpu.make_async_copy(
+                o_buf.at[slot, pl.ds(m * span, span)],
+                h1_out.at[m, pl.ds(owner * span, span)],
+                h1_sem.at[m, slot],
+            )
+            for m in range(2)
+        ]
+
+    def arrive_tokens(step):
+        @pl.when(step == 1)
+        def _():
+            tokens.from_sibling("own")
+
+        @pl.when(step == 2)
+        def _():
+            tokens.from_sibling("x")
+
+        @pl.when(step == 4)
+        def _():
+            tokens.forward_third()
+            tokens.from_sibling("y")
+
+        @pl.when(step == 5)
+        def _():
+            z_out.forward()
+
+        @pl.when(step == 6)
+        def _():
+            tokens.from_sibling("diag")
+
+    token_source = [(x_all, x_buf)]
+
+    def project(step, carry):
+        slot = lax.rem(step, 2)
+        owner = nearest_first(step)
+        for c in loads(nearest_first, step, token_source):
+            c.wait()
+
+        @pl.when(step >= 2)
+        def _():
+            for c in h1_copies(step - 2):
+                c.wait()
+
+        x = x_buf[slot].astype(jnp.float32)
+        gain = gains[0:1, :].astype(jnp.float32)
+        h_one = (x * norm_scale(x) * gain).astype(LOW)
+        o_buf[slot] = h_one
+        for c in h1_copies(step):
+            c.start()
+        arrive_tokens(step + 1)
+
+        @pl.when(step < 7)
+        def _():
+            for c in loads(nearest_first, step + 1, token_source):
+                c.start()
+
+        projected = dot(h_one, wa[...]).astype(LOW)
+        for m in range(2):
+            there = pl.ds(owner * span, span)
+            mine = projected[m * span : (m + 1) * span]
+            v_s[m, there, :] = mine[:, :wide]
+            q_s[m, there, :] = mine[:, wide : wide + qk]
+            k_s[m, there, :] = mine[:, wide + qk : wide + 2 * qk]
+        return carry
+
+    lax.fori_loop(0, 8, project, 0)
+    for step in (6, 7):
+        for c in h1_copies(step):
+            c.wait()
+    z_out.wait()
+    out_w.start()
+    for g in (z_up[1], z_down[1]):
+        g.start()
+
+    finals = [
+        pltpu.make_async_copy(source, target, done_sem.at[i])
+        for i, (source, target) in enumerate(
+            (
+                (q_s, q_out),
+                (k_s, k_out),
+                (v_s, v_out),
+                (wa, wa_out),
+                (gains, gain_out),
+                (att_s, att_out),
+                (tok, tok_out),
+                (mid, mid_out),
+            )
+        )
+    ]
+    for c in finals[:5]:
+        c.start()
+
+    length = v_s.shape[1]
+    block = 256
+
+    def attend_stream(m, carry):
+        for i in range(length // block):
+            rows_i = slice(i * block, (i + 1) * block)
+            seen = (i + 1) * block
+            for head in range(wide // HEAD_V):
+                lanes = slice(head * HEAD_V, (head + 1) * HEAD_V)
+                unused, unused_mask, weight = weights_of(
+                    q_s[m, rows_i, :], k_s[m, :seen, :], head, first_ref[m, rows_i, :], i * block
+                )
+                denom = jnp.sum(weight, axis=1, keepdims=True)
+                numer = dot(weight.astype(LOW), v_s[m, :seen, lanes])
+                att_s[m, rows_i, lanes] = (numer / denom).astype(LOW)
+        return carry
+
+    lax.fori_loop(0, 2, attend_stream, 0)
+    out_w.forward_first()
+    cots.start()
+    finals[5].start()
+
+    to_mine = pl.ds(pl.multiple_of(me * wide, 128), wide)
+    swaps = []
+    for i in range(1, 8):
+        other = lax.rem(me + i, 8)
+        for m in range(2):
+            swaps.append(
+                remote(
+                    esend,
+                    erecv,
+                    2 * (i - 1) + m,
+                    att_s.at[m, pl.ds(other * span, span)],
+                    tok.at[pl.ds(m * span, span), to_mine],
+                    other,
+                )
+            )
+            swaps[-1].start()
+    kept = [
+        pltpu.make_async_copy(
+            att_s.at[m, pl.ds(me * span, span)],
+            tok.at[pl.ds(m * span, span), to_mine],
+            self_sem.at[m],
+        )
+        for m in range(2)
+    ]
+    for c in kept:
+        c.start()
+    x_load = pltpu.make_async_copy(x_ref, x_buf.at[0], load_sem.at[0, 0])
+    x_load.start()
+
+    def w_load(step):
+        slot = lax.rem(step, 2)
+        return pltpu.make_async_copy(wo_all.at[nearest_first(step)], w_buf.at[slot], w_sem.at[slot])
+
+    w_load(0).start()
+    out_w.forward_second()
+    z_up[0].forward()
+    z_down[0].forward()
+    for c in kept:
+        c.wait()
+    for c in swaps:
+        c.wait_recv()
+    finals[6].start()
+    x_load.wait()
+
+    def arrive_out(step):
+        @pl.when(step == 1)
+        def _():
+            out_w.from_sibling("own")
+
+        @pl.when(step == 2)
+        def _():
+            out_w.from_sibling("x")
+
+        @pl.when(step == 4)
+        def _():
+            out_w.forward_third()
+            out_w.from_sibling("y")
+
+        @pl.when(step == 6)
+        def _():
+            out_w.from_sibling("diag")
+
+    def project_out(step, carry):
+        slot = lax.rem(step, 2)
+        owner = nearest_first(step)
+        w_load(step).wait()
+        arrive_out(step + 1)
+
+        @pl.when(step < 7)
+        def _():
+            w_load(step + 1).start()
+
+        there = pl.ds(pl.multiple_of(owner * wide, 128), wide)
+        mid[:, there] = dot(tok[...], w_buf[slot])
+        return carry
+
+    lax.fori_loop(0, 8, project_out, 0)
+    mid_value = x_buf[0].astype(jnp.float32) + mid[...]
+    mid[...] = mid_value
+    held[0] = (mid_value * norm_scale(mid_value) * gains[1:2, :].astype(jnp.float32)).astype(LOW)
+    finals[7].start()
+    hidden_in.start()
+    own_h2 = pltpu.make_async_copy(held.at[0], h2_all.at[me], self_sem.at[2])
+    own_c = pltpu.make_async_copy(c_ref, c_all.at[me], self_sem.at[3])
+    own_h2.start()
+    own_c.start()
+    cots.forward_first()
+    cots.forward_second()
+    for g in (z_up[2], z_down[2]):
+        g.start()
+    own_h2.wait()
+    own_c.wait()
+    z_up[0].wait()
+    z_down[0].wait()
+
+    sources = [(h2_all, x_buf), (c_all, c_buf)]
+
+    def out_copy(order, step):
+        slot = lax.rem(step, 2)
+        return pltpu.make_async_copy(o_buf.at[slot], out_part.at[order(step)], out_sem.at[slot])
+
+    def hidden_chunk(k, owner, h, c):
+        count = 4 * CHUNKS[k]
+        pair = pl.ds(columns[k], 2 * count)
+        here = pl.ds(hiddens[k], count)
+        both = dot(h, wgu[:, pair])
+        gate, up = both[:, :count], both[:, count:]
+        g_act = contract(c, wd[here, :], 1, 1)
+        sigmoid = jax.nn.sigmoid(gate)
+        silu = gate * sigmoid
+        act = (silu * up).astype(LOW)
+        g_gate = (g_act * up * sigmoid * (1.0 + gate * (1.0 - sigmoid))).astype(LOW)
+        g_up = (g_act * silu).astype(LOW)
+        there = pl.ds(owner * rows, rows)
+        act_s[there, here] = act
+        g_both = jnp.concatenate([g_gate, g_up], axis=1)
+        ggu_s[there, pair] = g_both
+        return act, g_both
+
+    def add_grads(k, step, h, c, act, g_both):
+        count = 4 * CHUNKS[k]
+
+        @pl.when(step == 0)
+        def _():
+            sum_gu[...] = jnp.zeros_like(sum_gu)
+            sum_d[...] = jnp.zeros_like(sum_d)
+
+        sum_gu[:, : 2 * count] += contract(h, g_both, 0, 0)
+        sum_d[:count, :] += contract(act, c, 0, 0)
+
+    def emit(k):
+        count = 4 * CHUNKS[k]
+        pending = [None, None]
+        for i in range(width // rows):
+            slot = i % 2
+            if pending[slot] is not None:
+                pending[slot].wait()
+            o_buf[slot, :, : 2 * count] = sum_gu[i * rows : (i + 1) * rows, : 2 * count].astype(LOW)
+            pending[slot] = pltpu.make_async_copy(
+                o_buf.at[slot, :, pl.ds(0, 2 * count)],
+                dgu_out.at[pl.ds(i * rows, rows), pl.ds(columns[k], 2 * count)],
+                out_sem.at[slot],
+            )
+            pending[slot].start()
+        for c in pending:
+            c.wait()
+        o_buf[0, :count, :] = sum_d[:count, :].astype(LOW)
+        downs = []
+        for owner in range(4):
+            downs.append(
+                pltpu.make_async_copy(
+                    o_buf.at[0, pl.ds(owner * CHUNKS[k], CHUNKS[k])],
+                    dd_out.at[pl.ds(owner * share + hiddens[k] // 4, CHUNKS[k])],
+                    h1_sem.at[owner // 2, owner % 2],
+                )
+            )
+            downs[-1].start()
+        for c in downs:
+            c.wait()
+
+    def forward_pass(k, arrive, step, carry):
+        slot = lax.rem(step, 2)
+        for c in loads(nearest_first, step, sources):
+            c.wait()
+        h, c = x_buf[slot], c_buf[slot]
+        act, g_both = hidden_chunk(k, nearest_first(step), h, c)
+        if arrive is not None:
+            arrive(step + 1)
+
+        @pl.when(step < 7)
+        def _():
+            for c in loads(nearest_first, step + 1, sources):
+                c.start()
+
+        add_grads(k, step, h, c, act, g_both)
+        return carry
+
+    def arrive_both(step):
+        hidden_in.arrive(step)
+
+        @pl.when(step == 1)
+        def _():
+            cots.from_sibling("own")
+
+        @pl.when(step == 2)
+        def _():
+            cots.from_sibling("x")
+
+        @pl.when(step == 4)
+        def _():
+            cots.forward_third()
+            cots.from_sibling("y")
+
+        @pl.when(step == 5)
+        def _():
+            z_up[1].forward()
+            z_down[1].forward()
+
+        @pl.when(step == 6)
+        def _():
+            cots.from_sibling("diag")
+
+    for c in loads(nearest_first, 0, sources):
+        c.start()
+    lax.fori_loop(0, 8, functools.partial(forward_pass, 0, arrive_both), 0)
+    hidden_in.sent()
+    z_up[1].wait()
+    z_down[1].wait()
+    for c in loads(nearest_first, 0, sources):
+        c.start()
+    emit(0)
+
+    def arrive_last(step):
+        @pl.when(step == 4)
+        def _():
+            z_up[2].forward()
+            z_down[2].forward()
+
+    lax.fori_loop(0, 8, functools.partial(forward_pass, 1, arrive_last), 0)
+    z_up[2].wait()
+    z_down[2].wait()
+    for c in loads(farthest_first, 0, sources):
+        c.start()
+    emit(1)
+
+    copy = functools.partial(remote, rsend, rrecv)
+    b_diag = copy(0, beside.at[0], got.at[2], sib)
+    b_x = copy(1, beside.at[1], got.at[1], sib)
+    b_y = copy(2, beside.at[0], got.at[3], sib)
+    b_own = copy(3, beside.at[1], got.at[0], sib)
+    x0 = copy(4, held.at[2, upper], one.at[0], xn)
+    y0 = copy(5, held.at[2, lower], one.at[1], yn)
+    x1 = copy(6, held.at[1, upper], one.at[2], xn)
+    y1 = copy(7, held.at[3, lower], one.at[3], yn)
+    y2 = copy(8, held.at[3, upper], two.at[0], yn)
+    x2 = copy(9, held.at[1, lower], two.at[1], xn)
+
+    def last_pass(step, carry):
+        slot = lax.rem(step, 2)
+        owner = farthest_first(step)
+        there = pl.ds(owner * rows, rows)
+        for c in loads(farthest_first, step, sources):
+            c.wait()
+        h, c = x_buf[slot], c_buf[slot]
+        act, g_both = hidden_chunk(2, owner, h, c)
+        part = contract(ggu_s[there, :], wgu[...], 1, 1).astype(LOW)
+
+        for k, place, sent in ((0, 0, b_diag), (2, 1, b_x), (4, 0, b_y), (6, 1, b_own)):
+
+            @pl.when(step == k)
+            def _(k=k, place=place, sent=sent):
+                if k == 4:
+                    b_diag.wait_send()
+                if k == 6:
+                    b_x.wait_send()
+                beside[place] = part
+                sent.start()
+
+        for k, place, arrived in ((1, 2, b_diag), (3, 1, b_x), (5, 3, b_y), (7, 0, b_own)):
+
+            @pl.when(step == k)
+            def _(k=k, place=place, arrived=arrived):
+                arrived.wait_recv()
+                held[place] = part + got[place]
+                if k == 1:
+                    x0.start()
+                    y0.start()
+                if k == 3:
+                    x1.start()
+                if k == 5:
+                    y1.start()
+                    y0.wait_recv()
+                    held[1, half:] = held[1, half:] + one[1]
+                    x2.start()
+                    x0.wait_recv()
+                    held[3, :half] = held[3, :half] + one[0]
+                    y2.start()
+
+        @pl.when(step >= 2)
+        def _():
+            out_copy(farthest_first, step - 2).wait()
+
+        o_buf[slot] = dot(act_s[there, :], wd[...]).astype(LOW)
+        out_copy(farthest_first, step).start()
+
+        @pl.when(step < 7)
+        def _():
+            for c in loads(farthest_first, step + 1, sources):
+                c.start()
+
+        add_grads(2, step, h, c, act, g_both)
+        return carry
+
+    lax.fori_loop(0, 8, last_pass, 0)
+    out_copy(farthest_first, 6).wait()
+    out_copy(farthest_first, 7).wait()
+    emit(2)
+    f32 = jnp.float32
+    x1.wait_recv()
+    y2.wait_recv()
+    gh_ref[:half] = held[0, :half].astype(f32) + one[2].astype(f32) + two[0].astype(f32)
+    y1.wait_recv()
+    x2.wait_recv()
+    gh_ref[half:] = held[0, half:].astype(f32) + one[3].astype(f32) + two[1].astype(f32)
+    for c in finals:
+        c.wait()
+    for c in (b_y, b_own, x0, y0, x1, y1, y2, x2, *swaps):
+        c.wait_send()
+    for g in (tokens, out_w, cots, z_gain, z_attn, z_out, *z_up, *z_down):
+        g.sent()
+
+
+def layer_front(tokens, cot, attn_slice, w_out, ffn_slice, w_down, gain_rows, first, wide, qk):
+    rows, width = tokens.shape
+    streams, length, unused = first.shape
+    hidden = 4 * sum(CHUNKS)
+    largest = 4 * max(CHUNKS)
+    shape = jax.ShapeDtypeStruct
+    f32 = jnp.float32
+    anywhere = pl.BlockSpec(memory_space=pl.ANY)
+    in_vmem = pl.BlockSpec(memory_space=pltpu.VMEM)
+    plane = shape((8, rows, width), LOW)
+    narrow = shape((streams, length, qk), LOW)
+    broad = shape((streams, length, wide), LOW)
+    attn_shape = (width, attn_slice.shape[1])
+    out_shape = [
+        plane,
+        plane,
+        plane,
+        shape((8, width, width // 8), LOW),
+        shape((streams, length, width), LOW),
+        narrow,
+        narrow,
+        broad,
+        broad,
+        shape((rows, width), LOW),
+        shape((rows, width), f32),
+        shape(attn_shape, LOW),
+        shape((gain_rows.shape[0], width), LOW),
+        plane,
+        shape((rows, width), f32),
+        shape((width, 2 * hidden), LOW),
+        shape((hidden, width), LOW),
+    ]
+    dma = pltpu.SemaphoreType.DMA
+    vmem = pltpu.VMEM
+    return pl.pallas_call(
+        layer_kernel,
+        out_shape=out_shape,
+        in_specs=[anywhere] * 7 + [in_vmem],
+        out_specs=[anywhere] * 14 + [in_vmem] + [anywhere] * 2,
+        scratch_shapes=[
+            vmem(attn_shape, LOW),
+            vmem((width, 2 * hidden), LOW),
+            vmem((hidden, width), LOW),
+            vmem((gain_rows.shape[0], width), LOW),
+            vmem(narrow.shape, LOW),
+            vmem(narrow.shape, LOW),
+            vmem(broad.shape, LOW),
+            vmem(broad.shape, LOW),
+            vmem((rows, width), LOW),
+            vmem((rows, width), f32),
+            vmem((8 * rows, hidden), LOW),
+            vmem((8 * rows, 2 * hidden), LOW),
+            vmem((width, 2 * largest), f32),
+            vmem((largest, width), f32),
+            vmem((2, rows, width), LOW),
+            vmem((2, rows, width), LOW),
+            vmem((2, rows, width), LOW),
+            vmem((2, width, width // 8), LOW),
+            vmem((2, rows, width), LOW),
+            vmem((4, rows, width), LOW),
+            vmem((4, rows, width), LOW),
+            vmem((4, rows // 2, width), LOW),
+            vmem((2, rows // 2, width), LOW),
+            dma((4, 13)),
+            dma((4, 13)),
+            dma((9, 5)),
+            dma((9, 4)),
+            dma((9,)),
+            dma((14,)),
+            dma((14,)),
+            dma((10,)),
+            dma((10,)),
+            dma((2, 2)),
+            dma((2,)),
+            dma((2, 2)),
+            dma((2,)),
+            dma((8,)),
+            dma((4,)),
+        ],
+        compiler_params=pltpu.CompilerParams(
+            collective_id=21, has_side_effects=True, vmem_limit_bytes=63 * MIB
+        ),
+        cost_estimate=pl.CostEstimate(
+            flops=6 * 3 * 8 * rows * width * hidden,
+            bytes_accessed=400 * rows * width,
+            transcendentals=0,
+        ),
+        name="layer",
+    )(tokens, cot, attn_slice, w_out, ffn_slice, w_down, gain_rows, first)
+
+
+def ffn_lax(h_two, cot_all, gate_full, up_full, down_full):
+    pieces, rows, width = cot_all.shape
+    h_two_all = gather_plane(h_two, 5).reshape(-1, width)
+    cot_all = cot_all.reshape(-1, width)
+    gate = dot(h_two_all, gate_full)
+    up = dot(h_two_all, up_full)
+    g_act = contract(cot_all, down_full, 1, 1)
+    sigmoid = jax.nn.sigmoid(gate)
+    silu = gate * sigmoid
+    act = (silu * up).astype(LOW)
+    g_gate = (g_act * up * sigmoid * (1.0 + gate * (1.0 - sigmoid))).astype(LOW)
+    g_up = (g_act * silu).astype(LOW)
+    part = (contract(g_gate, gate_full, 1, 1) + contract(g_up, up_full, 1, 1)).astype(LOW)
+    return (
+        dot(act, down_full).astype(LOW).reshape(pieces, rows, width),
+        scatter_plane(part.reshape(pieces, rows, width), 7),
+        contract(h_two_all, g_gate, 0, 0).astype(LOW),
+        contract(h_two_all, g_up, 0, 0).astype(LOW),
+        contract(act, cot_all, 0, 0).astype(LOW),
+    )
+
+
 def norm_scale(rows):
     return lax.rsqrt(jnp.mean(rows * rows, axis=-1, keepdims=True) + epsilon)
 
@@ -390,41 +1242,31 @@
     hidden = FF // pieces
 
     out_width = D // pieces
-    attn_slice = jnp.concatenate(
-        [
-            lax.dynamic_slice_in_dim(w_value, first_head * HEAD_V, wide, 1),
-            lax.dynamic_slice_in_dim(w_out, place * out_width, out_width, 1),
-            lax.dynamic_slice_in_dim(w_query, first_head * QK_DIM, qk, 1),
-            lax.dynamic_slice_in_dim(w_key, first_head * QK_DIM, qk, 1),
-            gain_attn[:, None],
-            gain_mlp[:, None],
-        ],
-        axis=1,
-    )
     rows_dp = w_gate.shape[0]
     share = hidden // groups
     block = FF // groups
+    mine = micro * span
+    fused = pieces == 8 and groups == 4 and micro == 2 and span == 128
+    chunks = CHUNKS if fused else (share,)
 
     def hidden_columns(w):
-        return [
+        parts = [
             lax.dynamic_slice_in_dim(w, z * block + place * share, share, 1) for z in range(groups)
         ]
-
-    ffn_slice = jnp.concatenate(hidden_columns(w_gate) + hidden_columns(w_up), axis=1)
-    down_slice = lax.dynamic_slice_in_dim(w_down, place * share, share, 0)
-
-    def gather_dp(w):
-        return lax.all_gather(w, "dp", axis=0, tiled=True)
-
-    attn_got = gather_dp(attn_slice)
-    ffn_full = gather_dp(ffn_slice)
-    down_full = gather_dp(down_slice)
-    value_full = attn_got[:, :wide]
-    query_full = attn_got[:, wide + out_width : wide + out_width + qk]
-    key_full = attn_got[:, wide + out_width + qk : wide + out_width + 2 * qk]
-    gains = attn_got[:, wide + out_width + 2 * qk :].astype(jnp.float32)
-    gain_one, gain_two = gains[:, 0], gains[:, 1]
-    gate_full, up_full = ffn_full[:, :hidden], ffn_full[:, hidden:]
+        edges = [sum(chunks[:k]) for k in range(len(chunks) + 1)]
+        return [
+            [part[:, edges[k] : edges[k + 1]] for part in parts] for k in range(len(chunks))
+        ]
+
+    gate_parts, up_parts = hidden_columns(w_gate), hidden_columns(w_up)
+    ffn_slice = jnp.concatenate(
+        [part for k in range(len(chunks)) for part in gate_parts[k] + up_parts[k]], axis=1
+    )
+    attn_parts = [
+        lax.dynamic_slice_in_dim(w_value, first_head * HEAD_V, wide, 1),
+        lax.dynamic_slice_in_dim(w_query, first_head * QK_DIM, qk, 1),
+        lax.dynamic_slice_in_dim(w_key, first_head * QK_DIM, qk, 1),
+    ]
 
     lengths = lax.dynamic_slice_in_dim(doc_lengths[0], first_stream, streams, 0)
     starts = jnp.cumsum(lengths, axis=1) - lengths
@@ -432,18 +1274,9 @@
     begun = starts[:, None, :] <= position[None, :, None]
     first = jnp.max(jnp.where(begun, starts[:, None, :], 0), axis=2)[..., None]
 
-    mine = micro * span
+    x_own = tokens[0].reshape(mine, D)
+    flat = x_own.astype(jnp.float32)
     cot = cotangent[0].reshape(mine, D)
-    x_all = gather_plane(tokens[0].reshape(mine, D), 1)
-    out_full = gather_plane(attn_got[:, wide : wide + out_width], 2)
-    x_all = x_all.reshape(pieces, micro, span, D).transpose(1, 0, 2, 3)
-    x_all = lax.dynamic_slice_in_dim(x_all, first_stream, streams, 0)
-    x_all = x_all.astype(jnp.float32)
-    h_flat = (x_all * norm_scale(x_all) * gain_one).astype(LOW).reshape(streams * length, D)
-    value = dot(h_flat, value_full).astype(LOW).reshape(streams, length, wide)
-    query = dot(h_flat, query_full).astype(LOW).reshape(streams, length, qk)
-    key = dot(h_flat, key_full).astype(LOW).reshape(streams, length, qk)
-    att_heads = attend(query, key, value, first, heads)
 
     def to_tokens(by_head):
         sent = by_head.reshape(streams, pieces, span, wide).transpose(1, 0, 2, 3)
@@ -455,41 +1288,73 @@
         got = exchange_plane(sent.reshape(pieces, streams, span, wide), 4)
         return got.transpose(1, 0, 2, 3).reshape(streams, length, wide)
 
-    attended = to_tokens(att_heads)
-    flat = tokens[0].reshape(mine, D).astype(jnp.float32)
-    mid = flat + jnp.einsum(
-        "tk,skn->tsn", attended, out_full, preferred_element_type=jnp.float32
-    ).reshape(mine, D)
+    if fused:
+        attn_slice = jnp.concatenate(
+            attn_parts + [jnp.zeros((rows_dp, 128 - 2 * qk), LOW)], axis=1
+        )
+        gain_rows = jnp.concatenate(
+            [gain_attn[None], gain_mlp[None], jnp.zeros((14, rows_dp), LOW)], axis=0
+        )
+        front = layer_front(
+            x_own, cot, attn_slice, w_out, ffn_slice, w_down, gain_rows, first, wide, qk
+        )
+        out_full, h_all, query, key, value, att_heads, attended, mid = front[3:11]
+        attn_full, gains, out_part, g_h_two, d_ffn, d_down = front[11:]
+        h_flat = h_all.reshape(streams * length, D)
+        value_full = attn_full[:, :wide]
+        query_full = attn_full[:, wide : wide + qk]
+        key_full = attn_full[:, wide + qk : wide + 2 * qk]
+        gains = gains.astype(jnp.float32)
+        gain_one, gain_two = gains[0], gains[1]
+    else:
+
+        def gather_dp(w):
+            return lax.all_gather(w, "dp", axis=0, tiled=True)
+
+        attn_got = gather_dp(
+            jnp.concatenate(
+                attn_parts
+                + [
+                    lax.dynamic_slice_in_dim(w_out, place * out_width, out_width, 1),
+                    gain_attn[:, None],
+                    gain_mlp[:, None],
+                ],
+                axis=1,
+            )
+        )
+        ffn_full = gather_dp(ffn_slice)
+        down_full = gather_dp(lax.dynamic_slice_in_dim(w_down, place * share, share, 0))
+        value_full = attn_got[:, :wide]
+        query_full = attn_got[:, wide : wide + qk]
+        key_full = attn_got[:, wide + qk : wide + 2 * qk]
+        out_full = gather_plane(attn_got[:, wide + 2 * qk : wide + 2 * qk + out_width], 2)
+        gains = attn_got[:, wide + 2 * qk + out_width :].astype(jnp.float32)
+        gain_one, gain_two = gains[:, 0], gains[:, 1]
+        x_all = gather_plane(x_own, 1).reshape(pieces, micro, span, D).transpose(1, 0, 2, 3)
+        x_all = lax.dynamic_slice_in_dim(x_all, first_stream, streams, 0).astype(jnp.float32)
+        h_flat = (x_all * norm_scale(x_all) * gain_one).astype(LOW).reshape(streams * length, D)
+        value = dot(h_flat, value_full).astype(LOW).reshape(streams, length, wide)
+        query = dot(h_flat, query_full).astype(LOW).reshape(streams, length, qk)
+        key = dot(h_flat, key_full).astype(LOW).reshape(streams, length, qk)
+        att_heads = attend(query, key, value, first, heads)
+        attended = to_tokens(att_heads)
+        mid = flat + jnp.einsum(
+            "tk,skn->tsn", attended, out_full, preferred_element_type=jnp.float32
+        ).reshape(mine, D)
+        h_two = (mid * norm_scale(mid) * gain_two).astype(LOW)
+        out_part, g_h_two, d_gate, d_up, d_down = ffn_lax(
+            h_two, gather_plane(cot, 6), ffn_full[:, :hidden], ffn_full[:, hidden:], down_full
+        )
+        d_ffn = jnp.concatenate([d_gate, d_up], axis=1)
+
     inverse_two = norm_scale(mid)
     plain_two = mid * inverse_two
-    h_two = (plain_two * gain_two).astype(LOW)
-
-    h_two_all = gather_plane(h_two, 5).reshape(-1, D)
-    cot_all = gather_plane(cot, 6).reshape(-1, D)
-    gate = dot(h_two_all, gate_full)
-    up = dot(h_two_all, up_full)
-    g_act = contract(cot_all, down_full, 1, 1)
-    sigmoid = jax.nn.sigmoid(gate)
-    silu = gate * sigmoid
-    act = (silu * up).astype(LOW)
-    g_gate = (g_act * up * sigmoid * (1.0 + gate * (1.0 - sigmoid))).astype(LOW)
-    g_up = (g_act * silu).astype(LOW)
-    g_h_two_part = (contract(g_gate, gate_full, 1, 1) + contract(g_up, up_full, 1, 1)).astype(LOW)
-    g_h_two = scatter_plane(g_h_two_part.reshape(pieces, mine, D), 7)
-    grad_down = lax.psum_scatter(
-        contract(act, cot_all, 0, 0).astype(LOW), "dp", scatter_dimension=0, tiled=True
-    ).astype(jnp.float32)
-    grad_ffn = lax.psum_scatter(
-        jnp.concatenate(
-            [contract(h_two_all, g_gate, 0, 0).astype(LOW), contract(h_two_all, g_up, 0, 0).astype(LOW)],
-            axis=1,
-        ),
-        "dp",
-        scatter_dimension=0,
-        tiled=True,
-    )
-    out_part = dot(act, down_full).astype(LOW)
-    output = (mid + scatter_plane(out_part.reshape(pieces, mine, D), 8)).astype(LOW)
+
+    def scatter_dp(part):
+        return lax.psum_scatter(part, "dp", scatter_dimension=0, tiled=True)
+
+    sum_ffn, sum_down = scatter_dp(d_ffn), scatter_dp(d_down)
+    output = (mid + scatter_plane(out_part, 8)).astype(LOW)
 
     g_mid = cot.astype(jnp.float32) + norm_backward(g_h_two, plain_two, inverse_two, gain_two)
     g_mid_low = g_mid.astype(LOW)
@@ -522,7 +1387,8 @@
     grad_out = contract(attended, g_mid_low, 0, 0).astype(LOW)
     grad_out = grad_out.reshape(groups, pieces, own, D).transpose(1, 0, 2, 3)
     grad_out = scatter_plane(grad_out.reshape(pieces, groups * own, D), 10).astype(LOW)
-    grad_out = lax.psum_scatter(grad_out, "dp", scatter_dimension=0, tiled=True)
+    grad_out, sum_ffn, sum_down = lax.optimization_barrier((grad_out, sum_ffn, sum_down))
+    grad_out = scatter_dp(grad_out)
     grad_attn = jnp.concatenate(
         [
             contract(h_flat, g_value, 0, 0).astype(LOW),
@@ -533,8 +1399,9 @@
         ],
         axis=1,
     )
-    grad_attn = lax.psum_scatter(grad_attn, "dp", scatter_dimension=0, tiled=True)
-    ffn_got = exchange_plane(grad_ffn.reshape(pieces, own, 2 * hidden), 11).astype(jnp.float32)
+    grad_attn, grad_out = lax.optimization_barrier((grad_attn, grad_out))
+    grad_attn = scatter_dp(grad_attn)
+    ffn_got = exchange_plane(sum_ffn.reshape(pieces, own, 2 * hidden), 11).astype(jnp.float32)
     attn_got = exchange_plane(grad_attn.reshape(pieces, own, -1), 12).astype(jnp.float32)
     grad_gains = jnp.sum(attn_got[:, :, wide + 2 * qk :], axis=0)
     attn_got = jnp.sum(attn_got.reshape(pieces // sharers, sharers, own, -1), axis=1)
@@ -542,8 +1409,15 @@
     def by_rows(block):
         return block.transpose(1, 0, 2).reshape(own, -1)
 
-    def by_hidden(block):
-        return block.reshape(pieces, own, groups, share).transpose(1, 2, 0, 3).reshape(own, FF)
+    def by_hidden(second):
+        parts, start = [], 0
+        for count in chunks:
+            begin = start + second * groups * count
+            part = ffn_got[:, :, begin : begin + groups * count]
+            parts.append(part.reshape(pieces, own, groups, count))
+            start += 2 * groups * count
+        whole = jnp.concatenate(parts, axis=3)
+        return whole.transpose(1, 2, 0, 3).reshape(own, FF)
 
     return (
         output.reshape(tokens.shape),
@@ -552,9 +1426,9 @@
         by_rows(attn_got[:, :, wide + qk : wide + 2 * qk]),
         by_rows(attn_got[:, :, :wide]),
         grad_out.astype(jnp.float32),
-        by_hidden(ffn_got[:, :, :hidden]),
-        by_hidden(ffn_got[:, :, hidden:]),
-        grad_down,
+        by_hidden(0),
+        by_hidden(1),
+        sum_down.astype(jnp.float32),
         grad_gains[:, 0],
         grad_gains[:, 1],
     )

time: 845 us -> 684 us (0.81)
  matrix products: 175 us -> 58 us
  waiting for transfers between devices: 90.6 us -> 4.33 us
  Pallas kernels: 413 us -> 495 us
  other arithmetic: 41.5 us -> 15.4 us
  local copies, waits for them, and re-layouts: 101 us -> 84.1 us
    pallas_call x5 -> x1, Pallas kernels: 172 us -> 308 us  [layer_front(): pl.pallas_call(layer_kernel, out_shape=out_shape, in_specs=[anywhere] * 7...]
    reduce_scatter x4, waiting for transfers between devices: 90.5 us -> 3.59 us  [scatter_dp(): return lax.psum_scatter(part, 'dp', scatter_dimension=0, tiled=True)]
    dot_general x13 -> x7, matrix products: 120 us -> 52.3 us  [contract(): lax.dot_general(left, right, (((left_dim,), (right_dim,)), ((), ())), pre...]
    dot_general x7 -> x0, matrix products: 52.7 us -> none  [the longest x6 46.4 us: dot(): return jnp.dot(left, right, preferred_element_type=jnp.float32)]
    pallas_call x4 -> x3, Pallas kernels: 159 us -> 119 us  [scatter_plane(): pl.pallas_call(scatter_kernel, out_shape=jax.ShapeDtypeStruct((rows, colu...]
    convert_element_type x5 -> x1, other arithmetic: 21.2 us -> 1.26 us  [local(): sum_down.astype(jnp.float32)]
    pallas_call x4 -> x3, Pallas kernels: 57.7 us -> 42.5 us  [exchange_plane(): pl.pallas_call(exchange_kernel, out_shape=jax.ShapeDtypeStruct(x.shape, x...]
    dot_general x1 -> x0, local copies, waits for them, and re-layouts: 11.7 us -> none  [local(): jnp.einsum('tk,skn->tsn', attended, out_full, preferred_element_type=jnp....]
  transfers between devices with their start and end apart: 7 -> 4, of which waited for: 1 -> 1; matrix products, arithmetic and copies ran while one was open for 26% -> 18% of each run, Pallas kernels for 33% -> 27%
where the time goes in v5:
time: 684 us; the launch traced here: 672 us
  Pallas kernels  495 us (72%)
  local copies, waits for them, and re-layouts  84.1 us (12%)
  matrix products  58 us (8%)
  other arithmetic  15.4 us (2%)
  between operations  14.8 us (2%)
    pallas_call x1, Pallas kernels, layer_front(): pl.pallas_call(layer_kernel, out_shape=out_shape, in_specs=[anywhere] * 7...  308 us
    pallas_call x3, Pallas kernels, scatter_plane(): pl.pallas_call(scatter_kernel, out_shape=jax.ShapeDtypeStruct((rows, colu...  119 us
    dot_general x7, matrix products, contract(): lax.dot_general(left, right, (((left_dim,), (right_dim,)), ((), ())), pre...  52.3 us
    pallas_call x3, Pallas kernels, exchange_plane(): pl.pallas_call(exchange_kernel, out_shape=jax.ShapeDtypeStruct(x.shape, x...  42.5 us
    pallas_call x1, Pallas kernels, attend_back(): pl.pallas_call(functools.partial(attend_back_kernel, heads), grid=(stream...  24.8 us
    unnamed x52, local copies, waits for them, and re-layouts  14.4 us
  transfers between devices with their start and end apart: 4, of which 1 were waited for; matrix products, arithmetic and copies ran while one was open for 18% of the time, Pallas kernels for 27%

profile of v5, /device:TPU:1, one launch (start us, length us, event | category | flops | bytes accessed | tf_op | source)
XLA Modules:
  0.0 671.8 jit_solution(3854084240240619325)
XLA Ops:
  7.2 0.9 reduce_window_sum.14
  8.9 1.3 copy.99.first_ref
  10.2 0.7 broadcast_in_dim.21
  11.8 1.0 constant_dynamic-slice_fusion.26
  12.7 1.1 constant_dynamic-slice_fusion.24
  14.5 3.1 constant_dynamic-slice_fusion
  17.6 1.9 constant_dynamic-slice_fusion.16
  19.6 0.9 maximum_maximum_fusion.wa_ref
  20.4 6.1 concatenate.19.wgu_ref
  26.5 308.4 %layer.1 = (bf16[8,256,2048]{2,1,0:T(8,128)(2,1)}, bf16[8,256,2048]{2,1,0:T(8,128)(2,1)}, bf16[8,256,2048]{2,1,0:T(8,128)(2,1)}, bf16[8,2048,256]{2,1,0:T(8,128)...) custom-call(bf16[256,2048]{1,0:T(8,128)(2,1)} %bitcast.98, ...), custom_call_target="tpu_custom_call" | custom-call | flops 53150220288 | bytes 209715200 | tf_op jit(solution)/shard_map/layer/pallas_call | solution.py:1130
  335.0 0.7 reduce-scatter.5.cloned.1.call-update
  335.8 0.8 copy-done.3
  336.8 0.9 fusion.14
  337.7 0.7 multiply_reduce_fusion
  338.9 0.7 fusion.11
  339.6 0.7 copy-done.17
  340.4 5.6 convolution_convert_fusion
  346.0 8.3 %copy.108 = bf16[4,8,64,2048]{3,2,0,1:T(8,128)(2,1)} copy(bf16[4,8,64,2048]{3,2,1,0:T(8,128)(2,1)} %bitcast.96) | data formatting | bytes 16777216 | tf_op jit(solution)/shard_map/reshape | solution.py:1388
  354.3 3.4 copy-done
  357.6 40.5 %scatter.5 = f32[256,2048]{1,0:T(8,128)S(1)} custom-call(bf16[8,256,2048]{2,1,0:T(8,128)(2,1)S(1)} %bitcast.92), custom_call_target="tpu_custom_call" | custom-call | bytes 83886080 | tf_op jit(solution)/shard_map/scatter/pallas_call | solution.py:299
  398.1 1.1 convert_element_type.93
  399.2 5.7 fusion
  405.3 1.2 copy.132
  406.5 15.2 %exchange.3 = bf16[8,2,128,256]{3,2,1,0:T(8,128)(2,1)} custom-call(bf16[8,2,128,256]{3,2,1,0:T(8,128)(2,1)} %bitcast.103), custom_call_target="tpu_custom_call" | custom-call | bytes 20971520 | tf_op jit(solution)/shard_map/exchange/pallas_call | solution.py:341
  421.6 2.3 copy.102
  423.9 24.8 %attend_back.1 = (bf16[2,1024,32]{2,1,0:T(8,128)(2,1)}, bf16[2,1024,32]{2,1,0:T(8,128)(2,1)}, bf16[2,1024,256]{2,1,0:T(8,128)(2,1)}) custom-call(bf16[2,1024,32]{2,1,0:T(8,128)(2,1)} %get-tuple-element.37.q_ref, bf16[2,1024,32]{2,1,0:T(8,128)(2,1)} %get-tuple-element.38.k_ref, bf16[2,1024,256]{2,1,0:T(8,128)(2,1)} %get-tuple-element.39.v_ref, ...), custom_call_target="tpu_custom_call" | custom-call | tf_op jit(solution)/shard_map/attend_back/pallas_call | solution.py:122
  448.7 9.2 %fusion.9 = f32[2048,2048]{1,0:T(8,128)} fusion(bf16[2048,32]{1,0:T(8,128)(2,1)} %bitcast.107, bf16[2048,384]{1,0:T(8,128)(2,1)S(1)} %copy-done.11), kind=kOutput, calls=%fused_computation.29 | convolution fusion | flops 268435456 | bytes 17432576 | tf_op jit(solution)/shard_map/dot_general | solution.py:25
  457.9 8.1 %fusion.6 = f32[2048,2048]{1,0:T(8,128)} fusion(bf16[2048,256]{1,0:T(8,128)(2,1)S(1)} %bitcast.113, bf16[2048,384]{1,0:T(8,128)(2,1)S(1)} %copy-done.11), kind=kOutput, calls=%fused_computation.25 | convolution fusion | flops 2147483648 | bytes 18874368 | tf_op jit(solution)/shard_map/dot_general | solution.py:25
  466.0 15.8 %add_convert_fusion = bf16[2048,2048]{1,0:T(8,128)(2,1)} fusion(f32[2048,2048]{1,0:T(8,128)} %fusion.6, f32[2048,2048]{1,0:T(8,128)} %fusion.9, bf16[2048,32]{1,0:T(8,128)(2,1)S(1)} %bitcast.108, bf16[2048,384]{1,0:T(8,128)(2,1)S(1)} %copy-done.11), kind=kOutput, calls=%fused_computation | convolution fusion | flops 281018368 | bytes 42991616 | tf_op jit(solution)/shard_map/dot_general | solution.py:25
  481.8 8.3 %copy.104 = bf16[2,8,128,2048]{3,2,0,1:T(8,128)(2,1)} copy(bf16[2,8,128,2048]{3,2,1,0:T(8,128)(2,1)} %bitcast.97) | data formatting | bytes 16777216 | tf_op jit(solution)/shard_map/reshape | solution.py:1377
  490.1 3.4 copy-done.1
  493.5 38.4 %scatter.4 = f32[256,2048]{1,0:T(8,128)S(1)} custom-call(bf16[8,256,2048]{2,1,0:T(8,128)(2,1)S(1)} %bitcast.93), custom_call_target="tpu_custom_call" | custom-call | bytes 83886080 | tf_op jit(solution)/shard_map/scatter/pallas_call | solution.py:299
  533.3 5.1 fusion.3
  538.5 5.1 fusion.2
  543.6 3.3 fusion.1
  547.0 7.1 %concatenate.21 = bf16[2048,322]{0,1:T(8,128)(2,1)} concatenate(bf16[2048,256]{0,1:T(8,128)(2,1)} %fusion.1, bf16[2048,32]{0,1:T(8,128)(2,1)S(1)} %fusion.2, bf16[2048,32]{0,1:T(8,128)(2,1)S(1)} %fusion.3, bf16[2048,1]{0,1:T(2,128)(2,1)S(1)} %convert_element_type.89, bf16[2048,1]{0,1:T(2,128)(2,1)S(1)} %convert_element_type.91), dimensions={1} | concatenate | bytes 2637824 | tf_op jit(solution)/shard_map/concatenate | solution.py:1392
  554.1 3.6 reduce-scatter.9.cloned.1.call-done
  557.7 3.4 copy-done.2
  561.0 40.6 %scatter.3 = f32[256,2048]{1,0:T(8,128)S(1)} custom-call(bf16[8,256,2048]{2,1,0:T(8,128)(2,1)S(1)} %copy-done.2), custom_call_target="tpu_custom_call" | custom-call | bytes 83886080 | tf_op jit(solution)/shard_map/scatter/pallas_call | solution.py:299
  601.7 2.9 multiply_add_fusion
  604.6 19.3 %exchange.5 = bf16[8,64,1408]{2,1,0:T(8,128)(2,1)} custom-call(bf16[8,64,1408]{2,1,0:T(8,128)(2,1)} %bitcast.111), custom_call_target="tpu_custom_call" | custom-call | bytes 28835840 | tf_op jit(solution)/shard_map/exchange/pallas_call | solution.py:341
  623.9 2.4 fusion.12
  626.8 1.5 reshape.184
  628.3 1.1 fusion.13
  629.4 2.2 copy.116
  631.6 1.5 copy.117
  633.1 1.1 maximum_bitcast_fusion.1
  634.2 1.2 copy.118
  635.5 2.7 reshape.186
  638.6 1.5 reshape.180
  640.1 1.2 copy.113
  641.2 1.5 copy.114
  642.8 1.1 maximum_bitcast_fusion
  643.9 1.5 copy.115
  645.5 2.7 reshape.182
  648.1 1.3 convert_element_type.97
  649.4 0.8 convert_element_type.95
  650.2 1.9 copy.109
  652.1 8.0 %exchange.4 = bf16[8,64,322]{2,1,0:T(8,128)(2,1)} custom-call(bf16[8,64,322]{2,1,0:T(8,128)(2,1)} %bitcast.110), custom_call_target="tpu_custom_call" | custom-call | bytes 6594560 | tf_op jit(solution)/shard_map/exchange/pallas_call | solution.py:341
  660.1 1.1 convert_element_type.94
  661.5 0.8 copy.125
  662.5 0.7 copy.119
  663.3 0.7 copy.120
  664.0 0.7 slice_reduce_fusion.1
  (79 shorter events, 6.5 us)
Async XLA Ops:
  7.2 525.0 %reduce-scatter.7.cloned.1.call-start = ((), (), s32[]{:S(2)}) async-start(), calls=%async_computation.5 | async-start | bytes 3604480 | tf_op jit(solution)/shard_map/reduce_scatter | solution.py:1354
  335.0 197.2 %reduce-scatter.5.cloned.1.call-start = ((), (), s32[]{:S(2)}) async-start(), calls=%async_computation.4 | async-start | bytes 7208960 | tf_op jit(solution)/shard_map/reduce_scatter | solution.py:1354
  335.0 1.6 copy-start.3
  335.7 221.9 %reduce-scatter.9.cloned.1.call-start = ((), (), s32[]{:S(2)}) async-start(), calls=%async_computation.6 | async-start | bytes 1310720 | tf_op jit(solution)/shard_map/reduce_scatter | solution.py:1354
  335.8 1.9 copy-start.5
  337.7 1.2 copy-start.9
  338.9 1.4 copy-start.17
  354.3 3.4 copy-start
  423.9 24.8 %copy-start.11 = (bf16[2048,384]{1,0:T(8,128)(2,1)S(1)}, bf16[2048,384]{1,0:T(8,128)(2,1)}, u32[]{:S(2)}) copy-start(bf16[2048,384]{1,0:T(8,128)(2,1)} %get-tuple-element.43) | copy-start | bytes 4718596
  448.7 9.2 %copy-start.18 = (bf16[2,1024,256]{2,1,0:T(8,128)(2,1)S(1)}, bf16[2,1024,256]{2,1,0:T(8,128)(2,1)}, u32[]{:S(2)}) copy-start(bf16[2,1024,256]{2,1,0:T(8,128)(2,1)} %get-tuple-element.42) | copy-start | bytes 3145732
  457.9 8.1 %copy-start.13 = (bf16[2,1024,32]{2,1,0:T(8,128)(2,1)S(1)}, bf16[2,1024,32]{2,1,0:T(8,128)(2,1)}, u32[]{:S(2)}) copy-start(bf16[2,1024,32]{2,1,0:T(8,128)(2,1)} %get-tuple-element.45) | copy-start | bytes 393220
  490.1 3.4 copy-start.1
  493.5 38.4 %copy-start.8 = (bf16[1,2,128,2048]{3,2,1,0:T(8,128)(2,1)S(1)}, bf16[1,2,128,2048]{3,2,1,0:T(8,128)(2,1)}, u32[]{:S(2)}) copy-start(bf16[1,2,128,2048]{3,2,1,0:T(8,128)(2,1)} %param.12) | copy-start | bytes 3145732
  532.2 118.0 %reduce-scatter.11.cloned.1.call-start = ((), (), s32[]{:S(2)}) async-start(), calls=%async_computation.7 | async-start | bytes 1679360 | tf_op jit(solution)/shard_map/reduce_scatter | solution.py:1354
  532.3 1.0 copy-start.14
  533.3 5.1 copy-start.12
  533.3 10.2 %slice-start = ((s8[8388608]{0:T(1024)(128)(4,1)}), s8[4194304]{0:T(1024)(128)(4,1)S(1)}, s32[]{:S(2)}) async-start(s8[8388608]{0:T(1024)(128)(4,1)} %bitcast.94), calls=%async_computation.8 | async-start | bytes 8388608
  538.4 5.1 slice-start.1
  538.5 5.1 copy-start.19
  557.7 3.4 copy-start.2
  561.0 40.6 %copy-start.4 = (f32[256,2048]{1,0:T(8,128)S(1)}, f32[256,2048]{1,0:T(8,128)}, u32[]{:S(2)}) copy-start(f32[256,2048]{1,0:T(8,128)} %get-tuple-element.33) | copy-start | bytes 6291460
  561.0 40.6 %copy-start.6 = (f32[256,2048]{1,0:T(8,128)S(1)}, f32[256,2048]{1,0:T(8,128)}, u32[]{:S(2)}) copy-start(f32[256,2048]{1,0:T(8,128)} %get-tuple-element.35) | copy-start | bytes 6291460
  561.0 40.6 %copy-start.10 = (bf16[1,2,128,2048]{3,2,1,0:T(8,128)(2,1)S(1)}, bf16[1,2,128,2048]{3,2,1,0:T(8,128)(2,1)}, u32[]{:S(2)}) copy-start(bf16[1,2,128,2048]{3,2,1,0:T(8,128)(2,1)} %param.23) | copy-start | bytes 3145732
  626.3 1.9 copy-start.7
  635.5 2.7 copy-start.16
  638.1 1.9 copy-start.15
  645.5 2.7 copy-start.20
  645.5 3.9 copy-start.21
Sparse Core Ops, SparseCore 0:
  335.1 53.6 reduce-scatter.6
  391.1 102.3 reduce-scatter.4
  532.4 25.2 reduce-scatter.8
  559.9 30.3 reduce-scatter.10

commit v6 on v5

--- a/solution.py
+++ b/solution.py
@@ -1184,6 +1184,502 @@
     )(tokens, cot, attn_slice, w_out, ffn_slice, w_down, gain_rows, first)
 
 
+class PlaneScatter:
+    def __init__(self, beside, held, got, one, two, send, recv):
+        me, sib, xn, yn = partners()
+        half = got.shape[1] // 2
+        self.half = half
+        upper, lower = pl.ds(0, half), pl.ds(half, half)
+        copy = functools.partial(remote, send, recv)
+        self.held, self.got, self.one, self.two = held, got, one, two
+        self.pairs = [copy(i, beside(i), got.at[i], sib) for i in range(4)]
+        self.x0 = copy(4, held(2).at[upper], one.at[0], xn)
+        self.y0 = copy(5, held(2).at[lower], one.at[1], yn)
+        self.x1 = copy(6, held(1).at[upper], one.at[2], xn)
+        self.y1 = copy(7, held(3).at[lower], one.at[3], yn)
+        self.y2 = copy(8, held(3).at[upper], two.at[0], yn)
+        self.x2 = copy(9, held(1).at[lower], two.at[1], xn)
+
+    def start_pair(self, i):
+        self.pairs[i].start()
+
+    def start_pairs(self):
+        for i in (2, 1, 3, 0):
+            self.start_pair(i)
+
+    def add_pair(self, i):
+        self.pairs[i].wait_recv()
+        block = self.held(i)
+        block[...] = block[...] + self.got[i]
+        for c in {0: (), 1: (self.x1,), 2: (self.x0, self.y0), 3: (self.y1,)}[i]:
+            c.start()
+
+    def add_pairs(self):
+        for i in (2, 1, 3, 0):
+            self.add_pair(i)
+
+    def second(self):
+        half = self.half
+        self.y0.wait_recv()
+        block = self.held(1)
+        block[half:, :] = block[half:, :] + self.one[1]
+        self.x2.start()
+        self.x0.wait_recv()
+        block = self.held(3)
+        block[:half, :] = block[:half, :] + self.one[0]
+        self.y2.start()
+
+    def upper_sum(self):
+        f32 = jnp.float32
+        self.x1.wait_recv()
+        self.y2.wait_recv()
+        own = self.held(0)[: self.half, :].astype(f32)
+        return own + self.one[2].astype(f32) + self.two[0].astype(f32)
+
+    def lower_sum(self):
+        f32 = jnp.float32
+        self.y1.wait_recv()
+        self.x2.wait_recv()
+        own = self.held(0)[self.half :, :].astype(f32)
+        return own + self.one[3].astype(f32) + self.two[1].astype(f32)
+
+    def sent(self):
+        for c in (*self.pairs, self.x0, self.y0, self.x1, self.y1, self.y2, self.x2):
+            c.wait_send()
+
+
+def chips():
+    me, unused, xn, yn = partners()
+    return me, xn, xn + yn - me, yn
+
+
+def turn_kernel(
+    gh_ref,
+    mid_ref,
+    c_ref,
+    gain_ref,
+    wo_all,
+    part_ref,
+    tok_ref,
+    q_ref,
+    k_ref,
+    v_ref,
+    att_ref,
+    first_ref,
+    output_ref,
+    g_mid_out,
+    g_out,
+    go_out,
+    gain_out,
+    g_mid,
+    work,
+    g_low,
+    g_att,
+    g_heads,
+    g_s,
+    w_buf,
+    go_part,
+    held_o,
+    got_g,
+    one_g,
+    two_g,
+    got_o,
+    one_o,
+    two_o,
+    gk_sum,
+    gv_sum,
+    esend,
+    erecv,
+    ssend,
+    srecv,
+    load_sem,
+    w_sem,
+    self_sem,
+    done_sem,
+):
+    me, sib, xn, yn = partners()
+    flip = sib - me
+    rows, width = g_low.shape
+    span = rows // 2
+    wide, qk = v_ref.shape[2], q_ref.shape[2]
+    half = rows // 2
+    greet([lax.rem(me + i, 8) for i in range(1, 8)])
+    owners = chips()
+
+    loads = [
+        pltpu.make_async_copy(source, target, load_sem.at[i])
+        for i, (source, target) in enumerate(
+            ((gh_ref, g_mid), (mid_ref, work), (c_ref, g_low))
+        )
+    ]
+    held_loads = [
+        pltpu.make_async_copy(part_ref.at[owners[i]], held_o.at[i], load_sem.at[3 + i])
+        for i in range(4)
+    ]
+
+    def w_load(step):
+        slot = lax.rem(step, 2)
+        return pltpu.make_async_copy(wo_all.at[step], w_buf.at[slot], w_sem.at[slot])
+
+    for c in loads:
+        c.start()
+    w_load(0).start()
+    outs = PlaneScatter(
+        lambda i: part_ref.at[owners[i] + flip],
+        lambda i: held_o.at[i],
+        got_o,
+        one_o,
+        two_o,
+        ssend.at[0],
+        srecv.at[0],
+    )
+    weights = PlaneScatter(
+        lambda i: go_part.at[owners[i] + flip],
+        lambda i: go_part.at[owners[i]],
+        got_g,
+        one_g,
+        two_g,
+        ssend.at[1],
+        srecv.at[1],
+    )
+    outs.start_pairs()
+    for c in held_loads:
+        c.start()
+    for c in loads:
+        c.wait()
+
+    f32 = jnp.float32
+    mid = work[...]
+    inverse = norm_scale(mid)
+    normed = mid * inverse
+    grad = g_mid[...]
+    gain_out[...] = jnp.broadcast_to(
+        jnp.sum(grad * normed, axis=0, keepdims=True), gain_out.shape
+    )
+    gain = gain_ref[1:2, :].astype(f32)
+    grad_mid = g_low[...].astype(f32) + norm_backward(grad, normed, inverse, gain)
+    g_mid[...] = grad_mid
+    g_low[...] = grad_mid.astype(LOW)
+    done = [pltpu.make_async_copy(g_mid, g_mid_out, done_sem.at[0])]
+    done[0].start()
+
+    def back_out(step, carry):
+        slot = lax.rem(step, 2)
+        w_load(step).wait()
+
+        @pl.when(step < 7)
+        def _():
+            w_load(step + 1).start()
+
+        there = pl.ds(pl.multiple_of(step * wide, 128), wide)
+        term = contract(g_low[:, there], w_buf[slot], 1, 1)
+
+        @pl.when(step == 0)
+        def _():
+            work[...] = term
+
+        @pl.when(step > 0)
+        def _():
+            work[...] += term
+
+        return carry
+
+    lax.fori_loop(0, 8, back_out, 0)
+    g_att[...] = work[...].astype(LOW)
+    mid_load = pltpu.make_async_copy(mid_ref, work, load_sem.at[1])
+    mid_load.start()
+    swaps = []
+    here = pl.ds(me * span, span)
+    for i in range(1, 8):
+        other = lax.rem(me + i, 8)
+        lanes = pl.ds(pl.multiple_of(other * wide, 128), wide)
+        for m in range(2):
+            swaps.append(
+                remote(
+                    esend,
+                    erecv,
+                    2 * (i - 1) + m,
+                    g_att.at[pl.ds(m * span, span), lanes],
+                    g_heads.at[m, here],
+                    other,
+                )
+            )
+            swaps[-1].start()
+    kept = [
+        pltpu.make_async_copy(
+            g_att.at[pl.ds(m * span, span), pl.ds(pl.multiple_of(me * wide, 128), wide)],
+            g_heads.at[m, here],
+            self_sem.at[m],
+        )
+        for m in range(2)
+    ]
+    for c in kept:
+        c.start()
+
+    own = width // 32
+    for z in range(4):
+        lanes = slice(z * 8 * own, (z + 1) * 8 * own)
+        block = contract(tok_ref[:, lanes], g_low[...], 0, 0).astype(LOW)
+        for s in range(8):
+            go_part[s, z * own : (z + 1) * own, :] = block[s * own : (s + 1) * own]
+    weights.start_pairs()
+    for c in kept:
+        c.wait()
+    for c in swaps:
+        c.wait_recv()
+    weights.add_pairs()
+
+    length = v_ref.shape[1]
+    block = 256
+
+    def back_stream(m, carry):
+        gk_sum[...] = jnp.zeros_like(gk_sum)
+        gv_sum[...] = jnp.zeros_like(gv_sum)
+        for i in range(length // block):
+            rows_i = slice(i * block, (i + 1) * block)
+            seen = (i + 1) * block
+            query, key = q_ref[m, rows_i, :], k_ref[m, :seen, :]
+            g_query = jnp.zeros(query.shape, f32)
+            for head in range(wide // HEAD_V):
+                lanes = slice(head * HEAD_V, (head + 1) * HEAD_V)
+                scores, mask, weight = weights_of(
+                    query, key, head, first_ref[m, rows_i, :], i * block
+                )
+                denom = jnp.sum(weight, axis=1, keepdims=True)
+                a = (g_heads[m, rows_i, lanes].astype(f32) / denom).astype(LOW)
+                b = -jnp.sum(
+                    a.astype(f32) * att_ref[m, rows_i, lanes].astype(f32), axis=1, keepdims=True
+                )
+                g_weight = contract(a, v_ref[m, :seen, lanes], 1, 1) + b
+                slope = 1.0 / math.sqrt(QK_DIM) + scores * (1.0 / QK_DIM)
+                g_scores = jnp.where(mask, g_weight * slope, 0.0).astype(LOW)
+                g_query += head_lanes(dot(g_scores, key), head)
+                gk_sum[:seen, :] += contract(g_scores, head_lanes(query, head), 0, 0)
+                gv_sum[:seen, lanes] += contract(weight.astype(LOW), a, 0, 0)
+            g_s[m, rows_i, wide : wide + qk] = g_query.astype(LOW)
+        g_s[m, :, :wide] = gv_sum[...].astype(LOW)
+        g_s[m, :, wide + qk : wide + 2 * qk] = gk_sum[...].astype(LOW)
+        g_s[m, :, wide + 2 * qk :] = jnp.zeros((length, g_s.shape[2] - wide - 2 * qk), LOW)
+
+        @pl.when(m == 0)
+        def _():
+            for c in held_loads:
+                c.wait()
+            outs.add_pairs()
+
+        return carry
+
+    lax.fori_loop(0, 2, back_stream, 0)
+    weights.second()
+    done.append(pltpu.make_async_copy(g_s, g_out, done_sem.at[1]))
+    done[1].start()
+    mid_load.wait()
+    outs.second()
+    go_out[:half] = weights.upper_sum().astype(LOW)
+    go_out[half:] = weights.lower_sum().astype(LOW)
+    output_ref[:half] = (work[:half] + outs.upper_sum()).astype(LOW)
+    output_ref[half:] = (work[half:] + outs.lower_sum()).astype(LOW)
+    for c in done:
+        c.wait()
+    for c in swaps:
+        c.wait_send()
+    weights.sent()
+    outs.sent()
+
+
+def layer_turn(gh, mid, cot, gains, wo_all, part, tok, query, key, value, att, first, columns):
+    rows, width = mid.shape
+    streams, length, wide = value.shape
+    qk = query.shape[2]
+    shape = jax.ShapeDtypeStruct
+    f32 = jnp.float32
+    anywhere = pl.BlockSpec(memory_space=pl.ANY)
+    in_vmem = pl.BlockSpec(memory_space=pltpu.VMEM)
+    dma = pltpu.SemaphoreType.DMA
+    vmem = pltpu.VMEM
+    arriving = [
+        vmem((4, rows, width), LOW),
+        vmem((4, rows // 2, width), LOW),
+        vmem((2, rows // 2, width), LOW),
+    ]
+    return pl.pallas_call(
+        turn_kernel,
+        out_shape=[
+            shape((rows, width), LOW),
+            shape((rows, width), f32),
+            shape((streams, length, columns), LOW),
+            shape((rows, width), LOW),
+            shape((8, width), f32),
+        ],
+        in_specs=[anywhere] * 3 + [in_vmem] + [anywhere] * 2 + [in_vmem] * 6,
+        out_specs=[in_vmem, anywhere, anywhere, in_vmem, in_vmem],
+        scratch_shapes=[
+            vmem((rows, width), f32),
+            vmem((rows, width), f32),
+            vmem((rows, width), LOW),
+            vmem((rows, width), LOW),
+            vmem((streams, length, wide), LOW),
+            vmem((streams, length, columns), LOW),
+            vmem((2, width, wide), LOW),
+            vmem((8, rows, width), LOW),
+            vmem((4, rows, width), LOW),
+            *arriving,
+            *arriving,
+            vmem((length, qk), f32),
+            vmem((length, wide), f32),
+            dma((14,)),
+            dma((14,)),
+            dma((2, 10)),
+            dma((2, 10)),
+            dma((7,)),
+            dma((2,)),
+            dma((2,)),
+            dma((2,)),
+        ],
+        compiler_params=pltpu.CompilerParams(
+            collective_id=22, has_side_effects=True, vmem_limit_bytes=63 * MIB
+        ),
+        cost_estimate=moved(16 * rows * width),
+        name="turn",
+    )(gh, mid, cot, gains, wo_all, part, tok, query, key, value, att, first)
+
+
+def close_kernel(
+    g_ref,
+    wa_ref,
+    h1_ref,
+    g_mid_ref,
+    x_ref,
+    gain_ref,
+    sum_ref,
+    grad_ref,
+    attn_ref,
+    beside,
+    held,
+    got,
+    one,
+    two,
+    h_buf,
+    sums,
+    ssend,
+    srecv,
+    h_sem,
+):
+    me, sib, xn, yn = partners()
+    rows, width = x_ref.shape
+    span = rows // 2
+    half = rows // 2
+    f32 = jnp.float32
+    greet((sib, xn, yn))
+    scatter = PlaneScatter(
+        lambda i: beside.at[i], lambda i: held.at[i], got, one, two, ssend, srecv
+    )
+    streams, length, columns = g_ref.shape
+    pieces = length // rows
+
+    def h_load(step):
+        slot = lax.rem(step, 2)
+        return pltpu.make_async_copy(
+            h1_ref.at[step // pieces, pl.ds(lax.rem(step, pieces) * rows, rows)],
+            h_buf.at[slot],
+            h_sem.at[slot],
+        )
+
+    h_load(0).start()
+
+    def part_of(owner):
+        there = pl.ds(pl.multiple_of(owner * span, span), span)
+        grads = jnp.concatenate([g_ref[0, there, :], g_ref[1, there, :]], axis=0)
+        return contract(grads, wa_ref[...], 1, 1).astype(LOW)
+
+    owners = chips()
+    for i in (2, 1, 3, 0):
+        beside[i] = part_of(owners[i] + sib - me)
+        scatter.start_pair(i)
+        held[i] = part_of(owners[i])
+        scatter.add_pair(i)
+
+    def add_grads(step, carry):
+        slot = lax.rem(step, 2)
+        h_load(step).wait()
+
+        @pl.when(step < streams * pieces - 1)
+        def _():
+            h_load(step + 1).start()
+
+        there = pl.ds(pl.multiple_of(lax.rem(step, pieces) * rows, rows), rows)
+        term = contract(h_buf[slot], g_ref[step // pieces, there, :], 0, 0)
+
+        @pl.when(step == 0)
+        def _():
+            sums[...] = term
+
+        @pl.when(step > 0)
+        def _():
+            sums[...] += term
+
+        return carry
+
+    lax.fori_loop(0, streams * pieces, add_grads, 0)
+    scatter.second()
+
+    x = x_ref[...].astype(f32)
+    inverse = norm_scale(x)
+    normed = x * inverse
+    gain = gain_ref[0:1, :].astype(f32)
+
+    def finish(start, g_h):
+        part = slice(start, start + half)
+        grad_ref[part] = g_mid_ref[part] + norm_backward(g_h, normed[part], inverse[part], gain)
+        return jnp.sum(g_h * normed[part], axis=0, keepdims=True)
+
+    gain_sum = finish(0, scatter.upper_sum()) + finish(half, scatter.lower_sum())
+
+    both = jnp.concatenate(
+        [gain_sum, sum_ref[0:1, :], jnp.zeros((14, width), f32)], axis=0
+    ).astype(LOW)
+    at = columns - 64
+    entry = lax.broadcasted_iota(jnp.int32, (16, 128), 0)
+    lane = lax.broadcasted_iota(jnp.int32, (16, 128), 1)
+    pick = jnp.where(lane == entry + (at - (columns - 128)), 1.0, 0.0).astype(LOW)
+    attn_ref[:, : columns - 128] = sums[:, : columns - 128].astype(LOW)
+    tail = sums[:, columns - 128 :] + contract(both, pick, 0, 0)
+    attn_ref[:, columns - 128 :] = tail.astype(LOW)
+    scatter.sent()
+
+
+def layer_close(g_all, wa, h1_all, g_mid, tokens, gains, gain_sum):
+    rows, width = tokens.shape
+    shape = jax.ShapeDtypeStruct
+    anywhere = pl.BlockSpec(memory_space=pl.ANY)
+    in_vmem = pl.BlockSpec(memory_space=pltpu.VMEM)
+    dma = pltpu.SemaphoreType.DMA
+    vmem = pltpu.VMEM
+    return pl.pallas_call(
+        close_kernel,
+        out_shape=[shape((rows, width), jnp.float32), shape(wa.shape, LOW)],
+        in_specs=[in_vmem, in_vmem, anywhere] + [in_vmem] * 4,
+        out_specs=[in_vmem, in_vmem],
+        scratch_shapes=[
+            vmem((4, rows, width), LOW),
+            vmem((4, rows, width), LOW),
+            vmem((4, rows, width), LOW),
+            vmem((4, rows // 2, width), LOW),
+            vmem((2, rows // 2, width), LOW),
+            vmem((2, rows, width), LOW),
+            vmem(wa.shape, jnp.float32),
+            dma((10,)),
+            dma((10,)),
+            dma((2,)),
+        ],
+        compiler_params=pltpu.CompilerParams(
+            collective_id=23, has_side_effects=True, vmem_limit_bytes=56 * MIB
+        ),
+        cost_estimate=moved(16 * rows * width),
+        name="close",
+    )(g_all, wa, h1_all, g_mid, tokens, gains, gain_sum)
+
+
 def ffn_lax(h_two, cot_all, gate_full, up_full, down_full):
     pieces, rows, width = cot_all.shape
     h_two_all = gather_plane(h_two, 5).reshape(-1, width)
@@ -1299,13 +1795,7 @@
             x_own, cot, attn_slice, w_out, ffn_slice, w_down, gain_rows, first, wide, qk
         )
         out_full, h_all, query, key, value, att_heads, attended, mid = front[3:11]
-        attn_full, gains, out_part, g_h_two, d_ffn, d_down = front[11:]
-        h_flat = h_all.reshape(streams * length, D)
-        value_full = attn_full[:, :wide]
-        query_full = attn_full[:, wide : wide + qk]
-        key_full = attn_full[:, wide + qk : wide + 2 * qk]
-        gains = gains.astype(jnp.float32)
-        gain_one, gain_two = gains[0], gains[1]
+        attn_full, gain_rows_all, out_part, g_h_two, d_ffn, d_down = front[11:]
     else:
 
         def gather_dp(w):
@@ -1347,63 +1837,70 @@
         )
         d_ffn = jnp.concatenate([d_gate, d_up], axis=1)
 
-    inverse_two = norm_scale(mid)
-    plain_two = mid * inverse_two
-
     def scatter_dp(part):
         return lax.psum_scatter(part, "dp", scatter_dimension=0, tiled=True)
 
+    own = rows_dp // pieces
     sum_ffn, sum_down = scatter_dp(d_ffn), scatter_dp(d_down)
-    output = (mid + scatter_plane(out_part, 8)).astype(LOW)
-
-    g_mid = cot.astype(jnp.float32) + norm_backward(g_h_two, plain_two, inverse_two, gain_two)
-    g_mid_low = g_mid.astype(LOW)
-    g_att = jnp.einsum(
-        "tsn,skn->tk",
-        g_mid_low.reshape(mine, pieces, out_width),
-        out_full,
-        preferred_element_type=jnp.float32,
-    )
-    g_att = to_heads(g_att.astype(LOW))
-    g_query, g_key, g_value = attend_back(query, key, value, first, att_heads, g_att, heads)
-    g_value = g_value.reshape(streams * length, wide)
-    g_query = g_query.reshape(streams * length, qk)
-    g_key = g_key.reshape(streams * length, qk)
-    g_h_one_part = (
-        contract(g_value, value_full, 1, 1)
-        + contract(g_query, query_full, 1, 1)
-        + contract(g_key, key_full, 1, 1)
-    ).astype(LOW)
-    g_h_one_part = g_h_one_part.reshape(streams, pieces, span, D).transpose(1, 0, 2, 3)
-    if sharers > 1:
-        padded = jnp.zeros((pieces, micro, span, D), LOW)
-        g_h_one_part = lax.dynamic_update_slice_in_dim(padded, g_h_one_part, first_stream, 1)
-    g_h_one = scatter_plane(g_h_one_part.reshape(pieces, mine, D), 9)
-    inverse_one = norm_scale(flat)
-    plain_one = flat * inverse_one
-    input_grad = g_mid + norm_backward(g_h_one, plain_one, inverse_one, gain_one)
-
-    own = rows_dp // pieces
-    grad_out = contract(attended, g_mid_low, 0, 0).astype(LOW)
-    grad_out = grad_out.reshape(groups, pieces, own, D).transpose(1, 0, 2, 3)
-    grad_out = scatter_plane(grad_out.reshape(pieces, groups * own, D), 10).astype(LOW)
+
+    if fused:
+        output, g_mid, g_all, grad_out, gain_sum = layer_turn(
+            g_h_two, mid, cot, gain_rows_all, out_full, out_part, attended, query, key, value,
+            att_heads, first, attn_full.shape[1],
+        )
+        input_grad, grad_attn = layer_close(
+            g_all, attn_full, h_all, g_mid, x_own, gain_rows_all, gain_sum
+        )
+    else:
+        inverse_two = norm_scale(mid)
+        plain_two = mid * inverse_two
+        output = (mid + scatter_plane(out_part, 8)).astype(LOW)
+        g_mid = cot.astype(jnp.float32) + norm_backward(g_h_two, plain_two, inverse_two, gain_two)
+        g_mid_low = g_mid.astype(LOW)
+        g_att = jnp.einsum(
+            "tsn,skn->tk",
+            g_mid_low.reshape(mine, pieces, out_width),
+            out_full,
+            preferred_element_type=jnp.float32,
+        )
+        g_att = to_heads(g_att.astype(LOW))
+        g_query, g_key, g_value = attend_back(query, key, value, first, att_heads, g_att, heads)
+        g_value = g_value.reshape(streams * length, wide)
+        g_query = g_query.reshape(streams * length, qk)
+        g_key = g_key.reshape(streams * length, qk)
+        g_h_one_part = (
+            contract(g_value, value_full, 1, 1)
+            + contract(g_query, query_full, 1, 1)
+            + contract(g_key, key_full, 1, 1)
+        ).astype(LOW)
+        g_h_one_part = g_h_one_part.reshape(streams, pieces, span, D).transpose(1, 0, 2, 3)
+        if sharers > 1:
+            padded = jnp.zeros((pieces, micro, span, D), LOW)
+            g_h_one_part = lax.dynamic_update_slice_in_dim(padded, g_h_one_part, first_stream, 1)
+        g_h_one = scatter_plane(g_h_one_part.reshape(pieces, mine, D), 9)
+        inverse_one = norm_scale(flat)
+        plain_one = flat * inverse_one
+        input_grad = g_mid + norm_backward(g_h_one, plain_one, inverse_one, gain_one)
+        grad_out = contract(attended, g_mid_low, 0, 0).astype(LOW)
+        grad_out = grad_out.reshape(groups, pieces, own, D).transpose(1, 0, 2, 3)
+        grad_out = scatter_plane(grad_out.reshape(pieces, groups * own, D), 10).astype(LOW)
+        grad_attn = jnp.concatenate(
+            [
+                contract(h_flat, g_value, 0, 0).astype(LOW),
+                contract(h_flat, g_query, 0, 0).astype(LOW),
+                contract(h_flat, g_key, 0, 0).astype(LOW),
+                jnp.sum(g_h_one * plain_one, axis=0).astype(LOW)[:, None],
+                jnp.sum(g_h_two * plain_two, axis=0).astype(LOW)[:, None],
+            ],
+            axis=1,
+        )
+
     grad_out, sum_ffn, sum_down = lax.optimization_barrier((grad_out, sum_ffn, sum_down))
     grad_out = scatter_dp(grad_out)
-    grad_attn = jnp.concatenate(
-        [
-            contract(h_flat, g_value, 0, 0).astype(LOW),
-            contract(h_flat, g_query, 0, 0).astype(LOW),
-            contract(h_flat, g_key, 0, 0).astype(LOW),
-            jnp.sum(g_h_one * plain_one, axis=0).astype(LOW)[:, None],
-            jnp.sum(g_h_two * plain_two, axis=0).astype(LOW)[:, None],
-        ],
-        axis=1,
-    )
-    grad_attn, grad_out = lax.optimization_barrier((grad_attn, grad_out))
     grad_attn = scatter_dp(grad_attn)
     ffn_got = exchange_plane(sum_ffn.reshape(pieces, own, 2 * hidden), 11).astype(jnp.float32)
     attn_got = exchange_plane(grad_attn.reshape(pieces, own, -1), 12).astype(jnp.float32)
-    grad_gains = jnp.sum(attn_got[:, :, wide + 2 * qk :], axis=0)
+    grad_gains = jnp.sum(attn_got[:, :, wide + 2 * qk : wide + 2 * qk + 2], axis=0)
     attn_got = jnp.sum(attn_got.reshape(pieces // sharers, sharers, own, -1), axis=1)
 
     def by_rows(block):

time: 684 us -> 615 us (0.90)
  matrix products: 58 us -> 0 us
  waiting for transfers between devices: 4.33 us -> 48.1 us
  local copies, waits for them, and re-layouts: 84.1 us -> 42.6 us
  Pallas kernels: 495 us -> 485 us
    dot_general x8 -> x0, matrix products: 58 us -> none  [the longest x7 52.3 us: contract(): lax.dot_general(left, right, (((left_dim,), (right_dim,)), ((), ())), pre...]
    reduce_scatter x4, waiting for transfers between devices: 3.59 us -> 47.3 us  [scatter_dp(): return lax.psum_scatter(part, 'dp', scatter_dimension=0, tiled=True)]
    reshape x3 -> x0, local copies, waits for them, and re-layouts: 17.7 us -> none  [the longest x1 8.27 us: local(): g_h_one_part.reshape(streams, pieces, span, D).transpose(1, 0, 2, 3)]
    pallas_call x3 -> x2, Pallas kernels: 42.5 us -> 28.1 us  [exchange_plane(): pl.pallas_call(exchange_kernel, out_shape=jax.ShapeDtypeStruct(x.shape, x...]
    unnamed x52 -> x13, local copies, waits for them, and re-layouts: 14.4 us -> 4.46 us
    concatenate x1 -> x0, local copies, waits for them, and re-layouts: 7.12 us -> none  [local(): jnp.concatenate([contract(h_flat, g_value, 0, 0).astype(LOW), contract(h_...]
    pallas_call x4 -> x2, Pallas kernels: 144 us -> 150 us  [the longest x1 104 us: layer_turn(): pl.pallas_call(turn_kernel, out_shape=[shape((rows, width), LOW), shape((...]
  transfers between devices with their start and end apart: 4 -> 4, of which waited for: 1 -> 2; matrix products, arithmetic and copies ran while one was open for 18% -> 5% of each run, Pallas kernels for 27% -> 29%
where the time goes in v6:
time: 615 us; the launch traced here: 603 us
  Pallas kernels  485 us (79%)
  waiting for transfers between devices  48.1 us (8%)
  local copies, waits for them, and re-layouts  42.6 us (7%)
  between operations  14.4 us (2%)
  other arithmetic  12.2 us (2%)
    pallas_call x1, Pallas kernels, layer_front(): pl.pallas_call(layer_kernel, out_shape=out_shape, in_specs=[anywhere] * 7...  308 us
    pallas_call x1, Pallas kernels, layer_turn(): pl.pallas_call(turn_kernel, out_shape=[shape((rows, width), LOW), shape((...  104 us
    reduce_scatter x4, waiting for transfers between devices, scatter_dp(): return lax.psum_scatter(part, 'dp', scatter_dimension=0, tiled=True)  47.3 us
    pallas_call x1, Pallas kernels, layer_close(): pl.pallas_call(close_kernel, out_shape=[shape((rows, width), jnp.float32)...  45.3 us
    pallas_call x2, Pallas kernels, exchange_plane(): pl.pallas_call(exchange_kernel, out_shape=jax.ShapeDtypeStruct(x.shape, x...  28.1 us
  transfers between devices with their start and end apart: 4, of which 2 were waited for; matrix products, arithmetic and copies ran while one was open for 5% of the time, Pallas kernels for 29%

profile of v6, /device:TPU:1, one launch (start us, length us, event | category | flops | bytes accessed | tf_op | source)
XLA Modules:
  0.0 603.0 jit_solution(15243815843582587186)
XLA Ops:
  7.2 0.0 reduce-scatter.9.cloned.1.call-start
  7.2 0.1 pad.8.clone
  7.3 0.1 pad.12.clone
  7.4 0.9 reduce_window_sum.14
  8.3 0.7 bitcast_subtract_fusion
  8.9 0.7 broadcast_in_dim.29
  9.6 0.7 broadcast_in_dim.30
  10.3 0.1 select_reduce_fusion
  10.4 1.3 copy.64.first_ref
  11.8 1.0 constant_dynamic-slice_fusion.26
  12.7 0.7 maximum_maximum_fusion.1.gain_ref
  13.4 1.1 constant_dynamic-slice_fusion.24
  14.5 0.9 maximum_maximum_fusion.wa_ref
  15.4 1.9 constant_dynamic-slice_fusion.16
  17.3 3.1 constant_dynamic-slice_fusion
  20.5 6.2 %concatenate.16.wgu_ref = bf16[512,1408]{1,0:T(8,128)(2,1)} concatenate(bf16[512,64]{1,0:T(8,128)(2,1)S(1)} %get-tuple-element.139, bf16[512,64]{1,0:T(8,128)(2,1)S(1)} %get-tuple-element.140, bf16[512,64]{1,0:T(8,128)(2,1)S(1)} %get-tuple-element.141, bf16[512,64]{1,0:T(8,128)(2,1)S(1)} %get-tuple-element.142, bf16[512,64]{1,0:T(8,128)(2,1)S(1)} %get-tuple-element.120, ...), dimensions={1} | concatenate | bytes 2883584 | tf_op jit(solution)/shard_map/concatenate | solution.py:1758
  26.6 307.6 %layer.1 = (bf16[8,256,2048]{2,1,0:T(8,128)(2,1)}, bf16[8,256,2048]{2,1,0:T(8,128)(2,1)}, bf16[8,256,2048]{2,1,0:T(8,128)(2,1)}, bf16[8,2048,256]{2,1,0:T(8,128)...) custom-call(bf16[256,2048]{1,0:T(8,128)(2,1)} %bitcast.33, ...), custom_call_target="tpu_custom_call" | custom-call | flops 53150220288 | bytes 209715200 | tf_op jit(solution)/shard_map/layer/pallas_call | solution.py:1130
  334.2 0.0 reduce-scatter.9.cloned.1.call-update
  334.2 0.0 reduce-scatter.7.cloned.1.call-start
  334.3 0.7 reduce-scatter.7.cloned.1.call-update
  335.0 0.0 reduce-scatter.5.cloned.1.call-start
  335.0 104.4 %turn.1 = (bf16[256,2048]{1,0:T(8,128)(2,1)}, f32[256,2048]{1,0:T(8,128)}, bf16[2,1024,384]{2,1,0:T(8,128)(2,1)}, bf16[256,2048]{1,0:T(8,128)(2,1)}, f32[8,2048]{1,0:T(8,128)}) custom-call(f32[256,2048]{1,0:T(8,128)} %get-tuple-element.35.gh_ref, f32[256,2048]{1,0:T(8,128)} %get-tuple-element.36.mid_ref, bf16[256,2048]{1,0:T(8,128)(2,1)} %bitcast.37, ...), custom_call_target="tpu_custom_call" | custom-call | bytes 83886080 | tf_op jit(solution)/shard_map/turn/pallas_call | solution.py:1505
  439.5 45.3 %close.1 = (f32[256,2048]{1,0:T(8,128)}, bf16[2048,384]{1,0:T(8,128)(2,1)}) custom-call(bf16[2,1024,384]{2,1,0:T(8,128)(2,1)} %get-tuple-element.46.g_ref, bf16[2048,384]{1,0:T(8,128)(2,1)} %get-tuple-element.47.wa_ref, bf16[2,1024,2048]{2,1,0:T(8,128)(2,1)} %get-tuple-element.48.h1_ref, f32[256,2048]{1,0:T(8,128)} %get-tuple-element.49.g_mid_ref, ...), custom_call_target="tpu_custom_call" | custom-call | bytes 83886080 | tf_op jit(solution)/shard_map/close/pallas_call | solution.py:1658
  484.8 0.0 reduce-scatter.5.cloned.1.call-update
  484.8 0.3 reduce-scatter.11.cloned.1.call-start
  485.0 0.0 reduce-scatter.9.cloned.1.call-done
  485.1 9.4 %reduce-scatter.7.cloned.1.call-done = bf16[512,1408]{1,0:T(8,128)(2,1)} async-done(((bf16[2048,1408]{1,0:T(8,128)(2,1)}), bf16[512,1408]{1,0:T(8,128)(2,1)}) %reduce-scatter.7.cloned.1.call-update) | async-done | bytes 1441808 | tf_op jit(solution)/shard_map/reduce_scatter | solution.py:1841
  494.5 0.0 reduce-scatter.11.cloned.1.call-update
  494.5 37.9 %reduce-scatter.5.cloned.1.call-done = bf16[512,384]{1,0:T(8,128)(2,1)} async-done(((bf16[2048,384]{1,0:T(8,128)(2,1)}), bf16[512,384]{1,0:T(8,128)(2,1)}) %reduce-scatter.5.cloned.1.call-update) | async-done | bytes 393232 | tf_op jit(solution)/shard_map/reduce_scatter | solution.py:1841
  532.4 8.8 %exchange.2 = bf16[8,64,384]{2,1,0:T(8,128)(2,1)} custom-call(bf16[8,64,384]{2,1,0:T(8,128)(2,1)} %bitcast.41), custom_call_target="tpu_custom_call" | custom-call | bytes 7864320 | tf_op jit(solution)/shard_map/exchange/pallas_call | solution.py:341
  541.2 1.1 convert_element_type.12
  542.3 0.1 slice_bitcast_fusion.1
  542.4 0.1 copy.67
  542.5 0.7 copy.76
  543.3 0.8 copy.77
  544.1 0.1 copy.66
  544.2 0.7 copy.75
  545.0 0.1 slice_reduce_fusion
  545.1 0.7 slice_reduce_fusion.1
  545.8 19.3 %exchange.3 = bf16[8,64,1408]{2,1,0:T(8,128)(2,1)} custom-call(bf16[8,64,1408]{2,1,0:T(8,128)(2,1)} %bitcast.32), custom_call_target="tpu_custom_call" | custom-call | bytes 28835840 | tf_op jit(solution)/shard_map/exchange/pallas_call | solution.py:341
  565.1 1.9 fusion.1
  567.0 0.3 copy.72
  567.3 0.4 copy.73
  567.7 0.7 copy-done
  568.4 1.2 fusion
  569.6 0.5 reshape.93
  570.0 0.0 copy-done.2
  570.0 1.2 copy.69
  571.2 1.5 copy.70
  572.7 2.5 reshape.94
  575.2 2.4 maximum_bitcast_fusion.1
  577.6 1.2 copy.74
  578.8 2.6 reshape.96
  581.4 1.5 reshape.89
  582.9 1.5 reshape.90
  584.4 1.1 maximum_bitcast_fusion
  585.6 1.2 copy.71
  586.8 0.0 copy-start.3
  586.8 2.7 reshape.92
  589.4 2.5 convert_element_type.15
  592.0 1.8 convert_element_type.13
  593.7 0.0 copy-done.3
  593.7 1.0 copy.80
  594.7 1.3 copy.81
  (8 shorter events, 0.1 us)
Async XLA Ops:
  7.2 477.9 %reduce-scatter.9.cloned.1.call-start = ((), (), s32[]{:S(2)}) async-start(), calls=%async_computation.6 | async-start | bytes 3604480 | tf_op jit(solution)/shard_map/reduce_scatter | solution.py:1841
  334.2 160.2 %reduce-scatter.7.cloned.1.call-start = ((), (), s32[]{:S(2)}) async-start(), calls=%async_computation.5 | async-start | bytes 7208960 | tf_op jit(solution)/shard_map/reduce_scatter | solution.py:1841
  335.0 197.4 %reduce-scatter.5.cloned.1.call-start = ((), (), s32[]{:S(2)}) async-start(), calls=%async_computation.4 | async-start | bytes 1966080 | tf_op jit(solution)/shard_map/reduce_scatter | solution.py:1841
  484.8 107.2 %reduce-scatter.11.cloned.1.call-start = ((), (), s32[]{:S(2)}) async-start(), calls=%async_computation.7 | async-start | bytes 1310720 | tf_op jit(solution)/shard_map/reduce_scatter | solution.py:1841
  567.0 1.4 copy-start
  568.4 1.6 copy-start.2
  586.8 7.0 %copy-start.3 = (bf16[256,2048]{1,0:T(8,128)(2,1)S(1)}, bf16[256,2048]{1,0:T(8,128)(2,1)}, u32[]{:S(2)}) copy-start(bf16[256,2048]{1,0:T(8,128)(2,1)} %get-tuple-element.45) | copy-start | bytes 3145732
  589.4 5.3 copy-start.1
Sparse Core Ops, SparseCore 0:
  334.4 55.4 reduce-scatter.8
  392.1 102.3 reduce-scatter.6
  496.8 35.5 reduce-scatter.4
  534.6 26.0 reduce-scatter.10

commit v7 on v6

--- a/solution.py
+++ b/solution.py
@@ -532,8 +532,12 @@
     gain_out,
     out_part,
     gh_ref,
+    dgu_first,
+    dd_first,
     dgu_out,
     dd_out,
+    dgu_all,
+    dd_all,
     wa,
     wgu,
     wd,
@@ -572,6 +576,8 @@
     w_sem,
     done_sem,
     self_sem,
+    fsend,
+    frecv,
 ):
     me, sib, xn, yn = partners()
     z = lax.axis_index("dp")
@@ -913,6 +919,20 @@
 
     def emit(k):
         count = 4 * CHUNKS[k]
+        rest = share - CHUNKS[0]
+
+        def gu_target(i):
+            there = pl.ds(i * rows, rows)
+            if k == 0:
+                return dgu_first.at[there]
+            return dgu_out.at[there, pl.ds(columns[k] - columns[1], 2 * count)]
+
+        def d_target(owner):
+            if k == 0:
+                return dd_first.at[pl.ds(owner * CHUNKS[0], CHUNKS[0])]
+            start = owner * rest + (hiddens[k] - hiddens[1]) // 4
+            return dd_out.at[pl.ds(start, CHUNKS[k])]
+
         pending = [None, None]
         for i in range(width // rows):
             slot = i % 2
@@ -920,9 +940,7 @@
                 pending[slot].wait()
             o_buf[slot, :, : 2 * count] = sum_gu[i * rows : (i + 1) * rows, : 2 * count].astype(LOW)
             pending[slot] = pltpu.make_async_copy(
-                o_buf.at[slot, :, pl.ds(0, 2 * count)],
-                dgu_out.at[pl.ds(i * rows, rows), pl.ds(columns[k], 2 * count)],
-                out_sem.at[slot],
+                o_buf.at[slot, :, pl.ds(0, 2 * count)], gu_target(i), out_sem.at[slot]
             )
             pending[slot].start()
         for c in pending:
@@ -933,7 +951,7 @@
             downs.append(
                 pltpu.make_async_copy(
                     o_buf.at[0, pl.ds(owner * CHUNKS[k], CHUNKS[k])],
-                    dd_out.at[pl.ds(owner * share + hiddens[k] // 4, CHUNKS[k])],
+                    d_target(owner),
                     h1_sem.at[owner // 2, owner % 2],
                 )
             )
@@ -992,6 +1010,12 @@
     for c in loads(nearest_first, 0, sources):
         c.start()
     emit(0)
+    sum_lines = [
+        LineScatter(dgu_first, depth, dgu_all, fsend.at[0], frecv.at[0], self_sem.at[0]),
+        LineScatter(dd_first, CHUNKS[0], dd_all, fsend.at[1], frecv.at[1], self_sem.at[1]),
+    ]
+    for g in sum_lines:
+        g.start()
 
     def arrive_last(step):
         @pl.when(step == 4)
@@ -1087,6 +1111,8 @@
     gh_ref[half:] = held[0, half:].astype(f32) + one[3].astype(f32) + two[1].astype(f32)
     for c in finals:
         c.wait()
+    for g in sum_lines:
+        g.wait()
     for c in (b_y, b_own, x0, y0, x1, y1, y2, x2, *swaps):
         c.wait_send()
     for g in (tokens, out_w, cots, z_gain, z_attn, z_out, *z_up, *z_down):
@@ -1122,8 +1148,12 @@
         shape((gain_rows.shape[0], width), LOW),
         plane,
         shape((rows, width), f32),
-        shape((width, 2 * hidden), LOW),
-        shape((hidden, width), LOW),
+        shape((width, 8 * CHUNKS[0]), LOW),
+        shape((4 * CHUNKS[0], width), LOW),
+        shape((width, 2 * hidden - 8 * CHUNKS[0]), LOW),
+        shape((hidden - 4 * CHUNKS[0], width), LOW),
+        shape((4, width // 4, 8 * CHUNKS[0]), LOW),
+        shape((4, CHUNKS[0], width), LOW),
     ]
     dma = pltpu.SemaphoreType.DMA
     vmem = pltpu.VMEM
@@ -1131,7 +1161,7 @@
         layer_kernel,
         out_shape=out_shape,
         in_specs=[anywhere] * 7 + [in_vmem],
-        out_specs=[anywhere] * 14 + [in_vmem] + [anywhere] * 2,
+        out_specs=[anywhere] * 14 + [in_vmem] + [anywhere] * 6,
         scratch_shapes=[
             vmem(attn_shape, LOW),
             vmem((width, 2 * hidden), LOW),
@@ -1171,6 +1201,8 @@
             dma((2,)),
             dma((8,)),
             dma((4,)),
+            dma((2, 3)),
+            dma((2, 4)),
         ],
         compiler_params=pltpu.CompilerParams(
             collective_id=21, has_side_effects=True, vmem_limit_bytes=63 * MIB
@@ -1182,6 +1214,38 @@
         ),
         name="layer",
     )(tokens, cot, attn_slice, w_out, ffn_slice, w_down, gain_rows, first)
+
+
+class LineScatter:
+    def __init__(self, source, count, target, send, recv, local):
+        z = lax.axis_index("dp")
+
+        def copy(k, to, owner):
+            return pltpu.make_async_remote_copy(
+                src_ref=source.at[pl.ds(to * count, count)],
+                dst_ref=target.at[owner],
+                send_sem=send.at[k],
+                recv_sem=recv.at[owner],
+                device_id={"dp": to},
+                device_id_type=MESH,
+            )
+
+        others = [lax.rem(z + o, 4) for o in (2, 1, 3)]
+        self.sends = [copy(k, other, z) for k, other in enumerate(others)]
+        self.arrivals = [copy(0, other, other) for other in others]
+        self.own = pltpu.make_async_copy(source.at[pl.ds(z * count, count)], target.at[z], local)
+
+    def start(self):
+        self.own.start()
+        for c in self.sends:
+            c.start()
+
+    def wait(self):
+        for c in self.arrivals:
+            c.wait_recv()
+        self.own.wait()
+        for c in self.sends:
+            c.wait_send()
 
 
 class PlaneScatter:
@@ -1266,11 +1330,12 @@
     v_ref,
     att_ref,
     first_ref,
+    h1_ref,
     output_ref,
     g_mid_out,
     g_out,
-    go_out,
     gain_out,
+    attn_ref,
     g_mid,
     work,
     g_low,
@@ -1288,6 +1353,8 @@
     two_o,
     gk_sum,
     gv_sum,
+    h_buf,
+    sums,
     esend,
     erecv,
     ssend,
@@ -1296,6 +1363,7 @@
     w_sem,
     self_sem,
     done_sem,
+    h_sem,
 ):
     me, sib, xn, yn = partners()
     flip = sib - me
@@ -1431,6 +1499,18 @@
 
     length = v_ref.shape[1]
     block = 256
+    streams = v_ref.shape[0]
+    pieces = length // rows
+
+    def h_load(step):
+        slot = lax.rem(step, 2)
+        return pltpu.make_async_copy(
+            h1_ref.at[step // pieces, pl.ds(lax.rem(step, pieces) * rows, rows)],
+            h_buf.at[slot],
+            h_sem.at[slot],
+        )
+
+    h_load(0).start()
 
     def back_stream(m, carry):
         gk_sum[...] = jnp.zeros_like(gk_sum)
@@ -1473,10 +1553,41 @@
     weights.second()
     done.append(pltpu.make_async_copy(g_s, g_out, done_sem.at[1]))
     done[1].start()
+    outs.second()
+
+    def add_grads(step, carry):
+        slot = lax.rem(step, 2)
+        h_load(step).wait()
+
+        @pl.when(step < streams * pieces - 1)
+        def _():
+            h_load(step + 1).start()
+
+        there = pl.ds(pl.multiple_of(lax.rem(step, pieces) * rows, rows), rows)
+        term = contract(h_buf[slot], g_s[step // pieces, there, :], 0, 0)
+
+        @pl.when(step == 0)
+        def _():
+            sums[...] = term
+
+        @pl.when(step > 0)
+        def _():
+            sums[...] += term
+
+        return carry
+
+    lax.fori_loop(0, streams * pieces, add_grads, 0)
+    narrow = sums.shape[1]
+    attn_ref[:, :narrow] = sums[...].astype(LOW)
     mid_load.wait()
-    outs.second()
-    go_out[:half] = weights.upper_sum().astype(LOW)
-    go_out[half:] = weights.lower_sum().astype(LOW)
+    for part, total in enumerate((weights.upper_sum(), weights.lower_sum())):
+        total = total.astype(LOW)
+        for z in range(2):
+            for i in range(8):
+                start = ((2 * part + z) * 8 + i) * own
+                attn_ref[start : start + own, narrow:] = total[
+                    z * own : (z + 1) * own, i * wide : (i + 1) * wide
+                ]
     output_ref[:half] = (work[:half] + outs.upper_sum()).astype(LOW)
     output_ref[half:] = (work[half:] + outs.lower_sum()).astype(LOW)
     for c in done:
@@ -1487,7 +1598,7 @@
     outs.sent()
 
 
-def layer_turn(gh, mid, cot, gains, wo_all, part, tok, query, key, value, att, first, columns):
+def layer_turn(gh, mid, cot, gains, wo_all, part, tok, query, key, value, att, first, h1, columns):
     rows, width = mid.shape
     streams, length, wide = value.shape
     qk = query.shape[2]
@@ -1508,10 +1619,10 @@
             shape((rows, width), LOW),
             shape((rows, width), f32),
             shape((streams, length, columns), LOW),
-            shape((rows, width), LOW),
             shape((8, width), f32),
+            shape((width, columns + wide), LOW),
         ],
-        in_specs=[anywhere] * 3 + [in_vmem] + [anywhere] * 2 + [in_vmem] * 6,
+        in_specs=[anywhere] * 3 + [in_vmem] + [anywhere] * 2 + [in_vmem] * 6 + [anywhere],
         out_specs=[in_vmem, anywhere, anywhere, in_vmem, in_vmem],
         scratch_shapes=[
             vmem((rows, width), f32),
@@ -1527,11 +1638,14 @@
             *arriving,
             vmem((length, qk), f32),
             vmem((length, wide), f32),
+            vmem((2, rows, width), LOW),
+            vmem((width, columns), f32),
             dma((14,)),
             dma((14,)),
             dma((2, 10)),
             dma((2, 10)),
             dma((7,)),
+            dma((2,)),
             dma((2,)),
             dma((2,)),
             dma((2,)),
@@ -1541,52 +1655,54 @@
         ),
         cost_estimate=moved(16 * rows * width),
         name="turn",
-    )(gh, mid, cot, gains, wo_all, part, tok, query, key, value, att, first)
+    )(gh, mid, cot, gains, wo_all, part, tok, query, key, value, att, first, h1)
 
 
 def close_kernel(
     g_ref,
     wa_ref,
-    h1_ref,
     g_mid_ref,
     x_ref,
     gain_ref,
     sum_ref,
     grad_ref,
-    attn_ref,
+    gains_ref,
     beside,
     held,
     got,
     one,
     two,
-    h_buf,
-    sums,
+    gain_rows,
+    gain_line,
+    gain_columns,
+    gain_plane,
     ssend,
     srecv,
-    h_sem,
+    zsend,
+    zrecv,
+    esend,
+    erecv,
+    self_sem,
 ):
     me, sib, xn, yn = partners()
+    z = lax.axis_index("dp")
     rows, width = x_ref.shape
     span = rows // 2
     half = rows // 2
     f32 = jnp.float32
-    greet((sib, xn, yn))
+    barrier = pltpu.get_barrier_semaphore()
+    for i in range(1, 8):
+        pl.semaphore_signal(
+            barrier, inc=1, device_id={"seq": lax.rem(me + i, 8)}, device_id_type=MESH
+        )
+    for i in range(1, 4):
+        pl.semaphore_signal(
+            barrier, inc=1, device_id={"dp": lax.rem(z + i, 4)}, device_id_type=MESH
+        )
+    pl.semaphore_wait(barrier, 10)
     scatter = PlaneScatter(
         lambda i: beside.at[i], lambda i: held.at[i], got, one, two, ssend, srecv
     )
-    streams, length, columns = g_ref.shape
-    pieces = length // rows
-
-    def h_load(step):
-        slot = lax.rem(step, 2)
-        return pltpu.make_async_copy(
-            h1_ref.at[step // pieces, pl.ds(lax.rem(step, pieces) * rows, rows)],
-            h_buf.at[slot],
-            h_sem.at[slot],
-        )
-
-    h_load(0).start()
-
     def part_of(owner):
         there = pl.ds(pl.multiple_of(owner * span, span), span)
         grads = jnp.concatenate([g_ref[0, there, :], g_ref[1, there, :]], axis=0)
@@ -1599,28 +1715,6 @@
         held[i] = part_of(owners[i])
         scatter.add_pair(i)
 
-    def add_grads(step, carry):
-        slot = lax.rem(step, 2)
-        h_load(step).wait()
-
-        @pl.when(step < streams * pieces - 1)
-        def _():
-            h_load(step + 1).start()
-
-        there = pl.ds(pl.multiple_of(lax.rem(step, pieces) * rows, rows), rows)
-        term = contract(h_buf[slot], g_ref[step // pieces, there, :], 0, 0)
-
-        @pl.when(step == 0)
-        def _():
-            sums[...] = term
-
-        @pl.when(step > 0)
-        def _():
-            sums[...] += term
-
-        return carry
-
-    lax.fori_loop(0, streams * pieces, add_grads, 0)
     scatter.second()
 
     x = x_ref[...].astype(f32)
@@ -1635,30 +1729,83 @@
 
     gain_sum = finish(0, scatter.upper_sum()) + finish(half, scatter.lower_sum())
 
-    both = jnp.concatenate(
-        [gain_sum, sum_ref[0:1, :], jnp.zeros((14, width), f32)], axis=0
-    ).astype(LOW)
-    at = columns - 64
+    both = jnp.concatenate([gain_sum, sum_ref[0:1, :], jnp.zeros((14, width), f32)], axis=0)
+    gain_rows[...] = both.astype(LOW)
+    depth = width // 4
+
+    def lanes(owner):
+        return pl.ds(pl.multiple_of(owner * depth, 128), depth)
+
+    def over_line(k, to, owner):
+        return pltpu.make_async_remote_copy(
+            src_ref=gain_rows.at[:, lanes(to)],
+            dst_ref=gain_line.at[owner],
+            send_sem=zsend.at[k],
+            recv_sem=zrecv.at[owner],
+            device_id={"dp": to},
+            device_id_type=MESH,
+        )
+
+    others = [lax.rem(z + o, 4) for o in (1, 2, 3)]
+    sends = [over_line(k, other, z) for k, other in enumerate(others)]
+    own = pltpu.make_async_copy(gain_rows.at[:, lanes(z)], gain_line.at[z], self_sem.at[0])
+    own.start()
+    for c in sends:
+        c.start()
+    own.wait()
+    for other in others:
+        over_line(0, other, other).wait_recv()
+    total = gain_line[0].astype(f32)
+    for k in range(1, 4):
+        total = total + gain_line[k].astype(f32)
     entry = lax.broadcasted_iota(jnp.int32, (16, 128), 0)
     lane = lax.broadcasted_iota(jnp.int32, (16, 128), 1)
-    pick = jnp.where(lane == entry + (at - (columns - 128)), 1.0, 0.0).astype(LOW)
-    attn_ref[:, : columns - 128] = sums[:, : columns - 128].astype(LOW)
-    tail = sums[:, columns - 128 :] + contract(both, pick, 0, 0)
-    attn_ref[:, columns - 128 :] = tail.astype(LOW)
+    pick = jnp.where(lane == entry, 1.0, 0.0).astype(LOW)
+    gain_columns[...] = contract(total.astype(LOW), pick, 0, 0).astype(LOW)
+    count = depth // 8
+    own = pltpu.make_async_copy(
+        gain_columns.at[pl.ds(me * count, count)], gain_plane.at[me], self_sem.at[1]
+    )
+    own.start()
+    swaps = []
+    for i in range(1, 8):
+        other = lax.rem(me + i, 8)
+        swaps.append(
+            remote(
+                esend,
+                erecv,
+                i - 1,
+                gain_columns.at[pl.ds(other * count, count)],
+                gain_plane.at[me],
+                other,
+            )
+        )
+        swaps[-1].start()
+    own.wait()
+    for c in swaps:
+        c.wait_recv()
+    total = gain_plane[0].astype(f32)
+    for k in range(1, 8):
+        total = total + gain_plane[k].astype(f32)
+    gains_ref[...] = total
     scatter.sent()
-
-
-def layer_close(g_all, wa, h1_all, g_mid, tokens, gains, gain_sum):
+    for c in (*sends, *swaps):
+        c.wait_send()
+
+
+def layer_close(g_all, wa, g_mid, tokens, gains, gain_sum):
     rows, width = tokens.shape
     shape = jax.ShapeDtypeStruct
-    anywhere = pl.BlockSpec(memory_space=pl.ANY)
     in_vmem = pl.BlockSpec(memory_space=pltpu.VMEM)
     dma = pltpu.SemaphoreType.DMA
     vmem = pltpu.VMEM
     return pl.pallas_call(
         close_kernel,
-        out_shape=[shape((rows, width), jnp.float32), shape(wa.shape, LOW)],
-        in_specs=[in_vmem, in_vmem, anywhere] + [in_vmem] * 4,
+        out_shape=[
+            shape((rows, width), jnp.float32),
+            shape((width // 32, 128), jnp.float32),
+        ],
+        in_specs=[in_vmem] * 6,
         out_specs=[in_vmem, in_vmem],
         scratch_shapes=[
             vmem((4, rows, width), LOW),
@@ -1666,10 +1813,16 @@
             vmem((4, rows, width), LOW),
             vmem((4, rows // 2, width), LOW),
             vmem((2, rows // 2, width), LOW),
-            vmem((2, rows, width), LOW),
-            vmem(wa.shape, jnp.float32),
+            vmem((16, width), LOW),
+            vmem((4, 16, width // 4), LOW),
+            vmem((width // 4, 128), LOW),
+            vmem((8, width // 32, 128), LOW),
             dma((10,)),
             dma((10,)),
+            dma((3,)),
+            dma((4,)),
+            dma((7,)),
+            dma((7,)),
             dma((2,)),
         ],
         compiler_params=pltpu.CompilerParams(
@@ -1677,7 +1830,7 @@
         ),
         cost_estimate=moved(16 * rows * width),
         name="close",
-    )(g_all, wa, h1_all, g_mid, tokens, gains, gain_sum)
+    )(g_all, wa, g_mid, tokens, gains, gain_sum)
 
 
 def ffn_lax(h_two, cot_all, gate_full, up_full, down_full):
@@ -1795,7 +1948,8 @@
             x_own, cot, attn_slice, w_out, ffn_slice, w_down, gain_rows, first, wide, qk
         )
         out_full, h_all, query, key, value, att_heads, attended, mid = front[3:11]
-        attn_full, gain_rows_all, out_part, g_h_two, d_ffn, d_down = front[11:]
+        attn_full, gain_rows_all, out_part, g_h_two = front[11:15]
+        d_ffn, d_down, ffn_blocks, down_blocks = front[17:]
     else:
 
         def gather_dp(w):
@@ -1844,12 +1998,12 @@
     sum_ffn, sum_down = scatter_dp(d_ffn), scatter_dp(d_down)
 
     if fused:
-        output, g_mid, g_all, grad_out, gain_sum = layer_turn(
+        output, g_mid, g_all, gain_sum, grad_attn = layer_turn(
             g_h_two, mid, cot, gain_rows_all, out_full, out_part, attended, query, key, value,
-            att_heads, first, attn_full.shape[1],
-        )
-        input_grad, grad_attn = layer_close(
-            g_all, attn_full, h_all, g_mid, x_own, gain_rows_all, gain_sum
+            att_heads, first, h_all, attn_full.shape[1],
+        )
+        input_grad, gain_columns = layer_close(
+            g_all, attn_full, g_mid, x_own, gain_rows_all, gain_sum
         )
     else:
         inverse_two = norm_scale(mid)
@@ -1884,6 +2038,7 @@
         grad_out = contract(attended, g_mid_low, 0, 0).astype(LOW)
         grad_out = grad_out.reshape(groups, pieces, own, D).transpose(1, 0, 2, 3)
         grad_out = scatter_plane(grad_out.reshape(pieces, groups * own, D), 10).astype(LOW)
+        grad_out = scatter_dp(grad_out)
         grad_attn = jnp.concatenate(
             [
                 contract(h_flat, g_value, 0, 0).astype(LOW),
@@ -1895,16 +2050,17 @@
             axis=1,
         )
 
-    grad_out, sum_ffn, sum_down = lax.optimization_barrier((grad_out, sum_ffn, sum_down))
-    grad_out = scatter_dp(grad_out)
+    grad_attn, sum_ffn, sum_down = lax.optimization_barrier((grad_attn, sum_ffn, sum_down))
     grad_attn = scatter_dp(grad_attn)
+    if fused:
+        grad_out = grad_attn[:, -out_width:].reshape(pieces, own, out_width)
+        grad_out = grad_out.transpose(1, 0, 2).reshape(own, D)
+        grad_attn = grad_attn[:, :-out_width]
+        first_ffn = jnp.sum(ffn_blocks.astype(jnp.float32), axis=0).astype(LOW)
+        sum_ffn = jnp.concatenate([first_ffn, sum_ffn], axis=1)
+        first_down = jnp.sum(down_blocks.astype(jnp.float32), axis=0)
+        sum_down = jnp.concatenate([first_down, sum_down.astype(jnp.float32)], axis=0)
     ffn_got = exchange_plane(sum_ffn.reshape(pieces, own, 2 * hidden), 11).astype(jnp.float32)
-    attn_got = exchange_plane(grad_attn.reshape(pieces, own, -1), 12).astype(jnp.float32)
-    grad_gains = jnp.sum(attn_got[:, :, wide + 2 * qk : wide + 2 * qk + 2], axis=0)
-    attn_got = jnp.sum(attn_got.reshape(pieces // sharers, sharers, own, -1), axis=1)
-
-    def by_rows(block):
-        return block.transpose(1, 0, 2).reshape(own, -1)
 
     def by_hidden(second):
         parts, start = [], 0
@@ -1916,6 +2072,18 @@
         whole = jnp.concatenate(parts, axis=3)
         return whole.transpose(1, 2, 0, 3).reshape(own, FF)
 
+    grad_gate, grad_up = by_hidden(0), by_hidden(1)
+    grad_attn, grad_gate, grad_up = lax.optimization_barrier((grad_attn, grad_gate, grad_up))
+    attn_got = exchange_plane(grad_attn.reshape(pieces, own, -1), 12).astype(jnp.float32)
+    if fused:
+        grad_gains = gain_columns
+    else:
+        grad_gains = jnp.sum(attn_got[:, :, wide + 2 * qk : wide + 2 * qk + 2], axis=0)
+    attn_got = jnp.sum(attn_got.reshape(pieces // sharers, sharers, own, -1), axis=1)
+
+    def by_rows(block):
+        return block.transpose(1, 0, 2).reshape(own, -1)
+
     return (
         output.reshape(tokens.shape),
         input_grad.reshape(tokens.shape),
@@ -1923,8 +2091,8 @@
         by_rows(attn_got[:, :, wide + qk : wide + 2 * qk]),
         by_rows(attn_got[:, :, :wide]),
         grad_out.astype(jnp.float32),
-        by_hidden(0),
-        by_hidden(1),
+        grad_gate,
+        grad_up,
         sum_down.astype(jnp.float32),
         grad_gains[:, 0],
         grad_gains[:, 1],

time: 615 us -> 622 us (1.011)
  Pallas kernels: 485 us -> 531 us
  waiting for transfers between devices: 48.1 us -> 2.69 us
    reduce_scatter x4 -> x3, waiting for transfers between devices: 47.3 us -> 1.96 us  [scatter_dp(): return lax.psum_scatter(part, 'dp', scatter_dimension=0, tiled=True)]
    pallas_call x1, Pallas kernels: 308 us -> 342 us  [layer_front(): pl.pallas_call(layer_kernel, out_shape=out_shape, in_specs=[anywhere] * 7...]
    pallas_call x1, Pallas kernels: 45.3 us -> 58.2 us  [layer_close(): pl.pallas_call(close_kernel, out_shape=[shape((rows, width), jnp.float32)...]
  transfers between devices with their start and end apart: 4 -> 3, of which waited for: 2 -> 1; matrix products, arithmetic and copies ran while one was open for 5% -> 5% of each run, Pallas kernels for 29% -> 30%
where the time goes in v7:
time: 622 us; the launch traced here: 610 us
  Pallas kernels  531 us (85%)
  local copies, waits for them, and re-layouts  47.4 us (8%)
  between operations  14.4 us (2%)
  other arithmetic  14.1 us (2%)
    pallas_call x1, Pallas kernels, layer_front(): pl.pallas_call(layer_kernel, out_shape=out_shape, in_specs=[anywhere] * 7...  342 us
    pallas_call x1, Pallas kernels, layer_turn(): pl.pallas_call(turn_kernel, out_shape=[shape((rows, width), LOW), shape((...  104 us
    pallas_call x1, Pallas kernels, layer_close(): pl.pallas_call(close_kernel, out_shape=[shape((rows, width), jnp.float32)...  58.2 us
    pallas_call x2, Pallas kernels, exchange_plane(): pl.pallas_call(exchange_kernel, out_shape=jax.ShapeDtypeStruct(x.shape, x...  27.2 us
  transfers between devices with their start and end apart: 3, of which 1 were waited for; matrix products, arithmetic and copies ran while one was open for 5% of the time, Pallas kernels for 30%

profile of v7, /device:TPU:1, one launch (start us, length us, event | category | flops | bytes accessed | tf_op | source)
XLA Modules:
  0.0 609.6 jit_solution(14465445242374932817)
XLA Ops:
  7.2 0.0 reduce-scatter.6.cloned.1.call-start
  7.2 0.1 pad.12.clone
  7.3 0.1 pad.16.clone
  7.4 0.9 reduce_window_sum.14
  8.3 0.7 bitcast_subtract_fusion
  8.9 0.7 broadcast_in_dim.29
  9.6 0.7 broadcast_in_dim.30
  10.3 0.1 select_reduce_fusion
  10.4 1.3 copy.40.first_ref
  11.8 1.0 constant_dynamic-slice_fusion.26
  12.7 0.7 maximum_maximum_fusion.1.gain_ref
  13.4 1.1 constant_dynamic-slice_fusion.24
  14.5 0.9 maximum_maximum_fusion.wa_ref
  15.4 1.9 constant_dynamic-slice_fusion.16
  17.3 3.1 constant_dynamic-slice_fusion
  20.5 6.2 %concatenate.22.wgu_ref = bf16[512,1408]{1,0:T(8,128)(2,1)} concatenate(bf16[512,64]{1,0:T(8,128)(2,1)S(1)} %get-tuple-element.127, bf16[512,64]{1,0:T(8,128)(2,1)S(1)} %get-tuple-element.128, bf16[512,64]{1,0:T(8,128)(2,1)S(1)} %get-tuple-element.129, bf16[512,64]{1,0:T(8,128)(2,1)S(1)} %get-tuple-element.130, bf16[512,64]{1,0:T(8,128)(2,1)S(1)} %get-tuple-element.108, ...), dimensions={1} | concatenate | bytes 2883584 | tf_op jit(solution)/shard_map/concatenate | solution.py:1911
  26.6 341.7 %layer.1 = (bf16[8,256,2048]{2,1,0:T(8,128)(2,1)}, bf16[8,256,2048]{2,1,0:T(8,128)(2,1)}, bf16[8,256,2048]{2,1,0:T(8,128)(2,1)}, bf16[8,2048,256]{2,1,0:T(8,128)...) custom-call(bf16[256,2048]{1,0:T(8,128)(2,1)} %bitcast.42, ...), custom_call_target="tpu_custom_call" | custom-call | flops 53150220288 | bytes 209715200 | tf_op jit(solution)/shard_map/layer/pallas_call | solution.py:1160
  368.4 0.0 reduce-scatter.6.cloned.1.call-update
  368.4 0.0 reduce-scatter.4.cloned.1.call-start
  368.4 0.7 reduce-scatter.4.cloned.1.call-update
  369.2 0.0 reduce-scatter.8.cloned.1.call-start
  369.2 103.7 %turn.1 = (bf16[256,2048]{1,0:T(8,128)(2,1)}, f32[256,2048]{1,0:T(8,128)}, bf16[2,1024,384]{2,1,0:T(8,128)(2,1)}, f32[8,2048]{1,0:T(8,128)}, bf16[2048,640]{1,0:T(8,128)(2,1)}) custom-call(f32[256,2048]{1,0:T(8,128)} %get-tuple-element.40.gh_ref, f32[256,2048]{1,0:T(8,128)} %get-tuple-element.41.mid_ref, bf16[256,2048]{1,0:T(8,128)(2,1)} %bitcast.41, ...), custom_call_target="tpu_custom_call" | custom-call | bytes 83886080 | tf_op jit(solution)/shard_map/turn/pallas_call | solution.py:1616
  472.9 0.0 reduce-scatter.6.cloned.1.call-done
  473.0 1.9 reduce-scatter.4.cloned.1.call-done
  474.9 0.0 reduce-scatter.8.cloned.1.call-update
  474.9 58.2 %close.1 = (f32[256,2048]{1,0:T(8,128)}, f32[64,128]{1,0:T(8,128)}) custom-call(bf16[2,1024,384]{2,1,0:T(8,128)(2,1)} %get-tuple-element.52.g_ref, bf16[2048,384]{1,0:T(8,128)(2,1)} %get-tuple-element.53.wa_ref, f32[256,2048]{1,0:T(8,128)} %get-tuple-element.54.g_mid_ref, bf16[256,2048]{1,0:T(8,128)(2,1)} %bitcast.43, ...), custom_call_target="tpu_custom_call" | custom-call | bytes 83886080 | tf_op jit(solution)/shard_map/close/pallas_call | solution.py:1802
  533.2 0.6 reduce_sum.25
  533.8 1.5 slice_reduce_fusion
  535.4 2.2 convert_reduce_fusion
  537.6 1.2 pad_maximum_fusion
  538.8 19.1 %exchange.2 = bf16[8,64,1408]{2,1,0:T(8,128)(2,1)} custom-call(bf16[8,64,1408]{2,1,0:T(8,128)(2,1)} %bitcast.35), custom_call_target="tpu_custom_call" | custom-call | bytes 28835840 | tf_op jit(solution)/shard_map/exchange/pallas_call | solution.py:341
  558.0 1.0 convert_element_type.33
  559.0 1.9 fusion.1
  560.9 0.3 copy.45
  561.2 0.4 copy.46
  561.6 0.7 copy-done
  562.3 1.2 fusion
  563.5 0.5 reshape.95
  563.9 1.2 copy.42
  565.1 1.5 copy.43
  566.6 2.5 reshape.96
  569.1 2.4 maximum_bitcast_fusion.1
  571.4 1.2 copy.47
  572.7 2.6 reshape.98
  575.3 1.5 reshape.91
  576.8 1.5 reshape.92
  578.3 1.1 maximum_bitcast_fusion
  579.4 1.2 copy.44
  580.7 0.0 copy-start.1
  580.7 2.7 reshape.94
  583.4 1.2 pad_maximum_fusion.1
  584.6 1.8 slice.148
  586.3 8.0 %exchange.3 = bf16[8,64,384]{2,1,0:T(8,128)(2,1)} custom-call(bf16[8,64,384]{2,1,0:T(8,128)(2,1)} %bitcast.39), custom_call_target="tpu_custom_call" | custom-call | bytes 7864320 | tf_op jit(solution)/shard_map/exchange/pallas_call | solution.py:341
  594.4 0.0 slice-start
  594.4 1.1 convert_element_type.27
  595.5 0.1 slice_bitcast_fusion.1
  595.7 0.8 copy.55
  596.5 0.1 copy.49
  596.7 0.7 copy.53
  597.4 0.8 copy.54
  598.2 0.1 copy.48
  598.3 0.7 copy.52
  599.1 2.3 copy.58
  601.4 1.3 copy.59
  (20 shorter events, 0.1 us)
Async XLA Ops:
  7.2 465.8 %reduce-scatter.6.cloned.1.call-start = ((), (), s32[]{:S(2)}) async-start(), calls=%async_computation.4 | async-start | bytes 2293760 | tf_op jit(solution)/shard_map/reduce_scatter | solution.py:1995
  368.4 106.5 %reduce-scatter.4.cloned.1.call-start = ((), (), s32[]{:S(2)}) async-start(), calls=%async_computation.3 | async-start | bytes 4587520 | tf_op jit(solution)/shard_map/reduce_scatter | solution.py:1995
  369.2 215.4 %reduce-scatter.8.cloned.1.call-start = ((), (), s32[]{:S(2)}) async-start(), calls=%async_computation.5 | async-start | bytes 3276800 | tf_op jit(solution)/shard_map/reduce_scatter | solution.py:1995
  474.9 58.2 %copy-start.3 = (bf16[4,512,512]{2,1,0:T(8,128)(2,1)S(1)}, bf16[4,512,512]{2,1,0:T(8,128)(2,1)}, u32[]{:S(2)}) copy-start(bf16[4,512,512]{2,1,0:T(8,128)(2,1)} %get-tuple-element.61) | copy-start | bytes 6291460
  533.2 4.4 copy-start.6
  538.8 19.2 %copy-start.7 = (bf16[112,2048]{1,0:T(8,128)(2,1)S(1)}, bf16[112,2048]{1,0:T(8,128)(2,1)}, u32[]{:S(2)}) copy-start(bf16[112,2048]{1,0:T(8,128)(2,1)} %reduce-scatter.6.cloned.1.call-done) | copy-start | bytes 1376260
  560.9 1.4 copy-start
  562.3 1.6 copy-start.5
  580.7 2.7 copy-start.1
  580.7 2.7 copy-start.4
  594.4 1.3 slice-start
  596.5 4.8 copy-start.2
Sparse Core Ops, SparseCore 0:
  368.5 36.4 reduce-scatter.5
  407.3 67.5 reduce-scatter.3
  477.2 53.5 reduce-scatter.7
